TPU v7x, 32 devices: a whole 2x2x4 slice. The times are simulated.
32 devices in a mesh: section: 2 (over core), ctx: 4 (over y, x), fsdp: 4 (over z).
Axes of the slice: x: 2, y: 2, z: 4, core: 2. Of those that a mesh axis runs over, the one named last changes fastest.
Arguments:
- tokens: bfloat16 [2, 4, 1024, 1536], P(None, 'fsdp', 'ctx'), may hold values from -6 to 6
- block_of: int32 [8], replicated, may hold values from 0 to 7, as said below
- routes: int32 [2, 2, 4, 1024, 4], P('section', None, 'fsdp', 'ctx'), may hold values from 0 to 7, all different within a row; in each aligned block of 256 rows (0 to 255, 256 to 511, ..., all dimensions but the last counted through in order) at most 160 rows name the same one
- combine: float32 [2, 2, 4, 1024, 4], P('section', None, 'fsdp', 'ctx'), may hold values from 0.25 to 0.75
- attn_norm: bfloat16 [2, 1536], P('section', ('ctx', 'fsdp')), may hold values from 0.5 to 1.5
- w_query: bfloat16 [2, 1536, 1536], P('section', ('ctx', 'fsdp')), may hold values from -0.15625 to 0.15625
- w_key: bfloat16 [2, 1536, 256], P('section', ('ctx', 'fsdp')), may hold values from -0.15625 to 0.15625
- w_value: bfloat16 [2, 1536, 256], P('section', ('ctx', 'fsdp')), may hold values from -0.15625 to 0.15625
- w_out: bfloat16 [2, 1536, 1536], P('section', ('ctx', 'fsdp')), may hold values from -0.875 to 0.875
- ffn_norm: bfloat16 [2, 1536], P('section', ('ctx', 'fsdp')), may hold values from 0.5 to 1.5
- w_gate: bfloat16 [2, 8, 1536, 768], P('section', None, ('ctx', 'fsdp')), may hold values from -0.15625 to 0.15625
- w_up: bfloat16 [2, 8, 1536, 768], P('section', None, ('ctx', 'fsdp')), may hold values from -0.15625 to 0.15625
- w_down: bfloat16 [2, 8, 768, 1536], P('section', None, ('ctx', 'fsdp')), may hold values from -0.21875 to 0.21875
- out_grad: bfloat16 [2, 4, 1024, 1536], P(None, 'fsdp', 'ctx'), may hold values from -6 to 6
Outputs:
- layer_out: bfloat16 [2, 2, 4, 1024, 1536], P('section', None, 'fsdp', 'ctx')
- input_grads: float32 [2, 2, 4, 1024, 1536], P('section', None, 'fsdp', 'ctx')
- grad_attn_norm: float32 [2, 1536], P('section', ('ctx', 'fsdp'))
- grad_query: float32 [2, 1536, 1536], P('section', ('ctx', 'fsdp'))
- grad_key: float32 [2, 1536, 256], P('section', ('ctx', 'fsdp'))
- grad_value: float32 [2, 1536, 256], P('section', ('ctx', 'fsdp'))
- grad_out: float32 [2, 1536, 1536], P('section', ('ctx', 'fsdp'))
- grad_ffn_norm: float32 [2, 1536], P('section', ('ctx', 'fsdp'))
- grad_gate: float32 [2, 8, 1536, 768], P('section', None, ('ctx', 'fsdp'))
- grad_up: float32 [2, 8, 1536, 768], P('section', None, ('ctx', 'fsdp'))
- grad_down: float32 [2, 8, 768, 1536], P('section', None, ('ctx', 'fsdp'))
Inputs may be any that keep to these rules, and one draw needn't show every extreme that they name: `block_of`: context index c holds slots 2c and 2c + 1 of every sequence; these hold causal blocks k and 7 - k for some k, and every block is held once. `routes`: A token's 4 experts differ. In each aligned block of 256 rows (the rows of one device in one micro-batch, one section) no expert is named by more than 160 rows, and in some blocks one is named by exactly 160.
All inputs are finite; a program needn't handle non-finite values.
Results may differ from a plain program's by a relative error of at most 0.025.
Values may be sent and summed in bfloat16 or wider, within the bound.
No kernel may reach another device: no remote copies, remote signals or barrier semaphores. Data moves between devices by JAX's collectives and lax.ppermute only.
A program may use at most 448 MiB of HBM per device.

v0:
```python
import functools

import jax
import jax.numpy as jnp
from jax import lax
from jax.experimental import pallas as pl
from jax.experimental.pallas import tpu as pltpu
from jax.sharding import PartitionSpec as P

QH = 12
KVH = 2
HD = 128
GROUP = QH // KVH
TOP = 4
EXPERTS = 8
bf16 = jnp.bfloat16
f32 = jnp.float32


epsilon = 1e-06
masked_out = -1e30
gap = 256


def swap(value, axis, bit):
    count = lax.axis_size(axis)
    return lax.ppermute(value, axis, [(source, source ^ bit) for source in range(count)])


def tie(*values):
    return lax.optimization_barrier(values)


def after(value, earlier):
    return tie(value, earlier)[0]


def at(value, index, axis=0):
    return lax.dynamic_index_in_dim(value, index, axis, keepdims=False)


def dot(spec, left, right, kind=f32):
    return jnp.einsum(spec, left, right, preferred_element_type=kind)


def cost(micros):
    return pl.CostEstimate(
        flops=int(micros * 1e9), bytes_accessed=int(micros * 3e6), transcendentals=0
    )


def kernel_params():
    return pltpu.CompilerParams(vmem_limit_bytes=56 * 1024 * 1024)


def nt(left, right):
    return lax.dot_general(left, right, (((1,), (1,)), ((), ())), preferred_element_type=f32)


def nn(left, right):
    return jnp.dot(left, right, preferred_element_type=f32)


def head_rows(ref):
    return jnp.concatenate([ref[:, i * HD : (i + 1) * HD] for i in range(GROUP)], axis=0)


def softmax_rows(ids_ref, queries, keys, half, own):
    scores = nt(queries, keys) * HD ** (-0.5)
    tall, wide = scores.shape
    row = lax.broadcasted_iota(jnp.int32, (half, 1), 0)
    row = jnp.concatenate([row] * (tall // half), axis=0) + ids_ref[own] * half
    lane = lax.broadcasted_iota(jnp.int32, (1, half), 1)
    column = [lane + ids_ref[block] * half for block in range(wide // half)]
    column = jnp.concatenate(column, axis=1)
    scores = jnp.where(row >= column, scores, masked_out)
    shifted = jnp.exp(scores - jnp.max(scores, axis=1, keepdims=True))
    return shifted / jnp.sum(shifted, axis=1, keepdims=True)


def attend_kernel(ids_ref, query_ref, key_ref, value_ref, out_ref):
    half = query_ref.shape[0]
    probs = softmax_rows(ids_ref, head_rows(query_ref), key_ref[...], half, pl.program_id(1))
    out = nn(probs.astype(bf16), value_ref[...]).astype(bf16)
    for i in range(GROUP):
        out_ref[:, i * HD : (i + 1) * HD] = out[i * half : (i + 1) * half]


def attend_specs(rows, seq_len):
    half = rows // 2
    by_head = pl.BlockSpec((half, GROUP * HD), lambda g, h, ids: (h, g))
    keys = pl.BlockSpec((seq_len, HD), lambda g, h, ids: (0, g))
    values = pl.BlockSpec((seq_len, HD), lambda g, h, ids: (0, KVH + g))
    return by_head, keys, values


def attend_call(ids, queries, key_value):
    rows, seq_len = (queries.shape[0], key_value.shape[0])
    by_head, keys, values = attend_specs(rows, seq_len)
    return pl.pallas_call(
        attend_kernel,
        grid_spec=pltpu.PrefetchScalarGridSpec(
            num_scalar_prefetch=1,
            grid=(KVH, 2),
            in_specs=[by_head, keys, values],
            out_specs=by_head,
        ),
        out_shape=jax.ShapeDtypeStruct((rows, QH * HD), bf16),
        compiler_params=kernel_params(),
        cost_estimate=cost(1),
        name="attend",
    )(ids, queries, key_value, key_value)


def attend_back_kernel(ids_ref, query_ref, key_ref, value_ref, cot_ref, dq_ref, *refs):
    out, (dk_ref, dv_ref) = (refs[:-2], refs[-2:])
    half = query_ref.shape[0]
    group, own = (pl.program_id(0), pl.program_id(1))
    queries, cot = (head_rows(query_ref), head_rows(cot_ref))
    probs = softmax_rows(ids_ref, queries, key_ref[...], half, own)
    d_probs = nt(cot, value_ref[...])
    inner = jnp.sum(probs * d_probs, axis=1, keepdims=True)
    d_scores = (probs * (d_probs - inner)).astype(bf16)
    d_queries = (nn(d_scores, key_ref[...]) * HD ** (-0.5)).astype(bf16)
    for i in range(GROUP):
        dq_ref[:, i * HD : (i + 1) * HD] = d_queries[i * half : (i + 1) * half]
    d_keys = nn(d_scores.T, queries) * HD ** (-0.5)
    d_values = nn(probs.astype(bf16).T, cot)

    @pl.when(own == 0)
    def _():
        dk_ref[...] = d_keys
        dv_ref[...] = d_values

    @pl.when(own != 0)
    def _():
        rows = 2 * half
        for block, ref in enumerate(out):
            part = slice(block * rows, (block + 1) * rows)
            for first, total, last in ((0, dk_ref, d_keys), (KVH * HD, dv_ref, d_values)):
                columns = pl.ds(pl.multiple_of(first + group * HD, HD), HD)
                ref[:, columns] = (total[part, :] + last[part]).astype(bf16)


def attend_back_call(ids, queries, key_value, cot):
    rows, seq_len = (queries.shape[0], key_value.shape[0])
    by_head, keys, values = attend_specs(rows, seq_len)
    blocks = seq_len // rows
    wide = 2 * KVH * HD
    result = pl.pallas_call(
        attend_back_kernel,
        grid_spec=pltpu.PrefetchScalarGridSpec(
            num_scalar_prefetch=1,
            grid=(KVH, 2),
            in_specs=[by_head, keys, values, by_head],
            out_specs=[by_head] + [pl.BlockSpec((rows, wide), lambda g, h, ids: (0, 0))] * blocks,
            scratch_shapes=[pltpu.VMEM((seq_len, HD), f32)] * 2,
        ),
        out_shape=[jax.ShapeDtypeStruct((rows, QH * HD), bf16)]
        + [jax.ShapeDtypeStruct((rows, wide), bf16)] * blocks,
        compiler_params=kernel_params(),
        cost_estimate=cost(1),
        name="attend_back",
    )(ids, queries, key_value, key_value, cot)
    return (result[0], result[1:])


def gelu_parts(gate):
    root = 0.7978845608028654
    inner = root * (gate + 0.044715 * gate * gate * gate)
    bent = jnp.tanh(inner)
    value = 0.5 * gate * (1.0 + bent)
    slope = root * (1.0 + 3.0 * 0.044715 * gate * gate)
    return value, 0.5 * (1.0 + bent) + 0.5 * gate * (1.0 - bent * bent) * slope


def give_back(pick_ref, total_ref, share_ref, before, out):
    blocks, capacity, _ = pick_ref.shape
    for d in range(blocks):
        part = total_ref[d * capacity : (d + 1) * capacity, :]
        if share_ref is not None:
            part = part * share_ref[d]
        back = nn(pick_ref[d].T, part.astype(bf16))
        if before:
            back = back + before[d][...]
        out[d][...] = back.astype(out[d].dtype)


def flat(ref):
    value = ref[...]
    return value.reshape(-1, value.shape[-1])


def add_up(total_ref, part, step):
    @pl.when(step == 0)
    def _():
        total_ref[...] = part

    @pl.when(step != 0)
    def _():
        total_ref[...] += part


def expert_kernel(blocks, adds, pick_ref, share_ref, gate_ref, up_ref, down_ref, *refs):
    rows, refs = (refs[:blocks], refs[blocks:])
    before, refs = (refs[: blocks * adds], refs[blocks * adds :])
    out, (picked_ref, gate_pre_ref, up_pre_ref, total_ref) = (refs[:blocks], refs[blocks:])
    step = pl.program_id(0)
    capacity = pick_ref.shape[1]

    @pl.when(step == 0)
    def _():
        for d in range(blocks):
            block = nn(pick_ref[d], rows[d][...]).astype(bf16)
            picked_ref[d * capacity : (d + 1) * capacity, :] = block

    gate_pre = nn(picked_ref[...], flat(gate_ref))
    up_pre = nn(picked_ref[...], flat(up_ref))
    gate_pre_ref[...] = gate_pre
    up_pre_ref[...] = up_pre
    active = (gelu_parts(gate_pre)[0] * up_pre).astype(bf16)
    add_up(total_ref, nn(active, flat(down_ref)), step)

    @pl.when(step == pl.num_programs(0) - 1)
    def _():
        give_back(pick_ref, total_ref, share_ref, before, out)


def whole_spec(shape):
    return pl.BlockSpec(
        shape, lambda step: (0,) * len(shape), pipeline_mode=pl.Buffered(buffer_count=1)
    )


def weight_operands(weights, deep, cut):
    if len(weights) == 1:
        unit = weights[0]
        shards, tall, width = unit.shape
        specs = [
            pl.BlockSpec((shards, deep, cut), lambda step: (0, 0, 2 * step)),
            pl.BlockSpec((shards, deep, cut), lambda step: (0, 0, 2 * step + 1)),
            pl.BlockSpec(
                (shards // 2, tall - deep, width), lambda step: (step, deep // (tall - deep), 0)
            ),
        ]
        return specs, [unit, unit, unit]
    pair, down = weights
    specs = [
        pl.BlockSpec((pair.shape[0], cut), lambda step: (0, 2 * step)),
        pl.BlockSpec((pair.shape[0], cut), lambda step: (0, 2 * step + 1)),
        pl.BlockSpec((cut, down.shape[1]), lambda step: (step, 0)),
    ]
    return specs, [pair, pair, down]


def expert_call(picks, shares, rows, weights, deep, hidden, before, micros):
    blocks, capacity, _ = picks.shape
    width, cut, tall = (rows[0].shape[1], hidden // 2, blocks * capacity)
    columns = pl.BlockSpec((tall, cut), lambda step: (0, step))
    row_specs = [whole_spec(block.shape) for block in rows]
    specs, operands = weight_operands(weights, deep, cut)
    result = pl.pallas_call(
        functools.partial(expert_kernel, blocks, 1 if before else 0),
        grid=(2,),
        in_specs=[whole_spec(picks.shape), whole_spec(shares.shape)]
        + specs
        + row_specs * (2 if before else 1),
        out_specs=row_specs + [whole_spec((tall, width)), columns, columns],
        out_shape=[jax.ShapeDtypeStruct(block.shape, bf16) for block in rows]
        + [
            jax.ShapeDtypeStruct((tall, width), bf16),
            jax.ShapeDtypeStruct((tall, hidden), f32),
            jax.ShapeDtypeStruct((tall, hidden), f32),
        ],
        scratch_shapes=[pltpu.VMEM((tall, width), f32)],
        compiler_params=kernel_params(),
        cost_estimate=cost(micros),
        name="expert",
    )(picks, shares, *operands, *rows, *before)
    return (list(result[:blocks]), list(result[blocks:]))


def expert_back_kernel(
    blocks, adds, pick_ref, share_ref, gate_pre_ref, up_pre_ref, gate_ref, up_ref, down_ref, *refs
):
    rows, refs = (refs[:blocks], refs[blocks:])
    before, refs = (refs[: blocks * adds], refs[blocks * adds :])
    out, refs = (refs[:blocks], refs[blocks:])
    slots_ref, d_gate_ref, d_up_ref, active_ref, total_ref = refs
    step = pl.program_id(0)
    capacity = pick_ref.shape[1]

    @pl.when(step == 0)
    def _():
        for d in range(blocks):
            block = nn(pick_ref[d], rows[d][...]) * share_ref[d]
            slots_ref[d * capacity : (d + 1) * capacity, :] = block.astype(bf16)

    d_active = nt(slots_ref[...], flat(down_ref))
    value, slope = gelu_parts(gate_pre_ref[...])
    up_pre = up_pre_ref[...]
    d_gate = (d_active * up_pre * slope).astype(bf16)
    d_up = (d_active * value).astype(bf16)
    active_ref[...] = (value * up_pre).astype(bf16)
    d_gate_ref[...] = d_gate
    d_up_ref[...] = d_up
    add_up(total_ref, nt(d_gate, flat(gate_ref)) + nt(d_up, flat(up_ref)), step)

    @pl.when(step == pl.num_programs(0) - 1)
    def _():
        give_back(pick_ref, total_ref, None, before, out)


def expert_back_call(picks, shares, rows, kept, weights, deep, before, micros):
    _, gate_pre, up_pre = kept
    blocks, capacity, _ = picks.shape
    width, (tall, hidden) = (rows[0].shape[1], gate_pre.shape)
    cut = hidden // 2
    columns = pl.BlockSpec((tall, cut), lambda step: (0, step))
    row_specs = [whole_spec(block.shape) for block in rows]
    specs, operands = weight_operands(weights, deep, cut)
    result = pl.pallas_call(
        functools.partial(expert_back_kernel, blocks, 1 if before else 0),
        grid=(2,),
        in_specs=[whole_spec(picks.shape), whole_spec(shares.shape), columns, columns]
        + specs
        + row_specs * (2 if before else 1),
        out_specs=row_specs + [whole_spec((tall, width)), columns, columns, columns],
        out_shape=[jax.ShapeDtypeStruct(block.shape, bf16) for block in rows]
        + [jax.ShapeDtypeStruct((tall, width), bf16)]
        + [jax.ShapeDtypeStruct((tall, hidden), bf16)] * 3,
        scratch_shapes=[pltpu.VMEM((tall, width), f32)],
        compiler_params=kernel_params(),
        cost_estimate=cost(micros),
        name="expert_back",
    )(picks, shares, gate_pre, up_pre, *operands, *rows, *before)
    return (list(result[:blocks]), list(result[blocks:]))


def expert_grads_kernel(parts, deep, *refs):
    picked, slots, d_gate, d_up, active = (refs[i * parts : (i + 1) * parts] for i in range(5))
    grad_refs, turned_ref = (refs[5 * parts : -1], refs[-1])
    step = pl.program_id(0)

    def below(some):
        return jnp.concatenate([ref[...] for ref in some], axis=0)

    @pl.when(step == 0)
    def _():
        turned_ref[...] = below(picked).T

    grad_gate = nn(turned_ref[...], below(d_gate)).astype(bf16)
    grad_up = nn(turned_ref[...], below(d_up)).astype(bf16)
    grad_down = nn(below(active).T, below(slots)).astype(bf16)
    cut = grad_gate.shape[1]
    if len(grad_refs) == 1:
        unit_ref = grad_refs[0]
        shards, tall, width = unit_ref.shape
        for side in range(2):

            @pl.when(step == side)
            def _():
                left, some = (2 * side * cut, shards // 2)
                unit_ref[:, :deep, left : left + cut] = grad_gate.reshape(shards, deep, cut)
                left = left + cut
                unit_ref[:, :deep, left : left + cut] = grad_up.reshape(shards, deep, cut)
                rest = grad_down.reshape(some, tall - deep, width)
                unit_ref[side * some : (side + 1) * some, deep:, :] = rest
    else:
        grad_refs[0][:, :cut] = grad_gate
        grad_refs[0][:, cut:] = grad_up
        grad_refs[1][...] = grad_down


def expert_grads_call(picked, saved, weights, deep):
    slots, d_gate, d_up, active = zip(*saved)
    width, hidden = (picked[0].shape[1], d_gate[0].shape[1])
    cut = hidden // 2
    columns = [pl.BlockSpec((part.shape[0], cut), lambda step: (0, step)) for part in picked]
    if len(weights) == 1:
        grad_specs = [whole_spec(weights[0].shape)]
    else:
        grad_specs = [
            pl.BlockSpec((width, 2 * cut), lambda step: (0, step)),
            pl.BlockSpec((cut, width), lambda step: (step, 0)),
        ]
    return list(
        pl.pallas_call(
            functools.partial(expert_grads_kernel, len(picked), deep),
            grid=(2,),
            in_specs=[whole_spec(part.shape) for part in picked] * 2 + columns * 3,
            out_specs=grad_specs,
            out_shape=[jax.ShapeDtypeStruct(part.shape, bf16) for part in weights],
            scratch_shapes=[pltpu.VMEM((width, sum(part.shape[0] for part in picked)), bf16)],
            compiler_params=kernel_params(),
            cost_estimate=cost(1),
            name="expert_grads",
        )(*picked, *slots, *d_gate, *d_up, *active)
    )


def norm_parts(value):
    scale = lax.rsqrt(jnp.mean(value * value, axis=1, keepdims=True) + epsilon)
    return scale, value * scale


def norm_back(grad, gain, value):
    scale, scaled = norm_parts(value)
    grown = grad * gain
    back = scale * (grown - scaled * jnp.mean(scaled * grown, axis=1, keepdims=True))
    return back, (grad * scaled).astype(bf16)


def add_all(refs):
    total = refs[0][...].astype(f32)
    for ref in refs[1:]:
        total = total + ref[...].astype(f32)
    return total


def side_offsets(core_ref, steps, cut):
    step, core = (pl.program_id(0), core_ref[0])
    own = pl.multiple_of((core * steps + step) * cut, cut)
    other = pl.multiple_of(((1 - core) * steps + step) * cut, cut)
    return own, other


def dense_call(kernel, core, steps, whole, halves, out, scratch, name, micros):
    cut = halves[0].shape[1] // steps

    def keep(shape):
        return pl.BlockSpec(
            shape, lambda step, core: (0,) * len(shape), pipeline_mode=pl.Buffered(buffer_count=1)
        )

    def tile(tall):
        return pl.BlockSpec((tall, cut), lambda step, core: (0, step))

    return pl.pallas_call(
        kernel,
        grid_spec=pltpu.PrefetchScalarGridSpec(
            num_scalar_prefetch=1,
            grid=(steps,),
            in_specs=[keep(part.shape) for part in whole] + [tile(halves[0].shape[0])] * 2,
            out_specs=[
                tile(part.shape[0]) if tiled else keep(part.shape) for part, tiled in out
            ],
            scratch_shapes=scratch,
        ),
        out_shape=[part for part, _ in out],
        compiler_params=kernel_params(),
        cost_estimate=cost(micros),
        name=name,
    )(core.astype(jnp.int32).reshape(1), *whole, *halves)


def shape_of(kind, *shape):
    return jax.ShapeDtypeStruct(shape, kind)


def enter_kernel(steps, terms, core_ref, gain_ref, *refs):
    parts, (own_ref, other_ref, sent_ref, normed_ref, out_ref) = (refs[:terms], refs[terms:])
    own, other = side_offsets(core_ref, steps, own_ref.shape[1])

    @pl.when(pl.program_id(0) == 0)
    def _():
        sent = add_all(parts).astype(bf16)
        sent_ref[...] = sent
        normed_ref[...] = (norm_parts(sent.astype(f32))[1] * gain_ref[...]).astype(bf16)

    cut = own_ref.shape[1]
    out_ref[:, pl.ds(own, cut)] = nn(normed_ref[...], own_ref[...]).astype(bf16)
    out_ref[:, pl.ds(other, cut)] = nn(normed_ref[...], other_ref[...]).astype(bf16)


def enter_call(core, parts, gain, halves):
    rows, width = parts[0].shape
    return dense_call(
        functools.partial(enter_kernel, 3, len(parts)),
        core,
        3,
        [gain] + parts,
        halves,
        [
            (shape_of(bf16, rows, width), False),
            (shape_of(bf16, rows, width), False),
            (shape_of(bf16, rows, 2 * halves[0].shape[1]), False),
        ],
        [],
        "enter",
        6,
    )


def leave_kernel(steps, core_ref, gain_ref, rows_ref, attended_ref, own_ref, other_ref,
                 mid_ref, normed_ref):
    cut = own_ref.shape[1]
    for start, ref in zip(side_offsets(core_ref, steps, cut), (own_ref, other_ref)):
        part = pl.ds(start, cut)
        mid_ref[:, part] = rows_ref[:, part].astype(f32) + nn(attended_ref[...], ref[...])

    @pl.when(pl.program_id(0) == steps - 1)
    def _():
        normed_ref[...] = (norm_parts(mid_ref[...])[1] * gain_ref[...]).astype(bf16)


def leave_call(core, rows_in, attended, gain, halves):
    rows, width = rows_in.shape
    return dense_call(
        functools.partial(leave_kernel, 2),
        core,
        2,
        [gain, rows_in, attended],
        halves,
        [(shape_of(f32, rows, width), False), (shape_of(bf16, rows, width), False)],
        [],
        "leave",
        5,
    )


def leave_back_kernel(steps, terms, core_ref, gain_ref, mid_ref, cot_ref, attended_ref, *refs):
    parts, refs = (refs[:terms], refs[terms:])
    own_ref, other_ref, after_ref, term_ref, d_attended_ref, *refs = refs
    own_grad_ref, other_grad_ref, branch_ref, turned_ref, total_ref = refs
    step, cut = (pl.program_id(0), own_ref.shape[1])

    @pl.when(step == 0)
    def _():
        back, term_ref[...] = norm_back(add_all(parts), gain_ref[...], mid_ref[...])
        back = back + cot_ref[...].astype(f32)
        after_ref[...] = back
        branch_ref[...] = back.astype(bf16)
        turned_ref[...] = attended_ref[...].T

    own, other = side_offsets(core_ref, steps, cut)
    d_own, d_other = (branch_ref[:, pl.ds(own, cut)], branch_ref[:, pl.ds(other, cut)])
    own_grad_ref[...] = nn(turned_ref[...], d_own).astype(bf16)
    other_grad_ref[...] = nn(turned_ref[...], d_other).astype(bf16)
    add_up(total_ref, nt(d_own, own_ref[...]) + nt(d_other, other_ref[...]), step)

    @pl.when(step == steps - 1)
    def _():
        d_attended_ref[...] = total_ref[...].astype(bf16)


def leave_back_call(core, parts, gain, mid, cotangent, attended, halves):
    rows, width = mid.shape
    half = (halves[0].shape[0], halves[0].shape[1])
    return dense_call(
        functools.partial(leave_back_kernel, 2, len(parts)),
        core,
        2,
        [gain, mid, cotangent, attended] + parts,
        halves,
        [
            (shape_of(f32, rows, width), False),
            (shape_of(bf16, rows, width), False),
            (shape_of(bf16, rows, width), False),
            (shape_of(bf16, *half), True),
            (shape_of(bf16, *half), True),
        ],
        [
            pltpu.VMEM((rows, width), bf16),
            pltpu.VMEM((width, rows), bf16),
            pltpu.VMEM((rows, width), f32),
        ],
        "leave_back",
        8,
    )


def enter_back_kernel(steps, terms, core_ref, gain_ref, rows_ref, normed_ref, after_ref, term_ref,
                      dq_ref, *refs):
    parts, refs = (refs[:terms], refs[terms:])
    own_ref, other_ref, entry_ref, sent_ref, own_grad_ref, other_grad_ref, *refs = refs
    entered_ref, turned_ref, total_ref = refs
    step, cut = (pl.program_id(0), own_ref.shape[1])
    rows, qw = dq_ref.shape

    @pl.when(step == 0)
    def _():
        entered_ref[:, :qw] = dq_ref[...]
        wide = parts[0].shape[1]
        entered_ref[:, qw : qw + wide] = add_all(parts).astype(bf16)
        entered_ref[:, qw + wide :] = jnp.zeros((rows, gap), bf16)
        turned_ref[...] = normed_ref[...].T

    own, other = side_offsets(core_ref, steps, cut)
    d_own, d_other = (entered_ref[:, pl.ds(own, cut)], entered_ref[:, pl.ds(other, cut)])
    own_grad_ref[...] = nn(turned_ref[...], d_own).astype(bf16)
    other_grad_ref[...] = nn(turned_ref[...], d_other).astype(bf16)
    add_up(total_ref, nt(d_own, own_ref[...]) + nt(d_other, other_ref[...]), step)

    @pl.when(step == steps - 1)
    def _():
        back, attn_term = norm_back(total_ref[...], gain_ref[...], rows_ref[...].astype(f32))
        back = back + after_ref[...]
        entry_ref[...] = back
        sent_ref[...] = back.astype(bf16)
        lane = lax.broadcasted_iota(jnp.int32, (rows, 128), 1)
        sums = nn(attn_term.T, (lane == 0).astype(bf16))
        sums = (sums + nn(term_ref[...].T, (lane == 1).astype(bf16))).astype(bf16)
        left = cut - gap

        @pl.when(core_ref[0] == 0)
        def _():
            other_grad_ref[:, left : left + 128] = sums

        @pl.when(core_ref[0] != 0)
        def _():
            own_grad_ref[:, left : left + 128] = sums


def enter_back_call(core, dq, parts, gain, rows_in, normed, after, term, halves):
    rows, width = rows_in.shape
    return dense_call(
        functools.partial(enter_back_kernel, 3, len(parts)),
        core,
        3,
        [gain, rows_in, normed, after, term, dq] + parts,
        halves,
        [
            (shape_of(f32, rows, width), False),
            (shape_of(bf16, rows, width), False),
            (shape_of(bf16, *halves[0].shape), True),
            (shape_of(bf16, *halves[0].shape), True),
        ],
        [
            pltpu.VMEM((rows, 2 * halves[0].shape[1]), bf16),
            pltpu.VMEM((width, rows), bf16),
            pltpu.VMEM((rows, width), f32),
        ],
        "enter_back",
        13,
    )


def place_kernel(count, joined, index_ref, *refs):
    step = pl.program_id(0)
    for bit in range(count):

        @pl.when(step == bit)
        def _():
            if joined:
                refs[count][...] = refs[bit][...]
            else:
                refs[count][0] = refs[bit][...]


def place_call(blocks, index):
    count = len(blocks)
    shape = blocks[0].shape
    zeros = (0,) * len(shape)
    joined = len(shape) == 2 and shape[0] % 16 == 0
    if joined:
        out_spec = pl.BlockSpec(shape, lambda step, at: (at[0] ^ step, 0))
        out_shape = (count * shape[0], shape[1])
    else:
        out_spec = pl.BlockSpec((1,) + shape, lambda step, at: (at[0] ^ step,) + zeros)
        out_shape = (count,) + shape
    return pl.pallas_call(
        functools.partial(place_kernel, count, joined),
        grid_spec=pltpu.PrefetchScalarGridSpec(
            num_scalar_prefetch=1,
            grid=(count,),
            in_specs=[pl.BlockSpec(shape, lambda step, at: zeros)] * count,
            out_specs=out_spec,
        ),
        out_shape=jax.ShapeDtypeStruct(out_shape, blocks[0].dtype),
        compiler_params=kernel_params(),
        cost_estimate=cost(2),
        name="place",
    )(index.astype(jnp.int32).reshape(1), *blocks)


def deal_kernel(count, index_ref, *refs):
    step = pl.program_id(0)
    for bit in range(count):

        @pl.when(step == bit)
        def _():
            for layer, ref in enumerate(refs[count:]):
                ref[0] = refs[bit][layer]


def deal_call(blocks, index):
    count = len(blocks)
    layers, *shape = blocks[0].shape
    shape = tuple(shape)
    zeros = (0,) * len(shape)
    return pl.pallas_call(
        functools.partial(deal_kernel, count),
        grid_spec=pltpu.PrefetchScalarGridSpec(
            num_scalar_prefetch=1,
            grid=(count,),
            in_specs=[pl.BlockSpec((layers,) + shape, lambda step, at: (0,) + zeros)] * count,
            out_specs=[pl.BlockSpec((1,) + shape, lambda step, at: (at[0] ^ step,) + zeros)]
            * layers,
        ),
        out_shape=[jax.ShapeDtypeStruct((count,) + shape, blocks[0].dtype)] * layers,
        compiler_params=kernel_params(),
        cost_estimate=cost(2),
        name="deal",
    )(index.astype(jnp.int32).reshape(1), *blocks)


def order_kernel(count, order_ref, *refs):
    step = pl.program_id(0)
    for i in range(count):

        @pl.when(step == i)
        def _():
            refs[count][:, 0] = refs[i][:, 0]


def order_call(blocks, order, unit):
    count = len(blocks)
    n_ctx, _, tall, wide = blocks[0].shape
    shape = (n_ctx, 1, tall, wide)
    source = pl.BlockSpec(
        shape, lambda step, at: (0, unit, 0, 0), pipeline_mode=pl.Buffered(buffer_count=1)
    )
    result = pl.pallas_call(
        functools.partial(order_kernel, count),
        grid_spec=pltpu.PrefetchScalarGridSpec(
            num_scalar_prefetch=1,
            grid=(count,),
            in_specs=[source] * count,
            out_specs=pl.BlockSpec(shape, lambda step, at: (0, at[step], 0, 0)),
        ),
        out_shape=jax.ShapeDtypeStruct((n_ctx, count, tall, wide), bf16),
        compiler_params=kernel_params(),
        cost_estimate=cost(4),
        name="order",
    )(order.astype(jnp.int32), *blocks)
    return result.reshape(n_ctx * count, tall, wide)


def finish_kernel(deep, index_ref, own_ref, other_ref, gate_ref, up_ref, down_ref):
    side = pl.program_id(1)
    wide = gate_ref.shape[2] // 2

    def write(source):
        for half in range(2):
            left, target = (2 * half * wide, slice(half * wide, (half + 1) * wide))
            gate_ref[:, :, target] = source[0, :, :deep, left : left + wide].astype(f32)
            left = left + wide
            up_ref[:, :, target] = source[0, :, :deep, left : left + wide].astype(f32)
        down_ref[...] = source[0, :, deep:, :].astype(f32)

    @pl.when(side == index_ref[1])
    def _():
        write(own_ref)

    @pl.when(side != index_ref[1])
    def _():
        write(other_ref)


def finish_call(own, other, deep, hidden, place, core):
    n_ctx, units, tall, width = own.shape
    experts = 2 * n_ctx * units
    source = pl.BlockSpec((1, units, tall, width), lambda bit, side, at: (bit, 0, 0, 0))
    target = lambda bit, side, at: (2 * (at[0] ^ bit) + side, 0, 0)
    return pl.pallas_call(
        functools.partial(finish_kernel, deep),
        grid_spec=pltpu.PrefetchScalarGridSpec(
            num_scalar_prefetch=1,
            grid=(n_ctx, 2),
            in_specs=[source, source],
            out_specs=[
                pl.BlockSpec((units, deep, hidden), target),
                pl.BlockSpec((units, deep, hidden), target),
                pl.BlockSpec((units, tall - deep, width), target),
            ],
        ),
        out_shape=[
            jax.ShapeDtypeStruct((experts, deep, hidden), f32),
            jax.ShapeDtypeStruct((experts, deep, hidden), f32),
            jax.ShapeDtypeStruct((experts, tall - deep, width), f32),
        ],
        compiler_params=kernel_params(),
        cost_estimate=cost(8),
        name="finish",
    )(jnp.stack([place, core]).astype(jnp.int32), own, other)


def body(
    tokens,
    block_of,
    routes,
    combine,
    attn_norm,
    w_query,
    w_key,
    w_value,
    w_out,
    ffn_norm,
    w_gate,
    w_up,
    w_down,
    out_grad,
):
    rows = tokens.shape[2]
    width = tokens.shape[3]
    half = rows // 2
    n_ctx = lax.axis_size("ctx")
    n_fsdp = lax.axis_size("fsdp")
    core, place, depth = (
        lax.axis_index(axis).astype(jnp.uint32) for axis in ("section", "ctx", "fsdp")
    )
    seq_len = rows * n_ctx
    capacity = rows * TOP * 5 // (4 * EXPERTS)
    score_scale = HD ** (-0.5)
    own_experts = EXPERTS // n_ctx
    hidden = w_gate.shape[3]
    shard_rows = w_query.shape[1]
    down_rows = w_down.shape[2]
    qw = w_query.shape[2]
    kw = w_key.shape[2]
    pieces = max(1, 2 * n_ctx // EXPERTS)
    per_core = max(1, EXPERTS // (2 * n_ctx))
    unit_rows = shard_rows + down_rows
    aligned = shard_rows % 16 == 0 and down_rows % 16 == 0

    def on_core(former, latter):
        return jnp.where(core == 0, former, latter)

    def own_other(low, high):
        return (on_core(low, high), on_core(high, low))

    early, late = (range(1, n_ctx // 2 + 1), range(n_ctx // 2 + 1, n_ctx))

    def send(value, bits):
        return [swap(value, "ctx", bit) for bit in bits]

    def spread(value):
        return [value] + send(value, early) + send(value, late)

    def spread_rows(value):
        near_blocks = send(value, early)
        value, near_blocks = tie(value, near_blocks)
        return [value] + near_blocks + send(value, late)

    def gather_back(blocks):
        return [blocks[0]] + [swap(blocks[bit], "ctx", bit) for bit in range(1, n_ctx)]

    info = jnp.concatenate([routes.astype(f32), combine], axis=-1)[0, :, 0].transpose(0, 2, 1)
    info_own, info_other = (at(info, core), swap(at(info, 1 - core), "section", 1))
    info = jnp.stack(own_other(info_own, info_other))
    info = jnp.stack([info] + [swap(info, "ctx", bit) for bit in range(1, n_ctx)], axis=1)

    gain_columns = jnp.stack([attn_norm[0], ffn_norm[0]], axis=1)
    gain_columns = jnp.pad(gain_columns, ((0, 0), (0, gap - 2)))
    enter_shard = jnp.concatenate([w_query[0], w_key[0], w_value[0], gain_columns], axis=1)
    enter_cut = enter_shard.shape[1] // 2
    leave_cut = w_out.shape[2] // 2
    low_shard = jnp.concatenate([enter_shard[:, :enter_cut], w_out[0, :, :leave_cut]], axis=1)
    high_shard = jnp.concatenate([enter_shard[:, enter_cut:], w_out[0, :, leave_cut:]], axis=1)
    lent = swap(on_core(high_shard, low_shard), "section", 1)
    dense_shards = (on_core(low_shard, lent), on_core(lent, high_shard))

    def gather_deep(shard):
        blocks = [shard] + [swap(shard, "fsdp", bit) for bit in range(1, n_fsdp)]
        return place_call(blocks, depth).reshape(-1, shard.shape[1])

    def join_square(blocks):
        return place_call(blocks, place).reshape(-1, blocks[0].shape[1])

    def gather_square(deep):
        return join_square(spread(deep))

    cut = hidden // 2
    unit_stack = jnp.concatenate(
        [
            jnp.concatenate(
                [w_gate[0, ..., :cut], w_up[0, ..., :cut], w_gate[0, ..., cut:], w_up[0, ..., cut:]],
                axis=2,
            ),
            w_down[0],
        ],
        axis=1,
    )
    if pieces == 2:
        unit_stack = jnp.stack(jnp.split(unit_stack, 2, axis=2), axis=1)
    unit_stack = unit_stack.reshape(n_ctx, 2, per_core, unit_rows, width // pieces)
    units_lent = swap(at(unit_stack, 1 - core, 1), "section", 1)
    unit_stacks = jnp.stack(own_other(at(unit_stack, core, 1), units_lent), axis=1)

    def deal_units(stack):
        blocks = [at(stack, place)]
        blocks += [swap(at(stack, place ^ bit), "ctx", bit) for bit in range(1, n_ctx)]
        return deal_call(blocks, place)

    ring = list(range(0, n_fsdp, 2)) + list(range(1, n_fsdp, 2))[::-1]
    ring_steps = [(ring[i], ring[(i + 1) % n_fsdp]) for i in range(n_fsdp)]
    ring_table = [[ring[ring.index(z) - i] for i in range(n_fsdp)] for z in range(n_fsdp)]
    behind_here = at(jnp.array(ring_table, jnp.uint32), depth)

    def ring_send(moved):
        return [blocks + [lax.ppermute(blocks[-1], "fsdp", ring_steps)] for blocks in moved]

    def own_units(blocks):
        return [order_call(blocks, behind_here, unit) for unit in range(per_core)]

    def pair_units(mine):
        other = [swap(part, "section", 1) for part in mine]
        units = list(mine) + other
        if pieces == 2:
            units = [jnp.concatenate(own_other(mine[0], other[0]), axis=2)]
        if aligned:
            return [[unit] for unit in units]
        return [
            [unit[:, :shard_rows].reshape(-1, width), unit[:, shard_rows:].reshape(-1, width)]
            for unit in units
        ]

    def cut_units(grads):
        if aligned:
            units = [unit for (unit,) in grads]
        else:
            units = [
                jnp.concatenate(
                    [part.reshape(n_ctx * n_fsdp, -1, width) for part in parts], axis=1
                )
                for parts in grads
            ]
        if pieces == 1:
            return (units[:per_core], units[per_core:])
        own, other = own_other(*jnp.split(units[0], 2, axis=2))
        return ([own], [other])

    def ring_part(terms, behind):
        spot = behind_here[behind % n_fsdp]
        return sum(at(term, spot, 1).astype(f32) for term in terms)

    def ring_start(own, received):
        terms = [part.reshape((n_ctx, n_fsdp) + part.shape[1:]) for part in (own, received)]
        return (terms, ring_part(terms, 1).astype(bf16))

    def ring_move(state):
        return [(terms, lax.ppermute(moving, "fsdp", ring_steps)) for terms, moving in state]

    def ring_add(state, step):
        return [
            (terms, (moved.astype(f32) + ring_part(terms, step + 1)).astype(bf16))
            for terms, moved in state
        ]

    def ring_step(state, step):
        return ring_add(ring_move(state), step)

    def ring_last(state):
        state = ring_add(state, 2)
        for step in range(3, n_fsdp - 1):
            state = ring_step(state, step)
        return ring_move(state)

    def ring_rest(state, first):
        for step in range(first, n_fsdp):
            state = ring_step(state, step)
        return [moving for _, moving in state]

    def scatter_units(moved):
        whole = jnp.stack(moved, axis=1)
        blocks = [at(whole, place)]
        blocks += [swap(at(whole, place ^ bit), "ctx", bit) for bit in range(1, n_ctx)]
        return jnp.stack(blocks)

    def trade_square(own, received, bits):
        own, received = (part.reshape(n_ctx, -1, part.shape[1]) for part in (own, received))

        def part(bit):
            return at(own, place ^ bit).astype(f32) + at(received, place ^ bit).astype(f32)

        return [part(bit) if bit == 0 else swap(part(bit).astype(bf16), "ctx", bit) for bit in bits]

    def sum_square(parts):
        return sum(part.astype(f32) for part in parts).astype(bf16)

    def reduce_deep(mine):
        mine = mine.reshape(n_fsdp, shard_rows, -1)
        total = at(mine, depth).astype(f32)
        for bit in range(1, n_fsdp):
            total = total + swap(at(mine, depth ^ bit), "fsdp", bit).astype(f32)
        return total

    if pieces == 1:
        units_here = jnp.arange(per_core, dtype=jnp.uint32)
        units_here = jnp.concatenate(
            [core * per_core + units_here, (1 - core) * per_core + units_here]
        )
    else:
        units_here = jnp.zeros((1,), jnp.uint32)
    named = (place * own_experts + units_here).astype(f32)
    matches = info[:, None, :, :TOP] == named[None, :, None, None, None]
    hits = jnp.any(matches, axis=3)
    shares = jnp.sum(jnp.where(matches, info[:, None, :, TOP:], 0.0), axis=3)
    earlier = jnp.arange(rows)[:, None] < jnp.arange(rows)[None, :]
    rank = dot("ledr,rq->ledq", hits.astype(bf16), earlier.astype(bf16))
    slots = jnp.arange(capacity, dtype=f32)
    picks = hits[:, :, :, None, :] & (rank[:, :, :, None, :] == slots[:, None])
    slot_shares = jnp.sum(jnp.where(picks, shares[:, :, :, None, :], 0.0), axis=-1, keepdims=True)
    picks = picks.astype(bf16)

    order = place.astype(jnp.int32) ^ jnp.arange(n_ctx, dtype=jnp.int32)
    block_ids = jnp.take(block_of.reshape(n_ctx, 2), order, axis=0)
    block_ids = block_ids.reshape(-1)

    def gains_of(halves):
        pair = on_core(halves[1][:, -gap : 2 - gap], halves[0][:, -gap : 2 - gap])
        pair = pair.astype(f32).T
        return (pair[:1], pair[1:])

    near = 1 + len(early)
    parts = (slice(0, near), slice(near, n_ctx))

    def experts(layer, blocks, weights, answer, beside_near=tuple, beside_far=lambda found: ()):
        kept, arrived = ({}, [])
        back = {}
        for index, part in enumerate(parts):
            rows_here = blocks[part]
            if index:
                back[0], rows_here, found = tie(back[0], rows_here, beside_near())
                if answer:
                    arrived = [swap(block, "ctx", bit) for bit, block in zip(early, back[0][1:])]
            back[index] = []
            for j in range(own_experts):
                back[index], kept[index, j] = expert_call(
                    picks[layer, j, part],
                    slot_shares[layer, j, part],
                    rows_here,
                    weights[j],
                    shard_rows,
                    hidden,
                    back[index],
                    3 if index == 0 else 1,
                )
        if not answer:
            return (back[0] + back[1], kept)
        back[1], arrived, found = tie(back[1], arrived, beside_far(found))
        arrived += [swap(block, "ctx", bit) for bit, block in zip(late, back[1])]
        return (back[0][:1] + arrived, kept, found)

    def experts_back(layer, blocks, weights, kept, delay, beside_near, beside_far, beside_end):
        back, saved = ({}, {})
        for index, part in enumerate(parts):
            rows_here = blocks[part]
            if index:
                back[0], rows_here, found_near = tie(back[0], rows_here, beside_near())
                arrived = [swap(block, "ctx", bit) for bit, block in zip(early, back[0][1:])]
            back[index] = []
            for j in range(own_experts):
                back[index], saved[index, j] = expert_back_call(
                    picks[layer, j, part],
                    slot_shares[layer, j, part],
                    rows_here,
                    kept[index, j],
                    weights[j],
                    shard_rows,
                    back[index],
                    4 if index == 0 else 1,
                )
        back[1], arrived, saved, found_far = tie(back[1], arrived, saved, beside_far(found_near))
        arrived += [swap(block, "ctx", bit) for bit, block in zip(late, back[1])]

        def grads_of(j, saved):
            picked = [kept[index, j][0] for index in range(2)]
            both = [saved[index, j] for index in range(2)]
            return expert_grads_call(picked, both, weights[j], shard_rows)

        now = [j for j in reversed(range(own_experts)) if not delay or j >= per_core]
        grads = {j: grads_of(j, saved) for j in now}
        arrived, grads, found_end = tie(arrived, grads, beside_end(found_far))
        returned = back[0][:1] + arrived
        if len(now) == own_experts:
            own, other = cut_units([grads[j] for j in range(own_experts)])
            received = [swap(part, "section", 1) for part in other]
            return (returned, lambda earlier: (own, received), found_end)
        received = [swap(grads[j][0], "section", 1) for j in reversed(now)]

        def finish(earlier):
            ready = after(saved, earlier)
            return ([grads_of(j, ready)[0] for j in range(per_core)], received)

        return (returned, finish, found_end)

    def keep_own(first, second):
        other = swap(on_core(second, first), "section", 1)
        return own_other(on_core(first, second), other)

    dense_first, dense_second = dense_shards
    deep = gather_deep(jnp.concatenate([dense_first, dense_second[:, :enter_cut]], axis=1))
    dealt_first, dealt_second = deal_units(unit_stacks)
    deep, dealt_first, dealt_second, picks, dense_second = tie(
        deep, dealt_first, dealt_second, picks, dense_second
    )
    dense_blocks, moved, leave_shard, enter_shard = tie(
        spread(deep[:, :enter_cut]),
        ring_send([[dealt_first]]),
        deep[:, enter_cut : enter_cut + leave_cut],
        deep[:, enter_cut + leave_cut :],
    )
    leave_blocks = [leave_shard] + send(leave_shard, early)
    enter_own = join_square(dense_blocks)
    enter_first = (enter_own, swap(enter_own, "section", 1))

    first_gains = gains_of(enter_first)
    first_in = after(at(tokens, core)[0], slot_shares)
    _, first_normed, first_entered = enter_call(core, [first_in], first_gains[0], enter_first)
    first_entered, leave_blocks = tie(first_entered, leave_blocks)
    key_value = first_entered[:, qw : qw + 2 * kw]
    first_kv, leave_shard = tie(jnp.concatenate(spread(key_value)), leave_shard)
    first_attended = attend_call(block_ids, first_entered, first_kv)
    moved = ring_send(moved)
    first_attended, leave_blocks, dealt_second, moved, enter_shard, dense_second = tie(
        first_attended,
        leave_blocks + send(leave_shard, late),
        dealt_second,
        moved,
        enter_shard,
        dense_second,
    )
    enter_blocks = [enter_shard] + send(enter_shard, early)
    for _ in range(2, n_fsdp - 1):
        moved = ring_send(moved)
    leave_own = join_square(leave_blocks)
    leave_first = (leave_own, swap(leave_own, "section", 1))
    first_mid, ffn_normed = leave_call(core, first_in, first_attended, first_gains[1], leave_first)
    ffn_normed, enter_blocks = tie(ffn_normed, enter_blocks)
    blocks = spread_rows(ffn_normed)
    blocks[:near], moved, dealt_second, enter_shard, leave_shard = tie(
        blocks[:near], moved, dealt_second, enter_shard, dense_second[:, enter_cut:]
    )
    first_weights = pair_units(own_units(moved[0]))
    returned, first_kept, (moved, leave_shard, enter_blocks) = experts(
        0,
        blocks,
        first_weights,
        True,
        lambda: gather_deep(leave_shard),
        lambda found: (dealt_second, found, enter_blocks + send(enter_shard, late)),
    )
    moved = ring_send([[moved]])
    enter_own = join_square(enter_blocks)
    enter_second = (enter_own, swap(enter_own, "section", 1))
    returned, leave_shard = tie(returned, leave_shard)
    leave_blocks = [leave_shard] + send(leave_shard, early)

    second_gains = gains_of(enter_second)
    second_in, second_normed, second_entered = enter_call(
        core, [first_mid] + returned, second_gains[0], enter_second
    )
    second_entered, leave_blocks, moved = tie(second_entered, leave_blocks, moved)
    moved = ring_send(moved)
    key_value = second_entered[:, qw : qw + 2 * kw]
    for _ in range(4, n_fsdp):
        moved = ring_send(moved)
    second_kv, leave_shard = tie(jnp.concatenate(spread(key_value)), leave_shard)
    second_attended = attend_call(block_ids, second_entered, second_kv)
    second_attended, leave_blocks, moved = tie(
        second_attended, leave_blocks + send(leave_shard, late), moved
    )
    moved = ring_send(moved)
    leave_own = join_square(leave_blocks)
    leave_second = (leave_own, swap(leave_own, "section", 1))
    second_mid, ffn_normed = leave_call(
        core, second_in, second_attended, second_gains[1], leave_second
    )
    blocks = spread_rows(ffn_normed)
    blocks[:near], moved = tie(blocks[:near], moved)
    second_weights = pair_units(own_units(moved[0]))
    second_returned, second_kept = experts(1, blocks, second_weights, False)
    cotangent = after(at(out_grad, core)[0], second_returned[:near])
    cot_blocks = spread_rows(cotangent)
    cot_blocks[:near], second_returned[near:] = tie(cot_blocks[:near], second_returned[near:])

    returned, finish, (second_returned, near_parts) = experts_back(
        1,
        cot_blocks,
        second_weights,
        second_kept,
        False,
        lambda: second_returned,
        lambda found: found,
        lambda found: (found, [swap(found[bit], "ctx", bit) for bit in early]),
    )
    far_parts = [swap(second_returned[bit], "ctx", bit) for bit in late]
    units_moving = [ring_start(*pair) for pair in zip(*finish(()))]
    after_rows, term, d_attended, *grads = leave_back_call(
        core,
        returned,
        second_gains[1],
        second_mid,
        cotangent,
        second_attended,
        leave_second,
    )
    leave_grads = (grads[0], swap(grads[1], "section", 1))
    d_queries, d_key_value = attend_back_call(block_ids, second_entered, second_kv, d_attended)
    d_queries, d_key_value, leave_grads, far_parts = tie(
        d_queries, d_key_value, leave_grads, far_parts
    )
    second_parts = second_returned[:1] + near_parts + far_parts
    second_out = second_mid + sum(part.astype(f32) for part in second_parts)
    d_key_value, units_moving = tie(gather_back(d_key_value), ring_move(units_moving))
    units_moving = ring_move(ring_add(units_moving, 1))
    leave_parts = trade_square(*leave_grads, range(n_ctx))
    second_entry, cotangent, *grads = enter_back_call(
        core,
        d_queries,
        d_key_value,
        second_gains[0],
        second_in,
        second_normed,
        after_rows,
        term,
        enter_second,
    )
    cotangent, grads, leave_parts, layer_rows = tie(
        cotangent, grads, leave_parts, (second_in, second_out.astype(bf16))
    )
    enter_grads = (grads[0], swap(grads[1], "section", 1))

    blocks = spread_rows(cotangent)
    blocks[:near], enter_grads, layer_rows = tie(blocks[:near], enter_grads, layer_rows)

    def dense_sums(parts):
        moving = [sum_square(some) for some in (parts, leave_parts)]
        return reduce_deep(jnp.concatenate(moving, axis=1))

    returned, finish, (units_moving, layer_outs, second_dense) = experts_back(
        0,
        blocks,
        first_weights,
        first_kept,
        False,
        lambda: (units_moving, trade_square(*enter_grads, [0, *early]), enter_grads),
        lambda found: (
            ring_last(found[0]),
            keep_own(*layer_rows),
            found[1] + trade_square(*found[2], late),
        ),
        lambda found: (found[0], found[1], dense_sums(found[2])),
    )
    second_moved = [moving for _, moving in ring_add(units_moving, n_fsdp - 1)]
    own, received = finish(())
    after_rows, term, d_attended, *grads = leave_back_call(
        core,
        returned,
        first_gains[1],
        first_mid,
        cotangent,
        first_attended,
        leave_first,
    )
    units_moving = [ring_start(*pair) for pair in zip(own, received)]
    leave_grads = (grads[0], swap(grads[1], "section", 1))
    d_queries, d_key_value = attend_back_call(block_ids, first_entered, first_kv, d_attended)
    d_queries, d_key_value, leave_grads = tie(d_queries, d_key_value, leave_grads)
    d_key_value, units_moving, leave_grads = tie(
        gather_back(d_key_value), ring_move(units_moving), leave_grads
    )
    leave_parts = trade_square(*leave_grads, [0, *early])
    units_moving = ring_move(ring_add(units_moving, 1))
    first_entry, _, *grads = enter_back_call(
        core,
        d_queries,
        d_key_value,
        first_gains[0],
        first_in,
        first_normed,
        after_rows,
        term,
        enter_first,
    )
    grads, leave_parts, leave_grads = tie(grads, leave_parts, leave_grads)
    enter_grads = (grads[0], swap(grads[1], "section", 1))
    enter_parts, leave_parts, first_entry = tie(
        trade_square(*enter_grads, range(n_ctx)),
        leave_parts + trade_square(*leave_grads, late),
        first_entry,
    )
    first_moving = [sum_square(parts) for parts in (enter_parts, leave_parts)]
    first_dense = reduce_deep(jnp.concatenate(first_moving, axis=1))
    scattered = scatter_units(ring_rest(ring_add(units_moving, 2), 3) + second_moved)
    first_scattered, second_scattered = (scattered[:, :per_core], scattered[:, per_core:])

    layer_out = jnp.stack(layer_outs)
    input_grads = jnp.stack(keep_own(first_entry, second_entry))
    low_dense, high_dense = keep_own(first_dense, second_dense)
    enter_grad = jnp.concatenate([low_dense[:, :enter_cut], high_dense[:, :enter_cut]], axis=1)
    grad_out = jnp.concatenate([low_dense[:, enter_cut:], high_dense[:, enter_cut:]], axis=1)
    grad_gains = enter_grad[:, qw + 2 * kw :]
    mine = on_core(first_scattered, second_scattered)
    other = swap(on_core(second_scattered, first_scattered), "section", 1)
    if aligned and pieces == 1:
        grad_gate, grad_up, grad_down = finish_call(mine, other, shard_rows, hidden, place, core)
    else:
        sides = [jnp.take(part, order, axis=0) for part in own_other(mine, other)]
        if pieces == 1:
            whole = jnp.stack(sides, axis=1).reshape(EXPERTS, unit_rows, width)
        else:
            whole = jnp.concatenate([side[:, 0] for side in sides], axis=2)
        pairs = whole[:, :shard_rows].astype(f32).reshape(EXPERTS, shard_rows, 2, 2, cut)
        grad_gate = pairs[:, :, :, 0].reshape(EXPERTS, shard_rows, hidden)
        grad_up = pairs[:, :, :, 1].reshape(EXPERTS, shard_rows, hidden)
        grad_down = whole[:, shard_rows:].astype(f32)
    return (
        layer_out[None, :, None],
        input_grads[None, :, None],
        grad_gains[:, 0][None],
        enter_grad[:, :qw][None],
        enter_grad[:, qw : qw + kw][None],
        enter_grad[:, qw + kw : qw + 2 * kw][None],
        grad_out[None],
        grad_gains[:, 1][None],
        grad_gate[None],
        grad_up[None],
        grad_down[None],
    )


def solution(mesh):
    rows_placed = P(None, "fsdp", "ctx", None)
    kept_placed = P("section", None, "fsdp", "ctx", None)
    gain_placed = P("section", ("ctx", "fsdp"))
    dense_placed = P("section", ("ctx", "fsdp"), None)
    expert_placed = P("section", None, ("ctx", "fsdp"), None)
    dense_all = (dense_placed,) * 4
    expert_all = (expert_placed,) * 3
    layer_placed = (gain_placed,) + dense_all + (gain_placed,) + expert_all
    return jax.shard_map(
        body,
        mesh=mesh,
        in_specs=(rows_placed, P(), kept_placed, kept_placed) + layer_placed + (rows_placed,),
        out_specs=(kept_placed, kept_placed) + layer_placed,
        check_vma=False,
    )
```

profile of v0, /device:TPU:0, one launch (start us, length us, event | category | flops | bytes accessed | tf_op | source)
XLA Modules:
  0.0 1044.1 jit_solution(14363373770425666649)
XLA Ops:
  39.1 6.9 collective-permute-done.1.refs_1_
  48.8 29.9 %collective-permute-done.2.refs_2_ = bf16[96,3072]{1,0:T(8,128)(2,1)S(1)} collective-permute-done((bf16[96,3072]{1,0:T(8,128)(2,1)S(1)}, bf16[96,3072]{1,0:T(8,128)(2,1)S(1)}, u32[]{:S(2)}, u32[]{:S(2)}) %collective-permute-start.2) | collective-permute-done | bytes 589856 | tf_op jit(solution)/shard_map/ppermute | solution.py:27
  89.8 10.7 %collective-permute-start.15 = (bf16[4,1,144,1536]{3,2,1,0:T(8,128)(2,1)}, bf16[4,1,144,1536]{3,2,1,0:T(8,128)(2,1)}, u32[]{:S(2)}, u32[]{:S(2)}) collective-permute-start(bf16[4,1,144,1536]{3,2,1,0:T(8,128)(2,1)} %get-tuple-element.441.refs_0_), channel_id=1, source_target_pairs={{0,2},{2,3},{3,1},{1,0},{4,6},{6,7},{7,5},{5,4},{8,10},{10,11},{11... | collective-permute-start | bytes 5308424 | tf_op jit(solution)/shard_map/ppermute | solution.py:902
  105.1 19.0 %collective-permute-done.12.refs_1_ = bf16[384,1152]{1,0:T(8,128)(2,1)S(1)} collective-permute-done((bf16[384,1152]{1,0:T(8,128)(2,1)S(1)}, bf16[384,1152]{1,0:T(8,128)(2,1)S(1)}, u32[]{:S(2)}, u32[]{:S(2)}) %collective-permute-start.12) | collective-permute-done | bytes 884768 | tf_op jit(solution)/shard_map/ppermute | solution.py:27
  124.1 15.2 %collective-permute-done.13.refs_2_ = bf16[384,1152]{1,0:T(8,128)(2,1)S(1)} collective-permute-done((bf16[384,1152]{1,0:T(8,128)(2,1)S(1)}, bf16[384,1152]{1,0:T(8,128)(2,1)S(1)}, u32[]{:S(2)}, u32[]{:S(2)}) %collective-permute-start.13) | collective-permute-done | bytes 884768 | tf_op jit(solution)/shard_map/ppermute | solution.py:27
  156.8 6.9 enter.2
  170.1 6.7 collective-permute-done.21
  185.0 12.0 %attend.2.attended_ref = bf16[256,1536]{1,0:T(8,128)(2,1)} custom-call(s32[8]{0:T(128)} %select_n.165.ids_ref, bf16[256,2304]{1,0:T(8,128)(2,1)} %get-tuple-element.414.query_ref, bf16[1024,512]{1,0:T(8,128)(2,1)} %pad_maximum_fusion.4.key_ref.value_ref, bf16[1024,512]{1,0:T(8,128)(2,1)} %pad_maximum_fusion.4.key_ref.value_ref), custom_call_target="tpu_custom_call" | custom-call | flops 1000000000 | bytes 3000000 | tf_op jit(solution)/shard_map/attend/pallas_call | solution.py:100
  206.6 6.0 leave.2
  212.5 11.5 %collective-permute-done.25.refs_1_ = bf16[384,1152]{1,0:T(8,128)(2,1)} collective-permute-done((bf16[384,1152]{1,0:T(8,128)(2,1)}, bf16[384,1152]{1,0:T(8,128)(2,1)}, u32[]{:S(2)}, u32[]{:S(2)}) %collective-permute-start.25) | collective-permute-done | bytes 884768 | tf_op jit(solution)/shard_map/ppermute | solution.py:27
  229.3 14.4 %collective-permute-done.27.refs_1_ = bf16[256,1536]{1,0:T(8,128)(2,1)S(1)} collective-permute-done((bf16[256,1536]{1,0:T(8,128)(2,1)}, bf16[256,1536]{1,0:T(8,128)(2,1)S(1)}, u32[]{:S(2)}, u32[]{:S(2)}) %collective-permute-start.27) | collective-permute-done | bytes 786464 | tf_op jit(solution)/shard_map/ppermute | solution.py:27
  245.2 7.2 order.2
  261.1 12.2 %expert.8 = (bf16[256,1536]{1,0:T(8,128)(2,1)}, bf16[256,1536]{1,0:T(8,128)(2,1)}, bf16[256,1536]{1,0:T(8,128)(2,1)}, bf16[480,1536]{1,0:T(8,128)(2,1)}, f32[480,768]{1,0:T(8,128)}, /*index=5*/f32[480,768]{1,0:T(8,128)}) custom-call(bf16[3,160,256]{2,1,0:T(8,128)(2,1)} %get-tuple-element.918.pick_ref, f32[3,160,1]{2,1,0:T(8,128)} %copy.330.share_ref, ...), custom_call_target="tpu_custom_call" | custom-call | flops 3000000000 | bytes 9000000 | tf_op jit(solution)/shard_map/expert/pallas_call | solution.py:262
  278.6 12.8 %expert.9 = (bf16[256,1536]{1,0:T(8,128)(2,1)}, bf16[256,1536]{1,0:T(8,128)(2,1)}, bf16[256,1536]{1,0:T(8,128)(2,1)}, bf16[480,1536]{1,0:T(8,128)(2,1)}, f32[480,768]{1,0:T(8,128)}, /*index=5*/f32[480,768]{1,0:T(8,128)}) custom-call(bf16[3,160,256]{2,1,0:T(8,128)(2,1)} %get-tuple-element.919.pick_ref, f32[3,160,1]{2,1,0:T(8,128)} %copy.331.share_ref, ...), custom_call_target="tpu_custom_call" | custom-call | flops 3000000000 | bytes 9000000 | tf_op jit(solution)/shard_map/expert/pallas_call | solution.py:262
  296.6 6.6 expert.10
  303.2 7.3 expert.11
  318.9 18.8 %collective-permute-done.39.refs_4_ = bf16[256,1536]{1,0:T(8,128)(2,1)S(1)} collective-permute-done((bf16[256,1536]{1,0:T(8,128)(2,1)S(1)}, bf16[256,1536]{1,0:T(8,128)(2,1)S(1)}, u32[]{:S(2)}, u32[]{:S(2)}) %collective-permute-start.39) | collective-permute-done | bytes 786464 | tf_op jit(solution)/shard_map/ppermute | solution.py:27
  342.3 8.4 enter.3
  353.8 5.5 collective-permute-done.42.refs_1_
  365.3 6.7 collective-permute-done.45
  378.1 12.0 %attend.3.attended_ref = bf16[256,1536]{1,0:T(8,128)(2,1)} custom-call(s32[8]{0:T(128)} %select_n.165.ids_ref, bf16[256,2304]{1,0:T(8,128)(2,1)} %get-tuple-element.489.query_ref, bf16[1024,512]{1,0:T(8,128)(2,1)} %pad_maximum_fusion.5.key_ref.value_ref, bf16[1024,512]{1,0:T(8,128)(2,1)} %pad_maximum_fusion.5.key_ref.value_ref), custom_call_target="tpu_custom_call" | custom-call | flops 1000000000 | bytes 3000000 | tf_op jit(solution)/shard_map/attend/pallas_call | solution.py:100
  393.1 6.4 collective-permute-done.47.refs_2_
  407.9 5.9 leave.3
  415.8 17.8 %collective-permute-done.49.refs_1_ = bf16[256,1536]{1,0:T(8,128)(2,1)S(1)} collective-permute-done((bf16[256,1536]{1,0:T(8,128)(2,1)}, bf16[256,1536]{1,0:T(8,128)(2,1)S(1)}, u32[]{:S(2)}, u32[]{:S(2)}) %collective-permute-start.49) | collective-permute-done | bytes 786464 | tf_op jit(solution)/shard_map/ppermute | solution.py:27
  434.5 10.7 %collective-permute-done.51.refs_3_ = bf16[4,1,144,1536]{3,2,1,0:T(8,128)(2,1)} collective-permute-done((bf16[4,1,144,1536]{3,2,1,0:T(8,128)(2,1)}, bf16[4,1,144,1536]{3,2,1,0:T(8,128)(2,1)}, u32[]{:S(2)}, u32[]{:S(2)}) %collective-permute-start.51) | collective-permute-done | bytes 1769504 | tf_op jit(solution)/shard_map/ppermute | solution.py:902
  445.2 7.0 order.3
  455.5 12.1 %expert.12 = (bf16[256,1536]{1,0:T(8,128)(2,1)}, bf16[256,1536]{1,0:T(8,128)(2,1)}, bf16[256,1536]{1,0:T(8,128)(2,1)}, bf16[480,1536]{1,0:T(8,128)(2,1)}, f32[480,768]{1,0:T(8,128)}, /*index=5*/f32[480,768]{1,0:T(8,128)}) custom-call(bf16[3,160,256]{2,1,0:T(8,128)(2,1)} %get-tuple-element.916.pick_ref, f32[3,160,1]{2,1,0:T(8,128)} %copy.336.share_ref, ...), custom_call_target="tpu_custom_call" | custom-call | flops 3000000000 | bytes 9000000 | tf_op jit(solution)/shard_map/expert/pallas_call | solution.py:262
  467.7 12.8 %expert.13 = (bf16[256,1536]{1,0:T(8,128)(2,1)}, bf16[256,1536]{1,0:T(8,128)(2,1)}, bf16[256,1536]{1,0:T(8,128)(2,1)}, bf16[480,1536]{1,0:T(8,128)(2,1)}, f32[480,768]{1,0:T(8,128)}, /*index=5*/f32[480,768]{1,0:T(8,128)}) custom-call(bf16[3,160,256]{2,1,0:T(8,128)(2,1)} %get-tuple-element.917.pick_ref, f32[3,160,1]{2,1,0:T(8,128)} %copy.337.share_ref, ...), custom_call_target="tpu_custom_call" | custom-call | flops 3000000000 | bytes 9000000 | tf_op jit(solution)/shard_map/expert/pallas_call | solution.py:262
  484.1 6.5 expert.14
  490.6 9.6 collective-permute-done.54.refs_1_
  502.5 7.2 expert.15
  509.8 13.4 %expert_back.8 = (bf16[256,1536]{1,0:T(8,128)(2,1)}, bf16[256,1536]{1,0:T(8,128)(2,1)}, bf16[256,1536]{1,0:T(8,128)(2,1)}, bf16[480,1536]{1,0:T(8,128)(2,1)}, bf...) custom-call(bf16[3,160,256]{2,1,0:T(8,128)(2,1)} %get-tuple-element.916.pick_ref, ...), custom_call_target="tpu_custom_call" | custom-call | flops 4000000000 | bytes 12000000 | tf_op jit(solution)/shard_map/expert_back/pallas_call | solution.py:322
  523.1 14.1 %expert_back.9 = (bf16[256,1536]{1,0:T(8,128)(2,1)}, bf16[256,1536]{1,0:T(8,128)(2,1)}, bf16[256,1536]{1,0:T(8,128)(2,1)}, bf16[480,1536]{1,0:T(8,128)(2,1)}, bf...) custom-call(bf16[3,160,256]{2,1,0:T(8,128)(2,1)} %get-tuple-element.917.pick_ref, ...), custom_call_target="tpu_custom_call" | custom-call | flops 4000000000 | bytes 12000000 | tf_op jit(solution)/shard_map/expert_back/pallas_call | solution.py:322
  539.4 7.5 expert_back.10
  546.9 8.0 expert_back.11
  559.8 13.6 %expert_grads.4 = bf16[16,144,1536]{2,1,0:T(8,128)(2,1)} custom-call(bf16[480,1536]{1,0:T(8,128)(2,1)} %get-tuple-element.580.refs_0_, bf16[160,1536]{1,0:T(8,128)(2,1)} %get-tuple-element.581.refs_1_, bf16[480,1536]{1,0:T(8,128)(2,1)} %get-tuple-element.582.refs_2_, bf16[160,1536]{1,0:T(8,128)(2,1)} %get-tuple-element.583.refs_3_, ...), custom_call_target="tpu_custom_call" | custom-call | flops 1000000000 | bytes 3000000 | tf_op jit(solution)/shard_map/expert_grads/pallas_call | solution.py:388
  573.4 13.9 %expert_grads.5 = bf16[16,144,1536]{2,1,0:T(8,128)(2,1)} custom-call(bf16[480,1536]{1,0:T(8,128)(2,1)} %get-tuple-element.590.refs_0_, bf16[160,1536]{1,0:T(8,128)(2,1)} %get-tuple-element.591.refs_1_, bf16[480,1536]{1,0:T(8,128)(2,1)} %get-tuple-element.592.refs_2_, bf16[160,1536]{1,0:T(8,128)(2,1)} %get-tuple-element.593.refs_3_, ...), custom_call_target="tpu_custom_call" | custom-call | flops 1000000000 | bytes 3000000 | tf_op jit(solution)/shard_map/expert_grads/pallas_call | solution.py:388
  591.4 11.3 %leave_back.2 = (f32[256,1536]{1,0:T(8,128)}, bf16[256,1536]{1,0:T(8,128)(2,1)}, bf16[256,1536]{1,0:T(8,128)(2,1)}, bf16[1536,768]{1,0:T(8,128)(2,1)}, bf16[1536,768]{1,0:T(8,128)(2,1)}) custom-call(s32[1]{0:T(128)} %bitcast.48.core_ref, f32[1,1536]{1,0:T(1,128)} %copy.344.gain_ref, f32[256,1536]{1,0:T(8,128)} %get-tuple-element.502.mid_ref, ...), custom_call_target="tpu_custom_call" | custom-call | flops 8000000000 | bytes 24000000 | tf_op jit(solution)/shard_map/leave_back/pallas_call | solution.py:439
  611.4 16.6 %attend_back.2 = (bf16[256,1536]{1,0:T(8,128)(2,1)}, bf16[256,512]{1,0:T(8,128)(2,1)}, bf16[256,512]{1,0:T(8,128)(2,1)}, bf16[256,512]{1,0:T(8,128)(2,1)}, bf16[256,512]{1,0:T(8,128)(2,1)}) custom-call(s32[8]{0:T(128)} %select_n.165.ids_ref, bf16[256,2304]{1,0:T(8,128)(2,1)} %get-tuple-element.489.query_ref, ...), custom_call_target="tpu_custom_call" | custom-call | flops 1000000000 | bytes 3000000 | tf_op jit(solution)/shard_map/attend_back/pallas_call | solution.py:150
  649.3 13.5 %enter_back.2 = (f32[256,1536]{1,0:T(8,128)}, bf16[256,1536]{1,0:T(8,128)(2,1)}, bf16[1536,1152]{1,0:T(8,128)(2,1)}, bf16[1536,1152]{1,0:T(8,128)(2,1)}) custom-call(s32[1]{0:T(128)} %bitcast.48.core_ref, f32[1,1536]{1,0:T(1,128)} %copy.347.gain_ref, bf16[256,1536]{1,0:T(8,128)(2,1)} %get-tuple-element.688.rows_ref, ...), custom_call_target="tpu_custom_call" | custom-call | flops 12999999488 | bytes 39000000 | tf_op jit(solution)/shard_map/enter_back/pallas_call | solution.py:439
  662.8 6.7 collective-permute-done.70
  671.5 4.7 fusion.5
  676.9 12.7 %collective-permute-done.72.refs_1_ = bf16[256,1536]{1,0:T(8,128)(2,1)S(1)} collective-permute-done((bf16[256,1536]{1,0:T(8,128)(2,1)}, bf16[256,1536]{1,0:T(8,128)(2,1)S(1)}, u32[]{:S(2)}, u32[]{:S(2)}) %collective-permute-start.72) | collective-permute-done | bytes 786464 | tf_op jit(solution)/shard_map/ppermute | solution.py:27
  696.8 13.8 %expert_back.12 = (bf16[256,1536]{1,0:T(8,128)(2,1)}, bf16[256,1536]{1,0:T(8,128)(2,1)}, bf16[256,1536]{1,0:T(8,128)(2,1)}, bf16[480,1536]{1,0:T(8,128)(2,1)}, b...) custom-call(bf16[3,160,256]{2,1,0:T(8,128)(2,1)} %get-tuple-element.918.pick_ref, ...), custom_call_target="tpu_custom_call" | custom-call | flops 4000000000 | bytes 12000000 | tf_op jit(solution)/shard_map/expert_back/pallas_call | solution.py:322
  710.6 14.0 %expert_back.13 = (bf16[256,1536]{1,0:T(8,128)(2,1)}, bf16[256,1536]{1,0:T(8,128)(2,1)}, bf16[256,1536]{1,0:T(8,128)(2,1)}, bf16[480,1536]{1,0:T(8,128)(2,1)}, b...) custom-call(bf16[3,160,256]{2,1,0:T(8,128)(2,1)} %get-tuple-element.919.pick_ref, ...), custom_call_target="tpu_custom_call" | custom-call | flops 4000000000 | bytes 12000000 | tf_op jit(solution)/shard_map/expert_back/pallas_call | solution.py:322
  724.6 7.7 collective-permute-done.75.refs_0_
  732.5 4.6 fusion.4
  748.1 7.7 expert_back.14
  755.7 7.8 expert_back.15
  763.6 15.0 %collective-permute-done.80.refs_2_ = bf16[256,1536]{1,0:T(8,128)(2,1)} collective-permute-done((bf16[256,1536]{1,0:T(8,128)(2,1)}, bf16[256,1536]{1,0:T(8,128)(2,1)}, u32[]{:S(2)}, u32[]{:S(2)}) %collective-permute-start.80) | collective-permute-done | bytes 786464 | tf_op jit(solution)/shard_map/ppermute | solution.py:27
  786.5 13.6 %expert_grads.6 = bf16[16,144,1536]{2,1,0:T(8,128)(2,1)} custom-call(bf16[480,1536]{1,0:T(8,128)(2,1)} %get-tuple-element.698.refs_0_, bf16[160,1536]{1,0:T(8,128)(2,1)} %get-tuple-element.699.refs_1_, bf16[480,1536]{1,0:T(8,128)(2,1)} %get-tuple-element.700.refs_2_, bf16[160,1536]{1,0:T(8,128)(2,1)} %get-tuple-element.701.refs_3_, ...), custom_call_target="tpu_custom_call" | custom-call | flops 1000000000 | bytes 3000000 | tf_op jit(solution)/shard_map/expert_grads/pallas_call | solution.py:388
  800.1 13.8 %expert_grads.7 = bf16[16,144,1536]{2,1,0:T(8,128)(2,1)} custom-call(bf16[480,1536]{1,0:T(8,128)(2,1)} %get-tuple-element.708.refs_0_, bf16[160,1536]{1,0:T(8,128)(2,1)} %get-tuple-element.709.refs_1_, bf16[480,1536]{1,0:T(8,128)(2,1)} %get-tuple-element.710.refs_2_, bf16[160,1536]{1,0:T(8,128)(2,1)} %get-tuple-element.711.refs_3_, ...), custom_call_target="tpu_custom_call" | custom-call | flops 1000000000 | bytes 3000000 | tf_op jit(solution)/shard_map/expert_grads/pallas_call | solution.py:388
  815.3 11.3 %leave_back.3 = (f32[256,1536]{1,0:T(8,128)}, bf16[256,1536]{1,0:T(8,128)(2,1)}, bf16[256,1536]{1,0:T(8,128)(2,1)}, bf16[1536,768]{1,0:T(8,128)(2,1)}, bf16[1536,768]{1,0:T(8,128)(2,1)}) custom-call(s32[1]{0:T(128)} %bitcast.48.core_ref, f32[1,1536]{1,0:T(1,128)} %copy.329.gain_ref, f32[256,1536]{1,0:T(8,128)} %get-tuple-element.474.refs_0_.mid_ref, ...), custom_call_target="tpu_custom_call" | custom-call | flops 8000000000 | bytes 24000000 | tf_op jit(solution)/shard_map/leave_back/pallas_call | solution.py:439
  831.2 16.6 %attend_back.3 = (bf16[256,1536]{1,0:T(8,128)(2,1)}, bf16[256,512]{1,0:T(8,128)(2,1)}, bf16[256,512]{1,0:T(8,128)(2,1)}, bf16[256,512]{1,0:T(8,128)(2,1)}, bf16[256,512]{1,0:T(8,128)(2,1)}) custom-call(s32[8]{0:T(128)} %select_n.165.ids_ref, bf16[256,2304]{1,0:T(8,128)(2,1)} %get-tuple-element.414.query_ref, ...), custom_call_target="tpu_custom_call" | custom-call | flops 1000000000 | bytes 3000000 | tf_op jit(solution)/shard_map/attend_back/pallas_call | solution.py:150
  851.4 5.9 collective-permute-done.89.refs_1_
  857.3 5.6 collective-permute-done.90.refs_2_
  862.9 8.9 collective-permute-done.93
  883.1 13.6 %enter_back.3 = (f32[256,1536]{1,0:T(8,128)}, bf16[256,1536]{1,0:T(8,128)(2,1)}, bf16[1536,1152]{1,0:T(8,128)(2,1)}, bf16[1536,1152]{1,0:T(8,128)(2,1)}) custom-call(s32[1]{0:T(128)} %bitcast.48.core_ref, f32[1,1536]{1,0:T(1,128)} %copy.328.gain_ref, bf16[256,1536]{1,0:T(8,128)(2,1)} %get-tuple-element.411.refs_0_.rows_ref, ...), custom_call_target="tpu_custom_call" | custom-call | flops 12999999488 | bytes 39000000 | tf_op jit(solution)/shard_map/enter_back/pallas_call | solution.py:439
  896.8 24.4 %collective-permute-done.106 = bf16[4,144,1536]{2,1,0:T(8,128)(2,1)} collective-permute-done((bf16[4,144,1536]{2,1,0:T(8,128)(2,1)}, bf16[4,144,1536]{2,1,0:T(8,128)(2,1)}, u32[]{:S(2)}, u32[]{:S(2)}) %collective-permute-start.106) | collective-permute-done | bytes 1769504 | tf_op jit(solution)/shard_map/ppermute | solution.py:943
  940.7 23.6 %collective-permute-done.107 = bf16[4,144,1536]{2,1,0:T(8,128)(2,1)S(1)} collective-permute-done((bf16[4,144,1536]{2,1,0:T(8,128)(2,1)S(1)}, bf16[4,144,1536]{2,1,0:T(8,128)(2,1)S(1)}, u32[]{:S(2)}, u32[]{:S(2)}) %collective-permute-start.107) | collective-permute-done | bytes 1769504 | tf_op jit(solution)/shard_map/ppermute | solution.py:943
  971.6 18.5 %collective-permute-done.99 = bf16[384,1152]{1,0:T(8,128)(2,1)S(1)} collective-permute-done((bf16[384,1152]{1,0:T(8,128)(2,1)S(1)}, bf16[384,1152]{1,0:T(8,128)(2,1)S(1)}, u32[]{:S(2)}, u32[]{:S(2)}) %collective-permute-start.99) | collective-permute-done | bytes 884768 | tf_op jit(solution)/shard_map/ppermute | solution.py:27
  995.8 13.2 %collective-permute-done.110 = bf16[2,144,1536]{2,1,0:T(8,128)(2,1)S(1)} collective-permute-done((bf16[2,144,1536]{2,1,0:T(8,128)(2,1)S(1)}, bf16[2,144,1536]{2,1,0:T(8,128)(2,1)S(1)}, u32[]{:S(2)}, u32[]{:S(2)}) %collective-permute-start.110) | collective-permute-done | bytes 884768 | tf_op jit(solution)/shard_map/ppermute | solution.py:27
  1009.2 15.2 %collective-permute-done.109 = bf16[2,144,1536]{2,1,0:T(8,128)(2,1)S(1)} collective-permute-done((bf16[2,144,1536]{2,1,0:T(8,128)(2,1)S(1)}, bf16[2,144,1536]{2,1,0:T(8,128)(2,1)S(1)}, u32[]{:S(2)}, u32[]{:S(2)}) %collective-permute-start.109) | collective-permute-done | bytes 884768 | tf_op jit(solution)/shard_map/ppermute | solution.py:27
  1032.6 8.7 finish.1
  (459 shorter events, 309.7 us)
Async XLA Ops:
  7.8 20.6 %collective-permute-start.4 = (bf16[4,1,144,1536]{3,2,0,1:T(8,128)(2,1)}, bf16[4,1,144,1536]{3,2,0,1:T(8,128)(2,1)}, u32[]{:S(2)}, u32[]{:S(2)}) collective-permute-start(bf16[4,1,144,1536]{3,2,0,1:T(8,128)(2,1)} %dynamic-slice_bitcast_fusion), channel_id=1, source_target_pairs={{0,16},{16,0},{1,17},{17,1},{2,18},{18,2},{3,19},{19,3},{4,20},{20... | collective-permute-start | bytes 5308424 | tf_op jit(solution)/shard_map/ppermute | solution.py:27
  33.0 51.0 %collective-permute-start.5 = (bf16[2,1,144,1536]{3,2,1,0:T(8,128)(2,1)S(1)}, bf16[2,1,144,1536]{3,2,1,0:T(8,128)(2,1)S(1)}, u32[]{:S(2)}, u32[]{:S(2)}) collective-permute-start(bf16[2,1,144,1536]{3,2,1,0:T(8,128)(2,1)S(1)} %get-tuple-element.898), channel_id=1, source_target_pairs={{0,4},{4,0},{8,12},{12,8},{1,5},{5,1},{9,13},{13,9},{2,6},{6,2},{1... | collective-permute-start | bytes 2654216 | tf_op jit(solution)/shard_map/ppermute | solution.py:27
  33.5 50.4 %collective-permute-start.6 = (bf16[2,1,144,1536]{3,2,1,0:T(8,128)(2,1)S(1)}, bf16[2,1,144,1536]{3,2,1,0:T(8,128)(2,1)S(1)}, u32[]{:S(2)}, u32[]{:S(2)}) collective-permute-start(bf16[2,1,144,1536]{3,2,1,0:T(8,128)(2,1)S(1)} %get-tuple-element.899), channel_id=1, source_target_pairs={{0,8},{4,12},{8,0},{12,4},{1,9},{5,13},{9,1},{13,5},{2,10},{6,14},... | collective-permute-start | bytes 2654216 | tf_op jit(solution)/shard_map/ppermute | solution.py:27
  35.0 48.9 %collective-permute-start.7 = (bf16[2,1,144,1536]{3,2,1,0:T(8,128)(2,1)S(1)}, bf16[2,1,144,1536]{3,2,1,0:T(8,128)(2,1)S(1)}, u32[]{:S(2)}, u32[]{:S(2)}) collective-permute-start(bf16[2,1,144,1536]{3,2,1,0:T(8,128)(2,1)S(1)} %get-tuple-element.896), channel_id=1, source_target_pairs={{0,12},{4,8},{8,4},{12,0},{1,13},{5,9},{9,5},{13,1},{2,14},{6,10},... | collective-permute-start | bytes 2654216 | tf_op jit(solution)/shard_map/ppermute | solution.py:27
  36.5 42.3 %collective-permute-start.2 = (bf16[96,3072]{1,0:T(8,128)(2,1)S(1)}, bf16[96,3072]{1,0:T(8,128)(2,1)S(1)}, u32[]{:S(2)}, u32[]{:S(2)}) collective-permute-start(bf16[96,3072]{1,0:T(8,128)(2,1)S(1)} %pad_maximum_fusion.7.refs_0_), channel_id=1, source_target_pairs={{0,2},{1,3},{2,0},{3,1},{4,6},{5,7},{6,4},{7,5},{8,10},{9,11},{10,... | collective-permute-start | bytes 1769480 | tf_op jit(solution)/shard_map/ppermute | solution.py:27
  46.0 32.7 %collective-permute-start.3 = (bf16[96,3072]{1,0:T(8,128)(2,1)S(1)}, bf16[96,3072]{1,0:T(8,128)(2,1)S(1)}, u32[]{:S(2)}, u32[]{:S(2)}) collective-permute-start(bf16[96,3072]{1,0:T(8,128)(2,1)S(1)} %pad_maximum_fusion.7.refs_0_), channel_id=1, source_target_pairs={{0,3},{1,2},{2,1},{3,0},{4,7},{5,6},{6,5},{7,4},{8,11},{9,10},{10,... | collective-permute-start | bytes 1769480 | tf_op jit(solution)/shard_map/ppermute | solution.py:27
  89.8 51.8 %collective-permute-start.15 = (bf16[4,1,144,1536]{3,2,1,0:T(8,128)(2,1)}, bf16[4,1,144,1536]{3,2,1,0:T(8,128)(2,1)}, u32[]{:S(2)}, u32[]{:S(2)}) collective-permute-start(bf16[4,1,144,1536]{3,2,1,0:T(8,128)(2,1)} %get-tuple-element.441.refs_0_), channel_id=1, source_target_pairs={{0,2},{2,3},{3,1},{1,0},{4,6},{6,7},{7,5},{5,4},{8,10},{10,11},{11... | collective-permute-start | bytes 5308424 | tf_op jit(solution)/shard_map/ppermute | solution.py:902
  101.5 22.6 %collective-permute-start.12 = (bf16[384,1152]{1,0:T(8,128)(2,1)S(1)}, bf16[384,1152]{1,0:T(8,128)(2,1)S(1)}, u32[]{:S(2)}, u32[]{:S(2)}) collective-permute-start(bf16[384,1152]{1,0:T(8,128)(2,1)S(1)} %get-tuple-element.407.refs_0_), channel_id=1, source_target_pairs={{0,4},{4,0},{8,12},{12,8},{1,5},{5,1},{9,13},{13,9},{2,6},{6,2},{1... | collective-permute-start | bytes 2654216 | tf_op jit(solution)/shard_map/ppermute | solution.py:27
  102.3 37.0 %collective-permute-start.13 = (bf16[384,1152]{1,0:T(8,128)(2,1)S(1)}, bf16[384,1152]{1,0:T(8,128)(2,1)S(1)}, u32[]{:S(2)}, u32[]{:S(2)}) collective-permute-start(bf16[384,1152]{1,0:T(8,128)(2,1)S(1)} %get-tuple-element.407.refs_0_), channel_id=1, source_target_pairs={{0,8},{4,12},{8,0},{12,4},{1,9},{5,13},{9,1},{13,5},{2,10},{6,14},... | collective-permute-start | bytes 2654216 | tf_op jit(solution)/shard_map/ppermute | solution.py:27
  103.9 36.7 %collective-permute-start.14 = (bf16[384,1152]{1,0:T(8,128)(2,1)S(1)}, bf16[384,1152]{1,0:T(8,128)(2,1)S(1)}, u32[]{:S(2)}, u32[]{:S(2)}) collective-permute-start(bf16[384,1152]{1,0:T(8,128)(2,1)S(1)} %get-tuple-element.407.refs_0_), channel_id=1, source_target_pairs={{0,12},{4,8},{8,4},{12,0},{1,13},{5,9},{9,5},{13,1},{2,14},{6,10},... | collective-permute-start | bytes 2654216 | tf_op jit(solution)/shard_map/ppermute | solution.py:27
  151.7 45.3 %collective-permute-start.23 = (bf16[4,1,144,1536]{3,2,1,0:T(8,128)(2,1)}, bf16[4,1,144,1536]{3,2,1,0:T(8,128)(2,1)}, u32[]{:S(2)}, u32[]{:S(2)}) collective-permute-start(bf16[4,1,144,1536]{3,2,1,0:T(8,128)(2,1)} %collective-permute-done.15.refs_1_), channel_id=1, source_target_pairs={{0,2},{2,3},{3,1},{1,0},{4,6},{6,7},{7,5},{5,4},{8,10},{10,11},{11... | collective-permute-start | bytes 5308424 | tf_op jit(solution)/shard_map/ppermute | solution.py:902
  201.7 42.6 %collective-permute-start.29 = (bf16[4,1,144,1536]{3,2,1,0:T(8,128)(2,1)}, bf16[4,1,144,1536]{3,2,1,0:T(8,128)(2,1)}, u32[]{:S(2)}, u32[]{:S(2)}) collective-permute-start(bf16[4,1,144,1536]{3,2,1,0:T(8,128)(2,1)} %collective-permute-done.23.refs_2_), channel_id=1, source_target_pairs={{0,2},{2,3},{3,1},{1,0},{4,6},{6,7},{7,5},{5,4},{8,10},{10,11},{11... | collective-permute-start | bytes 5308424 | tf_op jit(solution)/shard_map/ppermute | solution.py:902
  202.0 22.1 %collective-permute-start.25 = (bf16[384,1152]{1,0:T(8,128)(2,1)}, bf16[384,1152]{1,0:T(8,128)(2,1)}, u32[]{:S(2)}, u32[]{:S(2)}) collective-permute-start(bf16[384,1152]{1,0:T(8,128)(2,1)} %get-tuple-element.470.refs_0_), channel_id=1, source_target_pairs={{0,4},{4,0},{8,12},{12,8},{1,5},{5,1},{9,13},{13,9},{2,6},{6,2},{1... | collective-permute-start | bytes 2654216 | tf_op jit(solution)/shard_map/ppermute | solution.py:27
  203.2 21.8 %collective-permute-start.26 = (bf16[384,1152]{1,0:T(8,128)(2,1)}, bf16[384,1152]{1,0:T(8,128)(2,1)}, u32[]{:S(2)}, u32[]{:S(2)}) collective-permute-start(bf16[384,1152]{1,0:T(8,128)(2,1)} %get-tuple-element.470.refs_0_), channel_id=1, source_target_pairs={{0,8},{4,12},{8,0},{12,4},{1,9},{5,13},{9,1},{13,5},{2,10},{6,14},... | collective-permute-start | bytes 2654216 | tf_op jit(solution)/shard_map/ppermute | solution.py:27
  252.4 26.2 %collective-permute-start.30 = (bf16[16,144,1536]{2,1,0:T(8,128)(2,1)}, bf16[16,144,1536]{2,1,0:T(8,128)(2,1)}, u32[]{:S(2)}, u32[]{:S(2)}) collective-permute-start(bf16[16,144,1536]{2,1,0:T(8,128)(2,1)} %bitcast.286), channel_id=1, source_target_pairs={{0,16},{16,0},{1,17},{17,1},{2,18},{18,2},{3,19},{19,3},{4,20},{20... | collective-permute-start | bytes 21233672 | tf_op jit(solution)/shard_map/ppermute | solution.py:27
  254.2 37.2 %collective-permute-start.31 = (bf16[256,1536]{1,0:T(8,128)(2,1)S(1)}, bf16[256,1536]{1,0:T(8,128)(2,1)S(1)}, u32[]{:S(2)}, u32[]{:S(2)}) collective-permute-start(bf16[256,1536]{1,0:T(8,128)(2,1)S(1)} %copy-done.9), channel_id=1, source_target_pairs={{0,12},{4,8},{8,4},{12,0},{1,13},{5,9},{9,5},{13,1},{2,14},{6,10},... | collective-permute-start | bytes 2359304 | tf_op jit(solution)/shard_map/ppermute | solution.py:27
  273.3 37.2 %collective-permute-start.37 = (bf16[384,1152]{1,0:T(8,128)(2,1)}, bf16[384,1152]{1,0:T(8,128)(2,1)}, u32[]{:S(2)}, u32[]{:S(2)}) collective-permute-start(bf16[384,1152]{1,0:T(8,128)(2,1)} %get-tuple-element.470.refs_0_), channel_id=1, source_target_pairs={{0,12},{4,8},{8,4},{12,0},{1,13},{5,9},{9,5},{13,1},{2,14},{6,10},... | collective-permute-start | bytes 2654216 | tf_op jit(solution)/shard_map/ppermute | solution.py:27
  316.8 22.9 %collective-permute-start.38 = (bf16[1536,1152]{1,0:T(8,128)(2,1)}, bf16[1536,1152]{1,0:T(8,128)(2,1)S(1)}, u32[]{:S(2)}, u32[]{:S(2)}) collective-permute-start(bf16[1536,1152]{1,0:T(8,128)(2,1)} %place.10.refs_5_.refs_4_), channel_id=1, source_target_pairs={{0,16},{16,0},{1,17},{17,1},{2,18},{18,2},{3,19},{19,3},{4,20},{20... | collective-permute-start | bytes 10616840 | tf_op jit(solution)/shard_map/ppermute | solution.py:27
  316.8 20.9 %collective-permute-start.39 = (bf16[256,1536]{1,0:T(8,128)(2,1)S(1)}, bf16[256,1536]{1,0:T(8,128)(2,1)S(1)}, u32[]{:S(2)}, u32[]{:S(2)}) collective-permute-start(bf16[256,1536]{1,0:T(8,128)(2,1)S(1)} %copy-done.57), channel_id=1, source_target_pairs={{0,12},{4,8},{8,4},{12,0},{1,13},{5,9},{9,5},{13,1},{2,14},{6,10},... | collective-permute-start | bytes 2359304 | tf_op jit(solution)/shard_map/ppermute | solution.py:27
  318.3 41.0 %collective-permute-start.42 = (bf16[4,1,144,1536]{3,2,1,0:T(8,128)(2,1)}, bf16[4,1,144,1536]{3,2,1,0:T(8,128)(2,1)}, u32[]{:S(2)}, u32[]{:S(2)}) collective-permute-start(bf16[4,1,144,1536]{3,2,1,0:T(8,128)(2,1)} %get-tuple-element.510.refs_0_), channel_id=1, source_target_pairs={{0,2},{2,3},{3,1},{1,0},{4,6},{6,7},{7,5},{5,4},{8,10},{10,11},{11... | collective-permute-start | bytes 5308424 | tf_op jit(solution)/shard_map/ppermute | solution.py:902
  359.3 40.2 %collective-permute-start.47 = (bf16[4,1,144,1536]{3,2,1,0:T(8,128)(2,1)}, bf16[4,1,144,1536]{3,2,1,0:T(8,128)(2,1)}, u32[]{:S(2)}, u32[]{:S(2)}) collective-permute-start(bf16[4,1,144,1536]{3,2,1,0:T(8,128)(2,1)} %collective-permute-done.42.refs_1_), channel_id=1, source_target_pairs={{0,2},{2,3},{3,1},{1,0},{4,6},{6,7},{7,5},{5,4},{8,10},{10,11},{11... | collective-permute-start | bytes 5308424 | tf_op jit(solution)/shard_map/ppermute | solution.py:902
  403.0 42.2 %collective-permute-start.51 = (bf16[4,1,144,1536]{3,2,1,0:T(8,128)(2,1)}, bf16[4,1,144,1536]{3,2,1,0:T(8,128)(2,1)}, u32[]{:S(2)}, u32[]{:S(2)}) collective-permute-start(bf16[4,1,144,1536]{3,2,1,0:T(8,128)(2,1)} %collective-permute-done.47.refs_2_), channel_id=1, source_target_pairs={{0,2},{2,3},{3,1},{1,0},{4,6},{6,7},{7,5},{5,4},{8,10},{10,11},{11... | collective-permute-start | bytes 5308424 | tf_op jit(solution)/shard_map/ppermute | solution.py:902
  452.3 28.2 %collective-permute-start.53 = (bf16[256,1536]{1,0:T(8,128)(2,1)S(1)}, bf16[256,1536]{1,0:T(8,128)(2,1)S(1)}, u32[]{:S(2)}, u32[]{:S(2)}) collective-permute-start(bf16[256,1536]{1,0:T(8,128)(2,1)S(1)} %copy-done.15), channel_id=1, source_target_pairs={{0,12},{4,8},{8,4},{12,0},{1,13},{5,9},{9,5},{13,1},{2,14},{6,10},... | collective-permute-start | bytes 2359304 | tf_op jit(solution)/shard_map/ppermute | solution.py:27
  501.1 36.2 %collective-permute-start.56 = (bf16[256,1536]{1,0:T(8,128)(2,1)S(1)}, bf16[256,1536]{1,0:T(8,128)(2,1)S(1)}, u32[]{:S(2)}, u32[]{:S(2)}) collective-permute-start(bf16[256,1536]{1,0:T(8,128)(2,1)S(1)} %get-tuple-element.535.refs_0_.cot_ref), channel_id=1, source_target_pairs={{0,12},{4,8},{8,4},{12,0},{1,13},{5,9},{9,5},{13,1},{2,14},{6,10},... | collective-permute-start | bytes 2359304 | tf_op jit(solution)/shard_map/ppermute | solution.py:27
  556.3 31.0 %collective-permute-start.59 = (bf16[256,1536]{1,0:T(8,128)(2,1)}, bf16[256,1536]{1,0:T(8,128)(2,1)}, u32[]{:S(2)}, u32[]{:S(2)}) collective-permute-start(bf16[256,1536]{1,0:T(8,128)(2,1)} %get-tuple-element.579), channel_id=1, source_target_pairs={{0,12},{4,8},{8,4},{12,0},{1,13},{5,9},{9,5},{13,1},{2,14},{6,10},... | collective-permute-start | bytes 2359304 | tf_op jit(solution)/shard_map/ppermute | solution.py:27
  557.8 33.4 %collective-permute-start.60 = (bf16[256,1536]{1,0:T(8,128)(2,1)S(1)}, bf16[256,1536]{1,0:T(8,128)(2,1)}, u32[]{:S(2)}, u32[]{:S(2)}) collective-permute-start(bf16[256,1536]{1,0:T(8,128)(2,1)S(1)} %copy-done.53), channel_id=1, source_target_pairs={{0,4},{4,0},{8,12},{12,8},{1,5},{5,1},{9,13},{13,9},{2,6},{6,2},{1... | collective-permute-start | bytes 2359304 | tf_op jit(solution)/shard_map/ppermute | solution.py:27
  559.0 32.4 %collective-permute-start.61 = (bf16[256,1536]{1,0:T(8,128)(2,1)S(1)}, bf16[256,1536]{1,0:T(8,128)(2,1)}, u32[]{:S(2)}, u32[]{:S(2)}) collective-permute-start(bf16[256,1536]{1,0:T(8,128)(2,1)S(1)} %copy-done.52), channel_id=1, source_target_pairs={{0,8},{4,12},{8,0},{12,4},{1,9},{5,13},{9,1},{13,5},{2,10},{6,14},... | collective-permute-start | bytes 2359304 | tf_op jit(solution)/shard_map/ppermute | solution.py:27
  602.7 27.6 %collective-permute-start.62 = (bf16[1536,768]{1,0:T(8,128)(2,1)}, bf16[1536,768]{1,0:T(8,128)(2,1)}, u32[]{:S(2)}, u32[]{:S(2)}) collective-permute-start(bf16[1536,768]{1,0:T(8,128)(2,1)} %get-tuple-element.616), channel_id=1, source_target_pairs={{0,16},{16,0},{1,17},{17,1},{2,18},{18,2},{3,19},{19,3},{4,20},{20... | collective-permute-start | bytes 7077896 | tf_op jit(solution)/shard_map/ppermute | solution.py:27
  607.5 41.7 %collective-permute-start.68 = (bf16[4,144,1536]{2,1,0:T(8,128)(2,1)}, bf16[4,144,1536]{2,1,0:T(8,128)(2,1)}, u32[]{:S(2)}, u32[]{:S(2)}) collective-permute-start(bf16[4,144,1536]{2,1,0:T(8,128)(2,1)} %fusion.9), channel_id=1, source_target_pairs={{0,2},{2,3},{3,1},{1,0},{4,6},{6,7},{7,5},{5,4},{8,10},{10,11},{11... | collective-permute-start | bytes 5308424 | tf_op jit(solution)/shard_map/ppermute | solution.py:943
  610.0 20.3 %collective-permute-start.63 = (bf16[256,1536]{1,0:T(8,128)(2,1)}, bf16[256,1536]{1,0:T(8,128)(2,1)S(1)}, u32[]{:S(2)}, u32[]{:S(2)}) collective-permute-start(bf16[256,1536]{1,0:T(8,128)(2,1)} %get-tuple-element.617), channel_id=1, source_target_pairs={{0,12},{4,8},{8,4},{12,0},{1,13},{5,9},{9,5},{13,1},{2,14},{6,10},... | collective-permute-start | bytes 2359304 | tf_op jit(solution)/shard_map/ppermute | solution.py:27
  638.2 24.6 %collective-permute-start.69 = (bf16[384,768]{1,0:T(8,128)(2,1)}, bf16[384,768]{1,0:T(8,128)(2,1)}, u32[]{:S(2)}, u32[]{:S(2)}) collective-permute-start(bf16[384,768]{1,0:T(8,128)(2,1)} %get-tuple-element.888), channel_id=1, source_target_pairs={{0,4},{4,0},{8,12},{12,8},{1,5},{5,1},{9,13},{13,9},{2,6},{6,2},{1... | collective-permute-start | bytes 1769480 | tf_op jit(solution)/shard_map/ppermute | solution.py:27
  641.5 27.9 %collective-permute-start.70 = (bf16[384,768]{1,0:T(8,128)(2,1)}, bf16[384,768]{1,0:T(8,128)(2,1)}, u32[]{:S(2)}, u32[]{:S(2)}) collective-permute-start(bf16[384,768]{1,0:T(8,128)(2,1)} %get-tuple-element.887), channel_id=1, source_target_pairs={{0,8},{4,12},{8,0},{12,4},{1,9},{5,13},{9,1},{13,5},{2,10},{6,14},... | collective-permute-start | bytes 1769480 | tf_op jit(solution)/shard_map/ppermute | solution.py:27
  642.4 27.0 %collective-permute-start.71 = (bf16[384,768]{1,0:T(8,128)(2,1)}, bf16[384,768]{1,0:T(8,128)(2,1)}, u32[]{:S(2)}, u32[]{:S(2)}) collective-permute-start(bf16[384,768]{1,0:T(8,128)(2,1)} %get-tuple-element.886), channel_id=1, source_target_pairs={{0,12},{4,8},{8,4},{12,0},{1,13},{5,9},{9,5},{13,1},{2,14},{6,10},... | collective-permute-start | bytes 1769480 | tf_op jit(solution)/shard_map/ppermute | solution.py:27
  669.5 20.7 %collective-permute-start.74 = (bf16[1536,1152]{1,0:T(8,128)(2,1)}, bf16[1536,1152]{1,0:T(8,128)(2,1)S(1)}, u32[]{:S(2)}, u32[]{:S(2)}) collective-permute-start(bf16[1536,1152]{1,0:T(8,128)(2,1)} %get-tuple-element.643), channel_id=1, source_target_pairs={{0,16},{16,0},{1,17},{17,1},{2,18},{18,2},{3,19},{19,3},{4,20},{20... | collective-permute-start | bytes 10616840 | tf_op jit(solution)/shard_map/ppermute | solution.py:27
  669.5 20.2 %collective-permute-start.72 = (bf16[256,1536]{1,0:T(8,128)(2,1)}, bf16[256,1536]{1,0:T(8,128)(2,1)S(1)}, u32[]{:S(2)}, u32[]{:S(2)}) collective-permute-start(bf16[256,1536]{1,0:T(8,128)(2,1)} %get-tuple-element.646.refs_0_.cot_ref), channel_id=1, source_target_pairs={{0,4},{4,0},{8,12},{12,8},{1,5},{5,1},{9,13},{13,9},{2,6},{6,2},{1... | collective-permute-start | bytes 2359304 | tf_op jit(solution)/shard_map/ppermute | solution.py:27
  670.3 19.9 %collective-permute-start.73 = (bf16[256,1536]{1,0:T(8,128)(2,1)}, bf16[256,1536]{1,0:T(8,128)(2,1)S(1)}, u32[]{:S(2)}, u32[]{:S(2)}) collective-permute-start(bf16[256,1536]{1,0:T(8,128)(2,1)} %get-tuple-element.646.refs_0_.cot_ref), channel_id=1, source_target_pairs={{0,8},{4,12},{8,0},{12,4},{1,9},{5,13},{9,1},{13,5},{2,10},{6,14},... | collective-permute-start | bytes 2359304 | tf_op jit(solution)/shard_map/ppermute | solution.py:27
  676.2 56.0 %collective-permute-start.76 = (bf16[4,144,1536]{2,1,0:T(8,128)(2,1)}, bf16[4,144,1536]{2,1,0:T(8,128)(2,1)}, u32[]{:S(2)}, u32[]{:S(2)}) collective-permute-start(bf16[4,144,1536]{2,1,0:T(8,128)(2,1)} %fusion.5), channel_id=1, source_target_pairs={{0,2},{2,3},{3,1},{1,0},{4,6},{6,7},{7,5},{5,4},{8,10},{10,11},{11... | collective-permute-start | bytes 5308424 | tf_op jit(solution)/shard_map/ppermute | solution.py:943
  693.3 39.0 %collective-permute-start.77 = (bf16[384,1152]{1,0:T(8,128)(2,1)}, bf16[384,1152]{1,0:T(8,128)(2,1)}, u32[]{:S(2)}, u32[]{:S(2)}) collective-permute-start(bf16[384,1152]{1,0:T(8,128)(2,1)} %get-tuple-element.879), channel_id=1, source_target_pairs={{0,4},{4,0},{8,12},{12,8},{1,5},{5,1},{9,13},{13,9},{2,6},{6,2},{1... | collective-permute-start | bytes 2654216 | tf_op jit(solution)/shard_map/ppermute | solution.py:27
  694.5 38.0 %collective-permute-start.78 = (bf16[384,1152]{1,0:T(8,128)(2,1)}, bf16[384,1152]{1,0:T(8,128)(2,1)}, u32[]{:S(2)}, u32[]{:S(2)}) collective-permute-start(bf16[384,1152]{1,0:T(8,128)(2,1)} %get-tuple-element.878), channel_id=1, source_target_pairs={{0,8},{4,12},{8,0},{12,4},{1,9},{5,13},{9,1},{13,5},{2,10},{6,14},... | collective-permute-start | bytes 2654216 | tf_op jit(solution)/shard_map/ppermute | solution.py:27
  695.3 36.9 %collective-permute-start.75 = (bf16[256,1536]{1,0:T(8,128)(2,1)}, bf16[256,1536]{1,0:T(8,128)(2,1)}, u32[]{:S(2)}, u32[]{:S(2)}) collective-permute-start(bf16[256,1536]{1,0:T(8,128)(2,1)} %get-tuple-element.646.refs_0_.cot_ref), channel_id=1, source_target_pairs={{0,12},{4,8},{8,4},{12,0},{1,13},{5,9},{9,5},{13,1},{2,14},{6,10},... | collective-permute-start | bytes 2359304 | tf_op jit(solution)/shard_map/ppermute | solution.py:27
  737.1 41.5 %collective-permute-start.81 = (bf16[4,144,1536]{2,1,0:T(8,128)(2,1)}, bf16[4,144,1536]{2,1,0:T(8,128)(2,1)}, u32[]{:S(2)}, u32[]{:S(2)}) collective-permute-start(bf16[4,144,1536]{2,1,0:T(8,128)(2,1)} %fusion.4), channel_id=1, source_target_pairs={{0,2},{2,3},{3,1},{1,0},{4,6},{6,7},{7,5},{5,4},{8,10},{10,11},{11... | collective-permute-start | bytes 5308424 | tf_op jit(solution)/shard_map/ppermute | solution.py:943
  738.8 24.8 %collective-permute-start.79 = (bf16[256,1536]{1,0:T(8,128)(2,1)}, bf16[256,1536]{1,0:T(8,128)(2,1)}, u32[]{:S(2)}, u32[]{:S(2)}) collective-permute-start(bf16[256,1536]{1,0:T(8,128)(2,1)} %get-tuple-element.667), channel_id=1, source_target_pairs={{0,4},{4,0},{8,12},{12,8},{1,5},{5,1},{9,13},{13,9},{2,6},{6,2},{1... | collective-permute-start | bytes 2359304 | tf_op jit(solution)/shard_map/ppermute | solution.py:27
  739.6 38.9 %collective-permute-start.80 = (bf16[256,1536]{1,0:T(8,128)(2,1)}, bf16[256,1536]{1,0:T(8,128)(2,1)}, u32[]{:S(2)}, u32[]{:S(2)}) collective-permute-start(bf16[256,1536]{1,0:T(8,128)(2,1)} %get-tuple-element.668), channel_id=1, source_target_pairs={{0,8},{4,12},{8,0},{12,4},{1,9},{5,13},{9,1},{13,5},{2,10},{6,14},... | collective-permute-start | bytes 2359304 | tf_op jit(solution)/shard_map/ppermute | solution.py:27
  742.4 36.1 %collective-permute-start.83 = (bf16[384,1152]{1,0:T(8,128)(2,1)S(1)}, bf16[384,1152]{1,0:T(8,128)(2,1)S(1)}, u32[]{:S(2)}, u32[]{:S(2)}) collective-permute-start(bf16[384,1152]{1,0:T(8,128)(2,1)S(1)} %fusion.16), channel_id=1, source_target_pairs={{0,12},{4,8},{8,4},{12,0},{1,13},{5,9},{9,5},{13,1},{2,14},{6,10},... | collective-permute-start | bytes 2654216 | tf_op jit(solution)/shard_map/ppermute | solution.py:27
  780.6 33.3 %collective-permute-start.87 = (bf16[96,1920]{1,0:T(8,128)(2,1)S(1)}, bf16[96,1920]{1,0:T(8,128)(2,1)S(1)}, u32[]{:S(2)}, u32[]{:S(2)}) collective-permute-start(bf16[96,1920]{1,0:T(8,128)(2,1)S(1)} %get-tuple-element.910), channel_id=1, source_target_pairs={{0,3},{1,2},{2,1},{3,0},{4,7},{5,6},{6,5},{7,4},{8,11},{9,10},{10,... | collective-permute-start | bytes 1105928 | tf_op jit(solution)/shard_map/ppermute | solution.py:27
  783.2 31.8 %collective-permute-start.86 = (bf16[96,1920]{1,0:T(8,128)(2,1)S(1)}, bf16[96,1920]{1,0:T(8,128)(2,1)S(1)}, u32[]{:S(2)}, u32[]{:S(2)}) collective-permute-start(bf16[96,1920]{1,0:T(8,128)(2,1)S(1)} %get-tuple-element.911), channel_id=1, source_target_pairs={{0,2},{1,3},{2,0},{3,1},{4,6},{5,7},{6,4},{7,5},{8,10},{9,11},{10,... | collective-permute-start | bytes 1105928 | tf_op jit(solution)/shard_map/ppermute | solution.py:27
  783.5 31.5 %collective-permute-start.85 = (bf16[96,1920]{1,0:T(8,128)(2,1)S(1)}, bf16[96,1920]{1,0:T(8,128)(2,1)S(1)}, u32[]{:S(2)}, u32[]{:S(2)}) collective-permute-start(bf16[96,1920]{1,0:T(8,128)(2,1)S(1)} %get-tuple-element.909), channel_id=1, source_target_pairs={{0,1},{1,0},{2,3},{3,2},{4,5},{5,4},{6,7},{7,6},{8,9},{9,8},{10,11... | collective-permute-start | bytes 1105928 | tf_op jit(solution)/shard_map/ppermute | solution.py:27
  785.0 30.1 %collective-permute-start.84 = (bf16[256,1536]{1,0:T(8,128)(2,1)}, bf16[256,1536]{1,0:T(8,128)(2,1)}, u32[]{:S(2)}, u32[]{:S(2)}) collective-permute-start(bf16[256,1536]{1,0:T(8,128)(2,1)} %get-tuple-element.697), channel_id=1, source_target_pairs={{0,12},{4,8},{8,4},{12,0},{1,13},{5,9},{9,5},{13,1},{2,14},{6,10},... | collective-permute-start | bytes 2359304 | tf_op jit(solution)/shard_map/ppermute | solution.py:27
  826.6 21.2 %collective-permute-start.88 = (bf16[1536,768]{1,0:T(8,128)(2,1)}, bf16[1536,768]{1,0:T(8,128)(2,1)}, u32[]{:S(2)}, u32[]{:S(2)}) collective-permute-start(bf16[1536,768]{1,0:T(8,128)(2,1)} %get-tuple-element.747), channel_id=1, source_target_pairs={{0,16},{16,0},{1,17},{17,1},{2,18},{18,2},{3,19},{19,3},{4,20},{20... | collective-permute-start | bytes 7077896 | tf_op jit(solution)/shard_map/ppermute | solution.py:27
  830.9 40.9 %collective-permute-start.93 = (bf16[4,144,1536]{2,1,0:T(8,128)(2,1)}, bf16[4,144,1536]{2,1,0:T(8,128)(2,1)}, u32[]{:S(2)}, u32[]{:S(2)}) collective-permute-start(bf16[4,144,1536]{2,1,0:T(8,128)(2,1)} %fusion.10), channel_id=1, source_target_pairs={{0,2},{2,3},{3,1},{1,0},{4,6},{6,7},{7,5},{5,4},{8,10},{10,11},{11... | collective-permute-start | bytes 5308424 | tf_op jit(solution)/shard_map/ppermute | solution.py:943
  875.3 21.5 %collective-permute-start.94 = (bf16[384,768]{1,0:T(8,128)(2,1)}, bf16[384,768]{1,0:T(8,128)(2,1)}, u32[]{:S(2)}, u32[]{:S(2)}) collective-permute-start(bf16[384,768]{1,0:T(8,128)(2,1)} %get-tuple-element.884), channel_id=1, source_target_pairs={{0,4},{4,0},{8,12},{12,8},{1,5},{5,1},{9,13},{13,9},{2,6},{6,2},{1... | collective-permute-start | bytes 1769480 | tf_op jit(solution)/shard_map/ppermute | solution.py:27
  876.5 20.3 %collective-permute-start.95 = (bf16[384,768]{1,0:T(8,128)(2,1)}, bf16[384,768]{1,0:T(8,128)(2,1)}, u32[]{:S(2)}, u32[]{:S(2)}) collective-permute-start(bf16[384,768]{1,0:T(8,128)(2,1)} %get-tuple-element.883), channel_id=1, source_target_pairs={{0,8},{4,12},{8,0},{12,4},{1,9},{5,13},{9,1},{13,5},{2,10},{6,14},... | collective-permute-start | bytes 1769480 | tf_op jit(solution)/shard_map/ppermute | solution.py:27
  881.8 39.5 %collective-permute-start.106 = (bf16[4,144,1536]{2,1,0:T(8,128)(2,1)}, bf16[4,144,1536]{2,1,0:T(8,128)(2,1)}, u32[]{:S(2)}, u32[]{:S(2)}) collective-permute-start(bf16[4,144,1536]{2,1,0:T(8,128)(2,1)} %fusion.3), channel_id=1, source_target_pairs={{0,2},{2,3},{3,1},{1,0},{4,6},{6,7},{7,5},{5,4},{8,10},{10,11},{11... | collective-permute-start | bytes 5308424 | tf_op jit(solution)/shard_map/ppermute | solution.py:943
  896.8 39.5 %collective-permute-start.96 = (bf16[1536,1152]{1,0:T(8,128)(2,1)}, bf16[1536,1152]{1,0:T(8,128)(2,1)S(1)}, u32[]{:S(2)}, u32[]{:S(2)}) collective-permute-start(bf16[1536,1152]{1,0:T(8,128)(2,1)} %get-tuple-element.766), channel_id=1, source_target_pairs={{0,16},{16,0},{1,17},{17,1},{2,18},{18,2},{3,19},{19,3},{4,20},{20... | collective-permute-start | bytes 10616840 | tf_op jit(solution)/shard_map/ppermute | solution.py:27
  924.6 39.8 %collective-permute-start.107 = (bf16[4,144,1536]{2,1,0:T(8,128)(2,1)S(1)}, bf16[4,144,1536]{2,1,0:T(8,128)(2,1)S(1)}, u32[]{:S(2)}, u32[]{:S(2)}) collective-permute-start(bf16[4,144,1536]{2,1,0:T(8,128)(2,1)S(1)} %fusion.2), channel_id=1, source_target_pairs={{0,2},{2,3},{3,1},{1,0},{4,6},{6,7},{7,5},{5,4},{8,10},{10,11},{11... | collective-permute-start | bytes 5308424 | tf_op jit(solution)/shard_map/ppermute | solution.py:943
  934.8 34.2 %collective-permute-start.100 = (bf16[384,768]{1,0:T(8,128)(2,1)S(1)}, bf16[384,768]{1,0:T(8,128)(2,1)S(1)}, u32[]{:S(2)}, u32[]{:S(2)}) collective-permute-start(bf16[384,768]{1,0:T(8,128)(2,1)S(1)} %fusion.44), channel_id=1, source_target_pairs={{0,12},{4,8},{8,4},{12,0},{1,13},{5,9},{9,5},{13,1},{2,14},{6,10},... | collective-permute-start | bytes 1769480 | tf_op jit(solution)/shard_map/ppermute | solution.py:27
  937.2 33.5 %collective-permute-start.97 = (bf16[384,1152]{1,0:T(8,128)(2,1)S(1)}, bf16[384,1152]{1,0:T(8,128)(2,1)S(1)}, u32[]{:S(2)}, u32[]{:S(2)}) collective-permute-start(bf16[384,1152]{1,0:T(8,128)(2,1)S(1)} %get-tuple-element.876), channel_id=1, source_target_pairs={{0,4},{4,0},{8,12},{12,8},{1,5},{5,1},{9,13},{13,9},{2,6},{6,2},{1... | collective-permute-start | bytes 2654216 | tf_op jit(solution)/shard_map/ppermute | solution.py:27
  938.4 33.1 %collective-permute-start.98 = (bf16[384,1152]{1,0:T(8,128)(2,1)S(1)}, bf16[384,1152]{1,0:T(8,128)(2,1)S(1)}, u32[]{:S(2)}, u32[]{:S(2)}) collective-permute-start(bf16[384,1152]{1,0:T(8,128)(2,1)S(1)} %get-tuple-element.875), channel_id=1, source_target_pairs={{0,8},{4,12},{8,0},{12,4},{1,9},{5,13},{9,1},{13,5},{2,10},{6,14},... | collective-permute-start | bytes 2654216 | tf_op jit(solution)/shard_map/ppermute | solution.py:27
  939.3 50.8 %collective-permute-start.99 = (bf16[384,1152]{1,0:T(8,128)(2,1)S(1)}, bf16[384,1152]{1,0:T(8,128)(2,1)S(1)}, u32[]{:S(2)}, u32[]{:S(2)}) collective-permute-start(bf16[384,1152]{1,0:T(8,128)(2,1)S(1)} %get-tuple-element.874), channel_id=1, source_target_pairs={{0,12},{4,8},{8,4},{12,0},{1,13},{5,9},{9,5},{13,1},{2,14},{6,10},... | collective-permute-start | bytes 2654216 | tf_op jit(solution)/shard_map/ppermute | solution.py:27
  967.5 41.5 %collective-permute-start.110 = (bf16[2,144,1536]{2,1,0:T(8,128)(2,1)S(1)}, bf16[2,144,1536]{2,1,0:T(8,128)(2,1)S(1)}, u32[]{:S(2)}, u32[]{:S(2)}) collective-permute-start(bf16[2,144,1536]{2,1,0:T(8,128)(2,1)S(1)} %get-tuple-element.895), channel_id=1, source_target_pairs={{0,12},{4,8},{8,4},{12,0},{1,13},{5,9},{9,5},{13,1},{2,14},{6,10},... | collective-permute-start | bytes 2654216 | tf_op jit(solution)/shard_map/ppermute | solution.py:27
  969.0 55.4 %collective-permute-start.109 = (bf16[2,144,1536]{2,1,0:T(8,128)(2,1)S(1)}, bf16[2,144,1536]{2,1,0:T(8,128)(2,1)S(1)}, u32[]{:S(2)}, u32[]{:S(2)}) collective-permute-start(bf16[2,144,1536]{2,1,0:T(8,128)(2,1)S(1)} %get-tuple-element.894), channel_id=1, source_target_pairs={{0,8},{4,12},{8,0},{12,4},{1,9},{5,13},{9,1},{13,5},{2,10},{6,14},... | collective-permute-start | bytes 2654216 | tf_op jit(solution)/shard_map/ppermute | solution.py:27
  970.7 53.7 %collective-permute-start.108 = (bf16[2,144,1536]{2,1,0:T(8,128)(2,1)S(1)}, bf16[2,144,1536]{2,1,0:T(8,128)(2,1)S(1)}, u32[]{:S(2)}, u32[]{:S(2)}) collective-permute-start(bf16[2,144,1536]{2,1,0:T(8,128)(2,1)S(1)} %get-tuple-element.893), channel_id=1, source_target_pairs={{0,4},{4,0},{8,12},{12,8},{1,5},{5,1},{9,13},{13,9},{2,6},{6,2},{1... | collective-permute-start | bytes 2654216 | tf_op jit(solution)/shard_map/ppermute | solution.py:27
  993.1 31.8 %collective-permute-start.104 = (bf16[96,1920]{1,0:T(8,128)(2,1)S(1)}, bf16[96,1920]{1,0:T(8,128)(2,1)S(1)}, u32[]{:S(2)}, u32[]{:S(2)}) collective-permute-start(bf16[96,1920]{1,0:T(8,128)(2,1)S(1)} %get-tuple-element.907), channel_id=1, source_target_pairs={{0,3},{1,2},{2,1},{3,0},{4,7},{5,6},{6,5},{7,4},{8,11},{9,10},{10,... | collective-permute-start | bytes 1105928 | tf_op jit(solution)/shard_map/ppermute | solution.py:27
  995.7 29.2 %collective-permute-start.103 = (bf16[96,1920]{1,0:T(8,128)(2,1)S(1)}, bf16[96,1920]{1,0:T(8,128)(2,1)S(1)}, u32[]{:S(2)}, u32[]{:S(2)}) collective-permute-start(bf16[96,1920]{1,0:T(8,128)(2,1)S(1)} %get-tuple-element.908), channel_id=1, source_target_pairs={{0,2},{1,3},{2,0},{3,1},{4,6},{5,7},{6,4},{7,5},{8,10},{9,11},{10,... | collective-permute-start | bytes 1105928 | tf_op jit(solution)/shard_map/ppermute | solution.py:27
  (121 other events, 1744.1 us)
where the time goes:
time: 1050 us; the launch traced here: 1040 us
  Pallas kernels  402 us (38%)
  waiting for transfers between devices  382 us (36%)
  starting transfers between devices  127 us (12%)
  other arithmetic  87.9 us (8%)
  local copies, waits for them, and re-layouts  42.2 us (4%)
    ppermute x100, waiting for transfers between devices, swap(): lax.ppermute(value, axis, [(source, source ^ bit) for source in range(cou...  300 us
    ppermute x100, starting transfers between devices, swap(): lax.ppermute(value, axis, [(source, source ^ bit) for source in range(cou...  103 us
    pallas_call x8, Pallas kernels, expert_back_call(): pl.pallas_call(functools.partial(expert_back_kernel, blocks, 1 if before...  86.3 us
    pallas_call x8, Pallas kernels, expert_call(): pl.pallas_call(functools.partial(expert_kernel, blocks, 1 if before else...  77.5 us
    pallas_call x8, Pallas kernels, dense_call(): pl.pallas_call(kernel, grid_spec=pltpu.PrefetchScalarGridSpec(num_scalar_...  76.9 us
    ppermute x6, waiting for transfers between devices, ring_move(): lax.ppermute(moving, 'fsdp', ring_steps)  60 us
    pallas_call x4, Pallas kernels, expert_grads_call(): pl.pallas_call(functools.partial(expert_grads_kernel, len(picked), deep),...  54.8 us
    pallas_call x2, Pallas kernels, attend_back_call(): pl.pallas_call(attend_back_kernel, grid_spec=pltpu.PrefetchScalarGridSpec...  33.3 us
  transfers between devices with their start and end apart: 112, of which 59 were waited for; matrix products, arithmetic and copies ran while one was open for 10% of the time, Pallas kernels for 35%

commit v1 on v0

--- a/solution.py
+++ b/solution.py
@@ -1016,7 +1016,7 @@
     near = 1 + len(early)
     parts = (slice(0, near), slice(near, n_ctx))
 
-    def experts(layer, blocks, weights, answer, beside_near=tuple, beside_far=lambda found: ()):
+    def experts(layer, blocks, weights, answer, beside_near=tuple, beside_far=None):
         kept, arrived = ({}, [])
         back = {}
         for index, part in enumerate(parts):
@@ -1039,9 +1039,9 @@
                 )
         if not answer:
             return (back[0] + back[1], kept)
-        back[1], arrived, found = tie(back[1], arrived, beside_far(found))
+        back[1], arrived, far = tie(back[1], arrived, beside_far(found))
         arrived += [swap(block, "ctx", bit) for bit, block in zip(late, back[1])]
-        return (back[0][:1] + arrived, kept, found)
+        return (back[0][:1] + arrived, kept, found, far)
 
     def experts_back(layer, blocks, weights, kept, delay, beside_near, beside_far, beside_end):
         back, saved = ({}, {})
@@ -1128,24 +1128,23 @@
     leave_own = join_square(leave_blocks)
     leave_first = (leave_own, swap(leave_own, "section", 1))
     first_mid, ffn_normed = leave_call(core, first_in, first_attended, first_gains[1], leave_first)
-    ffn_normed, enter_blocks = tie(ffn_normed, enter_blocks)
     blocks = spread_rows(ffn_normed)
-    blocks[:near], moved, dealt_second, enter_shard, leave_shard = tie(
-        blocks[:near], moved, dealt_second, enter_shard, dense_second[:, enter_cut:]
+    blocks[:near], moved, dealt_second, enter_shard, leave_shard, enter_blocks = tie(
+        blocks[:near], moved, dealt_second, enter_shard, dense_second[:, enter_cut:], enter_blocks
     )
     first_weights = pair_units(own_units(moved[0]))
-    returned, first_kept, (moved, leave_shard, enter_blocks) = experts(
+    returned, first_kept, leave_shard, (enter_blocks, dealt_second) = experts(
         0,
         blocks,
         first_weights,
         True,
         lambda: gather_deep(leave_shard),
-        lambda found: (dealt_second, found, enter_blocks + send(enter_shard, late)),
-    )
-    moved = ring_send([[moved]])
+        lambda found: (enter_blocks + send(enter_shard, late), dealt_second),
+    )
+    moved = ring_send([[dealt_second]])
+    returned, leave_shard = tie(returned, leave_shard)
     enter_own = join_square(enter_blocks)
     enter_second = (enter_own, swap(enter_own, "section", 1))
-    returned, leave_shard = tie(returned, leave_shard)
     leave_blocks = [leave_shard] + send(leave_shard, early)
 
     second_gains = gains_of(enter_second)
@@ -1259,11 +1258,8 @@
     leave_grads = (grads[0], swap(grads[1], "section", 1))
     d_queries, d_key_value = attend_back_call(block_ids, first_entered, first_kv, d_attended)
     d_queries, d_key_value, leave_grads = tie(d_queries, d_key_value, leave_grads)
-    d_key_value, units_moving, leave_grads = tie(
-        gather_back(d_key_value), ring_move(units_moving), leave_grads
-    )
+    d_key_value, leave_grads = tie(gather_back(d_key_value), leave_grads)
     leave_parts = trade_square(*leave_grads, [0, *early])
-    units_moving = ring_move(ring_add(units_moving, 1))
     first_entry, _, *grads = enter_back_call(
         core,
         d_queries,
@@ -1275,8 +1271,11 @@
         term,
         enter_first,
     )
-    grads, leave_parts, leave_grads = tie(grads, leave_parts, leave_grads)
+    grads, leave_parts, leave_grads, units_moving = tie(
+        grads, leave_parts, leave_grads, ring_move(units_moving)
+    )
     enter_grads = (grads[0], swap(grads[1], "section", 1))
+    units_moving = after(ring_move(ring_add(units_moving, 1)), enter_grads)
     enter_parts, leave_parts, first_entry = tie(
         trade_square(*enter_grads, range(n_ctx)),
         leave_parts + trade_square(*leave_grads, late),

time: 1050 us -> 1080 us (1.029)
  waiting for transfers between devices: 382 us -> 404 us
    ppermute x100, waiting for transfers between devices: 300 us -> 346 us  [swap(): lax.ppermute(value, axis, [(source, source ^ bit) for source in range(cou...]
    ppermute x6, waiting for transfers between devices: 60 us -> 34 us  [ring_move(): lax.ppermute(moving, 'fsdp', ring_steps)]
  transfers between devices with their start and end apart: 112 -> 112, of which waited for: 59 -> 58; matrix products, arithmetic and copies ran while one was open for 10% -> 10% of each run, Pallas kernels for 35% -> 34%
where the time goes in v1:
time: 1080 us; the launch traced here: 1070 us
  waiting for transfers between devices  404 us (37%)
  Pallas kernels  402 us (37%)
  starting transfers between devices  131 us (12%)
  other arithmetic  86.5 us (8%)
  local copies, waits for them, and re-layouts  40.7 us (4%)
    ppermute x100, waiting for transfers between devices, swap(): lax.ppermute(value, axis, [(source, source ^ bit) for source in range(cou...  346 us
    ppermute x100, starting transfers between devices, swap(): lax.ppermute(value, axis, [(source, source ^ bit) for source in range(cou...  105 us
    pallas_call x8, Pallas kernels, expert_back_call(): pl.pallas_call(functools.partial(expert_back_kernel, blocks, 1 if before...  86.3 us
    pallas_call x8, Pallas kernels, expert_call(): pl.pallas_call(functools.partial(expert_kernel, blocks, 1 if before else...  77.4 us
    pallas_call x8, Pallas kernels, dense_call(): pl.pallas_call(kernel, grid_spec=pltpu.PrefetchScalarGridSpec(num_scalar_...  77 us
    pallas_call x4, Pallas kernels, expert_grads_call(): pl.pallas_call(functools.partial(expert_grads_kernel, len(picked), deep),...  54.8 us
    ppermute x6, waiting for transfers between devices, ring_move(): lax.ppermute(moving, 'fsdp', ring_steps)  34 us
    pallas_call x2, Pallas kernels, attend_back_call(): pl.pallas_call(attend_back_kernel, grid_spec=pltpu.PrefetchScalarGridSpec...  33.3 us
  transfers between devices with their start and end apart: 112, of which 58 were waited for; matrix products, arithmetic and copies ran while one was open for 10% of the time, Pallas kernels for 34%

profile of v1, /device:TPU:0, one launch (start us, length us, event | category | flops | bytes accessed | tf_op | source)
XLA Modules:
  0.0 1066.2 jit_solution(16782002127814085103)
XLA Ops:
  39.1 6.9 collective-permute-done.1.refs_1_
  48.8 29.9 %collective-permute-done.2.refs_2_ = bf16[96,3072]{1,0:T(8,128)(2,1)S(1)} collective-permute-done((bf16[96,3072]{1,0:T(8,128)(2,1)S(1)}, bf16[96,3072]{1,0:T(8,128)(2,1)S(1)}, u32[]{:S(2)}, u32[]{:S(2)}) %collective-permute-start.2) | collective-permute-done | bytes 589856 | tf_op jit(solution)/shard_map/ppermute | solution.py:27
  89.8 10.7 collective-permute-start.15
  105.1 19.0 %collective-permute-done.12.refs_1_ = bf16[384,1152]{1,0:T(8,128)(2,1)S(1)} collective-permute-done((bf16[384,1152]{1,0:T(8,128)(2,1)S(1)}, bf16[384,1152]{1,0:T(8,128)(2,1)S(1)}, u32[]{:S(2)}, u32[]{:S(2)}) %collective-permute-start.12) | collective-permute-done | bytes 884768 | tf_op jit(solution)/shard_map/ppermute | solution.py:27
  124.1 15.1 %collective-permute-done.13.refs_2_ = bf16[384,1152]{1,0:T(8,128)(2,1)S(1)} collective-permute-done((bf16[384,1152]{1,0:T(8,128)(2,1)S(1)}, bf16[384,1152]{1,0:T(8,128)(2,1)S(1)}, u32[]{:S(2)}, u32[]{:S(2)}) %collective-permute-start.13) | collective-permute-done | bytes 884768 | tf_op jit(solution)/shard_map/ppermute | solution.py:27
  156.8 6.9 enter.2
  170.1 6.7 collective-permute-done.21
  184.9 12.1 %attend.2.attended_ref = bf16[256,1536]{1,0:T(8,128)(2,1)} custom-call(s32[8]{0:T(128)} %select_n.165.ids_ref, bf16[256,2304]{1,0:T(8,128)(2,1)} %get-tuple-element.415.query_ref, bf16[1024,512]{1,0:T(8,128)(2,1)} %pad_maximum_fusion.4.key_ref.value_ref, bf16[1024,512]{1,0:T(8,128)(2,1)} %pad_maximum_fusion.4.key_ref.value_ref), custom_call_target="tpu_custom_call" | custom-call | flops 1000000000 | bytes 3000000 | tf_op jit(solution)/shard_map/attend/pallas_call | solution.py:100
  206.6 6.0 leave.2
  216.8 24.9 %collective-permute-done.25.refs_1_ = bf16[256,1536]{1,0:T(8,128)(2,1)S(1)} collective-permute-done((bf16[256,1536]{1,0:T(8,128)(2,1)}, bf16[256,1536]{1,0:T(8,128)(2,1)S(1)}, u32[]{:S(2)}, u32[]{:S(2)}) %collective-permute-start.25) | collective-permute-done | bytes 786464 | tf_op jit(solution)/shard_map/ppermute | solution.py:27
  243.5 7.2 order.2
  259.4 12.1 %expert.8 = (bf16[256,1536]{1,0:T(8,128)(2,1)}, bf16[256,1536]{1,0:T(8,128)(2,1)}, bf16[256,1536]{1,0:T(8,128)(2,1)}, bf16[480,1536]{1,0:T(8,128)(2,1)}, f32[480,768]{1,0:T(8,128)}, /*index=5*/f32[480,768]{1,0:T(8,128)}) custom-call(bf16[3,160,256]{2,1,0:T(8,128)(2,1)} %get-tuple-element.920.pick_ref, f32[3,160,1]{2,1,0:T(8,128)} %copy.330.share_ref, ...), custom_call_target="tpu_custom_call" | custom-call | flops 3000000000 | bytes 9000000 | tf_op jit(solution)/shard_map/expert/pallas_call | solution.py:262
  276.9 12.8 %expert.9 = (bf16[256,1536]{1,0:T(8,128)(2,1)}, bf16[256,1536]{1,0:T(8,128)(2,1)}, bf16[256,1536]{1,0:T(8,128)(2,1)}, bf16[480,1536]{1,0:T(8,128)(2,1)}, f32[480,768]{1,0:T(8,128)}, /*index=5*/f32[480,768]{1,0:T(8,128)}) custom-call(bf16[3,160,256]{2,1,0:T(8,128)(2,1)} %get-tuple-element.921.pick_ref, f32[3,160,1]{2,1,0:T(8,128)} %copy.331.share_ref, ...), custom_call_target="tpu_custom_call" | custom-call | flops 3000000000 | bytes 9000000 | tf_op jit(solution)/shard_map/expert/pallas_call | solution.py:262
  294.9 6.6 expert.10
  301.4 7.3 expert.11
  317.2 18.7 %collective-permute-done.39.refs_4_ = bf16[256,1536]{1,0:T(8,128)(2,1)S(1)} collective-permute-done((bf16[256,1536]{1,0:T(8,128)(2,1)S(1)}, bf16[256,1536]{1,0:T(8,128)(2,1)S(1)}, u32[]{:S(2)}, u32[]{:S(2)}) %collective-permute-start.39) | collective-permute-done | bytes 786464 | tf_op jit(solution)/shard_map/ppermute | solution.py:27
  340.6 8.4 enter.3
  351.7 5.9 collective-permute-done.42.refs_1_
  363.6 6.7 collective-permute-done.45
  376.4 12.0 %attend.3.attended_ref = bf16[256,1536]{1,0:T(8,128)(2,1)} custom-call(s32[8]{0:T(128)} %select_n.165.ids_ref, bf16[256,2304]{1,0:T(8,128)(2,1)} %get-tuple-element.488.query_ref, bf16[1024,512]{1,0:T(8,128)(2,1)} %pad_maximum_fusion.5.key_ref.value_ref, bf16[1024,512]{1,0:T(8,128)(2,1)} %pad_maximum_fusion.5.key_ref.value_ref), custom_call_target="tpu_custom_call" | custom-call | flops 1000000000 | bytes 3000000 | tf_op jit(solution)/shard_map/attend/pallas_call | solution.py:100
  391.4 6.3 collective-permute-done.47.refs_2_
  406.2 6.0 leave.3
  414.1 17.8 %collective-permute-done.49.refs_1_ = bf16[256,1536]{1,0:T(8,128)(2,1)S(1)} collective-permute-done((bf16[256,1536]{1,0:T(8,128)(2,1)}, bf16[256,1536]{1,0:T(8,128)(2,1)S(1)}, u32[]{:S(2)}, u32[]{:S(2)}) %collective-permute-start.49) | collective-permute-done | bytes 786464 | tf_op jit(solution)/shard_map/ppermute | solution.py:27
  432.5 11.0 %collective-permute-done.51.refs_3_ = bf16[4,1,144,1536]{3,2,1,0:T(8,128)(2,1)} collective-permute-done((bf16[4,1,144,1536]{3,2,1,0:T(8,128)(2,1)}, bf16[4,1,144,1536]{3,2,1,0:T(8,128)(2,1)}, u32[]{:S(2)}, u32[]{:S(2)}) %collective-permute-start.51) | collective-permute-done | bytes 1769504 | tf_op jit(solution)/shard_map/ppermute | solution.py:902
  443.5 7.1 order.3
  453.9 12.1 %expert.12 = (bf16[256,1536]{1,0:T(8,128)(2,1)}, bf16[256,1536]{1,0:T(8,128)(2,1)}, bf16[256,1536]{1,0:T(8,128)(2,1)}, bf16[480,1536]{1,0:T(8,128)(2,1)}, f32[480,768]{1,0:T(8,128)}, /*index=5*/f32[480,768]{1,0:T(8,128)}) custom-call(bf16[3,160,256]{2,1,0:T(8,128)(2,1)} %get-tuple-element.918.pick_ref, f32[3,160,1]{2,1,0:T(8,128)} %copy.336.share_ref, ...), custom_call_target="tpu_custom_call" | custom-call | flops 3000000000 | bytes 9000000 | tf_op jit(solution)/shard_map/expert/pallas_call | solution.py:262
  466.0 12.8 %expert.13 = (bf16[256,1536]{1,0:T(8,128)(2,1)}, bf16[256,1536]{1,0:T(8,128)(2,1)}, bf16[256,1536]{1,0:T(8,128)(2,1)}, bf16[480,1536]{1,0:T(8,128)(2,1)}, f32[480,768]{1,0:T(8,128)}, /*index=5*/f32[480,768]{1,0:T(8,128)}) custom-call(bf16[3,160,256]{2,1,0:T(8,128)(2,1)} %get-tuple-element.919.pick_ref, f32[3,160,1]{2,1,0:T(8,128)} %copy.337.share_ref, ...), custom_call_target="tpu_custom_call" | custom-call | flops 3000000000 | bytes 9000000 | tf_op jit(solution)/shard_map/expert/pallas_call | solution.py:262
  482.4 6.5 expert.14
  488.9 9.5 collective-permute-done.54.refs_1_
  500.5 7.2 expert.15
  507.7 13.3 %expert_back.8 = (bf16[256,1536]{1,0:T(8,128)(2,1)}, bf16[256,1536]{1,0:T(8,128)(2,1)}, bf16[256,1536]{1,0:T(8,128)(2,1)}, bf16[480,1536]{1,0:T(8,128)(2,1)}, bf...) custom-call(bf16[3,160,256]{2,1,0:T(8,128)(2,1)} %get-tuple-element.918.pick_ref, ...), custom_call_target="tpu_custom_call" | custom-call | flops 4000000000 | bytes 12000000 | tf_op jit(solution)/shard_map/expert_back/pallas_call | solution.py:322
  521.1 14.2 %expert_back.9 = (bf16[256,1536]{1,0:T(8,128)(2,1)}, bf16[256,1536]{1,0:T(8,128)(2,1)}, bf16[256,1536]{1,0:T(8,128)(2,1)}, bf16[480,1536]{1,0:T(8,128)(2,1)}, bf...) custom-call(bf16[3,160,256]{2,1,0:T(8,128)(2,1)} %get-tuple-element.919.pick_ref, ...), custom_call_target="tpu_custom_call" | custom-call | flops 4000000000 | bytes 12000000 | tf_op jit(solution)/shard_map/expert_back/pallas_call | solution.py:322
  537.4 7.5 expert_back.10
  545.0 8.0 expert_back.11
  558.2 13.6 %expert_grads.4 = bf16[16,144,1536]{2,1,0:T(8,128)(2,1)} custom-call(bf16[480,1536]{1,0:T(8,128)(2,1)} %get-tuple-element.579.refs_0_, bf16[160,1536]{1,0:T(8,128)(2,1)} %get-tuple-element.580.refs_1_, bf16[480,1536]{1,0:T(8,128)(2,1)} %get-tuple-element.581.refs_2_, bf16[160,1536]{1,0:T(8,128)(2,1)} %get-tuple-element.582.refs_3_, ...), custom_call_target="tpu_custom_call" | custom-call | flops 1000000000 | bytes 3000000 | tf_op jit(solution)/shard_map/expert_grads/pallas_call | solution.py:388
  571.8 13.9 %expert_grads.5 = bf16[16,144,1536]{2,1,0:T(8,128)(2,1)} custom-call(bf16[480,1536]{1,0:T(8,128)(2,1)} %get-tuple-element.589.refs_0_, bf16[160,1536]{1,0:T(8,128)(2,1)} %get-tuple-element.590.refs_1_, bf16[480,1536]{1,0:T(8,128)(2,1)} %get-tuple-element.591.refs_2_, bf16[160,1536]{1,0:T(8,128)(2,1)} %get-tuple-element.592.refs_3_, ...), custom_call_target="tpu_custom_call" | custom-call | flops 1000000000 | bytes 3000000 | tf_op jit(solution)/shard_map/expert_grads/pallas_call | solution.py:388
  589.8 11.3 %leave_back.2 = (f32[256,1536]{1,0:T(8,128)}, bf16[256,1536]{1,0:T(8,128)(2,1)}, bf16[256,1536]{1,0:T(8,128)(2,1)}, bf16[1536,768]{1,0:T(8,128)(2,1)}, bf16[1536,768]{1,0:T(8,128)(2,1)}) custom-call(s32[1]{0:T(128)} %bitcast.48.core_ref, f32[1,1536]{1,0:T(1,128)} %copy.344.gain_ref, f32[256,1536]{1,0:T(8,128)} %get-tuple-element.501.mid_ref, ...), custom_call_target="tpu_custom_call" | custom-call | flops 8000000000 | bytes 24000000 | tf_op jit(solution)/shard_map/leave_back/pallas_call | solution.py:439
  609.8 16.7 %attend_back.2 = (bf16[256,1536]{1,0:T(8,128)(2,1)}, bf16[256,512]{1,0:T(8,128)(2,1)}, bf16[256,512]{1,0:T(8,128)(2,1)}, bf16[256,512]{1,0:T(8,128)(2,1)}, bf16[256,512]{1,0:T(8,128)(2,1)}) custom-call(s32[8]{0:T(128)} %select_n.165.ids_ref, bf16[256,2304]{1,0:T(8,128)(2,1)} %get-tuple-element.488.query_ref, ...), custom_call_target="tpu_custom_call" | custom-call | flops 1000000000 | bytes 3000000 | tf_op jit(solution)/shard_map/attend_back/pallas_call | solution.py:150
  632.2 4.4 fusion.41
  647.6 13.6 %enter_back.2 = (f32[256,1536]{1,0:T(8,128)}, bf16[256,1536]{1,0:T(8,128)(2,1)}, bf16[1536,1152]{1,0:T(8,128)(2,1)}, bf16[1536,1152]{1,0:T(8,128)(2,1)}) custom-call(s32[1]{0:T(128)} %bitcast.48.core_ref, f32[1,1536]{1,0:T(1,128)} %copy.347.gain_ref, bf16[256,1536]{1,0:T(8,128)(2,1)} %get-tuple-element.687.rows_ref, ...), custom_call_target="tpu_custom_call" | custom-call | flops 12999999488 | bytes 39000000 | tf_op jit(solution)/shard_map/enter_back/pallas_call | solution.py:439
  661.2 6.3 collective-permute-done.70
  669.6 4.8 fusion.5
  675.1 12.6 %collective-permute-done.72.refs_1_ = bf16[256,1536]{1,0:T(8,128)(2,1)S(1)} collective-permute-done((bf16[256,1536]{1,0:T(8,128)(2,1)}, bf16[256,1536]{1,0:T(8,128)(2,1)S(1)}, u32[]{:S(2)}, u32[]{:S(2)}) %collective-permute-start.72) | collective-permute-done | bytes 786464 | tf_op jit(solution)/shard_map/ppermute | solution.py:27
  695.3 13.7 %expert_back.12 = (bf16[256,1536]{1,0:T(8,128)(2,1)}, bf16[256,1536]{1,0:T(8,128)(2,1)}, bf16[256,1536]{1,0:T(8,128)(2,1)}, bf16[480,1536]{1,0:T(8,128)(2,1)}, b...) custom-call(bf16[3,160,256]{2,1,0:T(8,128)(2,1)} %get-tuple-element.920.pick_ref, ...), custom_call_target="tpu_custom_call" | custom-call | flops 4000000000 | bytes 12000000 | tf_op jit(solution)/shard_map/expert_back/pallas_call | solution.py:322
  709.0 14.0 %expert_back.13 = (bf16[256,1536]{1,0:T(8,128)(2,1)}, bf16[256,1536]{1,0:T(8,128)(2,1)}, bf16[256,1536]{1,0:T(8,128)(2,1)}, bf16[480,1536]{1,0:T(8,128)(2,1)}, b...) custom-call(bf16[3,160,256]{2,1,0:T(8,128)(2,1)} %get-tuple-element.921.pick_ref, ...), custom_call_target="tpu_custom_call" | custom-call | flops 4000000000 | bytes 12000000 | tf_op jit(solution)/shard_map/expert_back/pallas_call | solution.py:322
  723.0 7.4 collective-permute-done.75.refs_0_
  730.6 4.6 fusion.4
  746.3 7.6 expert_back.14
  753.9 7.8 expert_back.15
  761.8 15.3 %collective-permute-done.80.refs_2_ = bf16[256,1536]{1,0:T(8,128)(2,1)} collective-permute-done((bf16[256,1536]{1,0:T(8,128)(2,1)}, bf16[256,1536]{1,0:T(8,128)(2,1)}, u32[]{:S(2)}, u32[]{:S(2)}) %collective-permute-start.80) | collective-permute-done | bytes 786464 | tf_op jit(solution)/shard_map/ppermute | solution.py:27
  785.0 13.6 %expert_grads.6 = bf16[16,144,1536]{2,1,0:T(8,128)(2,1)} custom-call(bf16[480,1536]{1,0:T(8,128)(2,1)} %get-tuple-element.697.refs_0_, bf16[160,1536]{1,0:T(8,128)(2,1)} %get-tuple-element.698.refs_1_, bf16[480,1536]{1,0:T(8,128)(2,1)} %get-tuple-element.699.refs_2_, bf16[160,1536]{1,0:T(8,128)(2,1)} %get-tuple-element.700.refs_3_, ...), custom_call_target="tpu_custom_call" | custom-call | flops 1000000000 | bytes 3000000 | tf_op jit(solution)/shard_map/expert_grads/pallas_call | solution.py:388
  798.6 13.8 %expert_grads.7 = bf16[16,144,1536]{2,1,0:T(8,128)(2,1)} custom-call(bf16[480,1536]{1,0:T(8,128)(2,1)} %get-tuple-element.707.refs_0_, bf16[160,1536]{1,0:T(8,128)(2,1)} %get-tuple-element.708.refs_1_, bf16[480,1536]{1,0:T(8,128)(2,1)} %get-tuple-element.709.refs_2_, bf16[160,1536]{1,0:T(8,128)(2,1)} %get-tuple-element.710.refs_3_, ...), custom_call_target="tpu_custom_call" | custom-call | flops 1000000000 | bytes 3000000 | tf_op jit(solution)/shard_map/expert_grads/pallas_call | solution.py:388
  813.8 11.3 %leave_back.3 = (f32[256,1536]{1,0:T(8,128)}, bf16[256,1536]{1,0:T(8,128)(2,1)}, bf16[256,1536]{1,0:T(8,128)(2,1)}, bf16[1536,768]{1,0:T(8,128)(2,1)}, bf16[1536,768]{1,0:T(8,128)(2,1)}) custom-call(s32[1]{0:T(128)} %bitcast.48.core_ref, f32[1,1536]{1,0:T(1,128)} %copy.329.gain_ref, f32[256,1536]{1,0:T(8,128)} %get-tuple-element.473.refs_0_.mid_ref, ...), custom_call_target="tpu_custom_call" | custom-call | flops 8000000000 | bytes 24000000 | tf_op jit(solution)/shard_map/leave_back/pallas_call | solution.py:439
  829.6 16.6 %attend_back.3 = (bf16[256,1536]{1,0:T(8,128)(2,1)}, bf16[256,512]{1,0:T(8,128)(2,1)}, bf16[256,512]{1,0:T(8,128)(2,1)}, bf16[256,512]{1,0:T(8,128)(2,1)}, bf16[256,512]{1,0:T(8,128)(2,1)}) custom-call(s32[8]{0:T(128)} %select_n.165.ids_ref, bf16[256,2304]{1,0:T(8,128)(2,1)} %get-tuple-element.415.query_ref, ...), custom_call_target="tpu_custom_call" | custom-call | flops 1000000000 | bytes 3000000 | tf_op jit(solution)/shard_map/attend_back/pallas_call | solution.py:150
  849.8 5.9 collective-permute-done.89.refs_1_
  855.7 5.2 collective-permute-done.90.refs_2_
  866.5 13.6 %enter_back.3 = (f32[256,1536]{1,0:T(8,128)}, bf16[256,1536]{1,0:T(8,128)(2,1)}, bf16[1536,1152]{1,0:T(8,128)(2,1)}, bf16[1536,1152]{1,0:T(8,128)(2,1)}) custom-call(s32[1]{0:T(128)} %bitcast.48.core_ref, f32[1,1536]{1,0:T(1,128)} %copy.328.gain_ref, bf16[256,1536]{1,0:T(8,128)(2,1)} %get-tuple-element.412.refs_0_.rows_ref, ...), custom_call_target="tpu_custom_call" | custom-call | flops 12999999488 | bytes 39000000 | tf_op jit(solution)/shard_map/enter_back/pallas_call | solution.py:439
  894.6 30.5 %collective-permute-done.106 = bf16[4,144,1536]{2,1,0:T(8,128)(2,1)S(1)} collective-permute-done((bf16[4,144,1536]{2,1,0:T(8,128)(2,1)S(1)}, bf16[4,144,1536]{2,1,0:T(8,128)(2,1)S(1)}, u32[]{:S(2)}, u32[]{:S(2)}) %collective-permute-start.106) | collective-permute-done | bytes 1769504 | tf_op jit(solution)/shard_map/ppermute | solution.py:943
  931.7 10.0 collective-permute-done.100
  953.7 26.8 %collective-permute-done.104 = bf16[96,1920]{1,0:T(8,128)(2,1)S(1)} collective-permute-done((bf16[96,1920]{1,0:T(8,128)(2,1)S(1)}, bf16[96,1920]{1,0:T(8,128)(2,1)S(1)}, u32[]{:S(2)}, u32[]{:S(2)}) %collective-permute-start.104) | collective-permute-done | bytes 368672 | tf_op jit(solution)/shard_map/ppermute | solution.py:27
  980.5 22.3 %collective-permute-done.103 = bf16[96,1920]{1,0:T(8,128)(2,1)S(1)} collective-permute-done((bf16[96,1920]{1,0:T(8,128)(2,1)S(1)}, bf16[96,1920]{1,0:T(8,128)(2,1)S(1)}, u32[]{:S(2)}, u32[]{:S(2)}) %collective-permute-start.103) | collective-permute-done | bytes 368672 | tf_op jit(solution)/shard_map/ppermute | solution.py:27
  1010.2 19.5 %collective-permute-done.110 = bf16[2,144,1536]{2,1,0:T(8,128)(2,1)S(1)} collective-permute-done((bf16[2,144,1536]{2,1,0:T(8,128)(2,1)S(1)}, bf16[2,144,1536]{2,1,0:T(8,128)(2,1)S(1)}, u32[]{:S(2)}, u32[]{:S(2)}) %collective-permute-start.110) | collective-permute-done | bytes 884768 | tf_op jit(solution)/shard_map/ppermute | solution.py:27
  1029.7 18.5 %collective-permute-done.109 = bf16[2,144,1536]{2,1,0:T(8,128)(2,1)S(1)} collective-permute-done((bf16[2,144,1536]{2,1,0:T(8,128)(2,1)S(1)}, bf16[2,144,1536]{2,1,0:T(8,128)(2,1)S(1)}, u32[]{:S(2)}, u32[]{:S(2)}) %collective-permute-start.109) | collective-permute-done | bytes 884768 | tf_op jit(solution)/shard_map/ppermute | solution.py:27
  1057.0 8.7 finish.1
  (463 shorter events, 304.9 us)
Async XLA Ops:
  7.8 20.6 %collective-permute-start.4 = (bf16[4,1,144,1536]{3,2,0,1:T(8,128)(2,1)}, bf16[4,1,144,1536]{3,2,0,1:T(8,128)(2,1)}, u32[]{:S(2)}, u32[]{:S(2)}) collective-permute-start(bf16[4,1,144,1536]{3,2,0,1:T(8,128)(2,1)} %dynamic-slice_bitcast_fusion), channel_id=1, source_target_pairs={{0,16},{16,0},{1,17},{17,1},{2,18},{18,2},{3,19},{19,3},{4,20},{20... | collective-permute-start | bytes 5308424 | tf_op jit(solution)/shard_map/ppermute | solution.py:27
  33.0 51.0 %collective-permute-start.5 = (bf16[2,1,144,1536]{3,2,1,0:T(8,128)(2,1)S(1)}, bf16[2,1,144,1536]{3,2,1,0:T(8,128)(2,1)S(1)}, u32[]{:S(2)}, u32[]{:S(2)}) collective-permute-start(bf16[2,1,144,1536]{3,2,1,0:T(8,128)(2,1)S(1)} %get-tuple-element.900), channel_id=1, source_target_pairs={{0,4},{4,0},{8,12},{12,8},{1,5},{5,1},{9,13},{13,9},{2,6},{6,2},{1... | collective-permute-start | bytes 2654216 | tf_op jit(solution)/shard_map/ppermute | solution.py:27
  33.5 50.4 %collective-permute-start.6 = (bf16[2,1,144,1536]{3,2,1,0:T(8,128)(2,1)S(1)}, bf16[2,1,144,1536]{3,2,1,0:T(8,128)(2,1)S(1)}, u32[]{:S(2)}, u32[]{:S(2)}) collective-permute-start(bf16[2,1,144,1536]{3,2,1,0:T(8,128)(2,1)S(1)} %get-tuple-element.901), channel_id=1, source_target_pairs={{0,8},{4,12},{8,0},{12,4},{1,9},{5,13},{9,1},{13,5},{2,10},{6,14},... | collective-permute-start | bytes 2654216 | tf_op jit(solution)/shard_map/ppermute | solution.py:27
  35.0 48.9 %collective-permute-start.7 = (bf16[2,1,144,1536]{3,2,1,0:T(8,128)(2,1)S(1)}, bf16[2,1,144,1536]{3,2,1,0:T(8,128)(2,1)S(1)}, u32[]{:S(2)}, u32[]{:S(2)}) collective-permute-start(bf16[2,1,144,1536]{3,2,1,0:T(8,128)(2,1)S(1)} %get-tuple-element.898), channel_id=1, source_target_pairs={{0,12},{4,8},{8,4},{12,0},{1,13},{5,9},{9,5},{13,1},{2,14},{6,10},... | collective-permute-start | bytes 2654216 | tf_op jit(solution)/shard_map/ppermute | solution.py:27
  36.5 42.3 %collective-permute-start.2 = (bf16[96,3072]{1,0:T(8,128)(2,1)S(1)}, bf16[96,3072]{1,0:T(8,128)(2,1)S(1)}, u32[]{:S(2)}, u32[]{:S(2)}) collective-permute-start(bf16[96,3072]{1,0:T(8,128)(2,1)S(1)} %pad_maximum_fusion.7.refs_0_), channel_id=1, source_target_pairs={{0,2},{1,3},{2,0},{3,1},{4,6},{5,7},{6,4},{7,5},{8,10},{9,11},{10,... | collective-permute-start | bytes 1769480 | tf_op jit(solution)/shard_map/ppermute | solution.py:27
  46.0 32.7 %collective-permute-start.3 = (bf16[96,3072]{1,0:T(8,128)(2,1)S(1)}, bf16[96,3072]{1,0:T(8,128)(2,1)S(1)}, u32[]{:S(2)}, u32[]{:S(2)}) collective-permute-start(bf16[96,3072]{1,0:T(8,128)(2,1)S(1)} %pad_maximum_fusion.7.refs_0_), channel_id=1, source_target_pairs={{0,3},{1,2},{2,1},{3,0},{4,7},{5,6},{6,5},{7,4},{8,11},{9,10},{10,... | collective-permute-start | bytes 1769480 | tf_op jit(solution)/shard_map/ppermute | solution.py:27
  89.8 51.7 %collective-permute-start.15 = (bf16[4,1,144,1536]{3,2,1,0:T(8,128)(2,1)}, bf16[4,1,144,1536]{3,2,1,0:T(8,128)(2,1)}, u32[]{:S(2)}, u32[]{:S(2)}) collective-permute-start(bf16[4,1,144,1536]{3,2,1,0:T(8,128)(2,1)} %get-tuple-element.441.refs_0_), channel_id=1, source_target_pairs={{0,2},{2,3},{3,1},{1,0},{4,6},{6,7},{7,5},{5,4},{8,10},{10,11},{11... | collective-permute-start | bytes 5308424 | tf_op jit(solution)/shard_map/ppermute | solution.py:902
  101.5 22.6 %collective-permute-start.12 = (bf16[384,1152]{1,0:T(8,128)(2,1)S(1)}, bf16[384,1152]{1,0:T(8,128)(2,1)S(1)}, u32[]{:S(2)}, u32[]{:S(2)}) collective-permute-start(bf16[384,1152]{1,0:T(8,128)(2,1)S(1)} %get-tuple-element.408.refs_0_), channel_id=1, source_target_pairs={{0,4},{4,0},{8,12},{12,8},{1,5},{5,1},{9,13},{13,9},{2,6},{6,2},{1... | collective-permute-start | bytes 2654216 | tf_op jit(solution)/shard_map/ppermute | solution.py:27
  102.3 37.0 %collective-permute-start.13 = (bf16[384,1152]{1,0:T(8,128)(2,1)S(1)}, bf16[384,1152]{1,0:T(8,128)(2,1)S(1)}, u32[]{:S(2)}, u32[]{:S(2)}) collective-permute-start(bf16[384,1152]{1,0:T(8,128)(2,1)S(1)} %get-tuple-element.408.refs_0_), channel_id=1, source_target_pairs={{0,8},{4,12},{8,0},{12,4},{1,9},{5,13},{9,1},{13,5},{2,10},{6,14},... | collective-permute-start | bytes 2654216 | tf_op jit(solution)/shard_map/ppermute | solution.py:27
  103.9 36.7 %collective-permute-start.14 = (bf16[384,1152]{1,0:T(8,128)(2,1)S(1)}, bf16[384,1152]{1,0:T(8,128)(2,1)S(1)}, u32[]{:S(2)}, u32[]{:S(2)}) collective-permute-start(bf16[384,1152]{1,0:T(8,128)(2,1)S(1)} %get-tuple-element.408.refs_0_), channel_id=1, source_target_pairs={{0,12},{4,8},{8,4},{12,0},{1,13},{5,9},{9,5},{13,1},{2,14},{6,10},... | collective-permute-start | bytes 2654216 | tf_op jit(solution)/shard_map/ppermute | solution.py:27
  151.7 45.3 %collective-permute-start.23 = (bf16[4,1,144,1536]{3,2,1,0:T(8,128)(2,1)}, bf16[4,1,144,1536]{3,2,1,0:T(8,128)(2,1)}, u32[]{:S(2)}, u32[]{:S(2)}) collective-permute-start(bf16[4,1,144,1536]{3,2,1,0:T(8,128)(2,1)} %collective-permute-done.15.refs_1_), channel_id=1, source_target_pairs={{0,2},{2,3},{3,1},{1,0},{4,6},{6,7},{7,5},{5,4},{8,10},{10,11},{11... | collective-permute-start | bytes 5308424 | tf_op jit(solution)/shard_map/ppermute | solution.py:902
  201.7 41.3 %collective-permute-start.27 = (bf16[4,1,144,1536]{3,2,1,0:T(8,128)(2,1)}, bf16[4,1,144,1536]{3,2,1,0:T(8,128)(2,1)}, u32[]{:S(2)}, u32[]{:S(2)}) collective-permute-start(bf16[4,1,144,1536]{3,2,1,0:T(8,128)(2,1)} %collective-permute-done.23.refs_2_), channel_id=1, source_target_pairs={{0,2},{2,3},{3,1},{1,0},{4,6},{6,7},{7,5},{5,4},{8,10},{10,11},{11... | collective-permute-start | bytes 5308424 | tf_op jit(solution)/shard_map/ppermute | solution.py:902
  202.8 39.8 %collective-permute-start.28 = (bf16[384,1152]{1,0:T(8,128)(2,1)}, bf16[384,1152]{1,0:T(8,128)(2,1)S(1)}, u32[]{:S(2)}, u32[]{:S(2)}) collective-permute-start(bf16[384,1152]{1,0:T(8,128)(2,1)} %get-tuple-element.469.refs_0_), channel_id=1, source_target_pairs={{0,4},{4,0},{8,12},{12,8},{1,5},{5,1},{9,13},{13,9},{2,6},{6,2},{1... | collective-permute-start | bytes 2654216 | tf_op jit(solution)/shard_map/ppermute | solution.py:27
  204.0 38.6 %collective-permute-start.29 = (bf16[384,1152]{1,0:T(8,128)(2,1)}, bf16[384,1152]{1,0:T(8,128)(2,1)S(1)}, u32[]{:S(2)}, u32[]{:S(2)}) collective-permute-start(bf16[384,1152]{1,0:T(8,128)(2,1)} %get-tuple-element.469.refs_0_), channel_id=1, source_target_pairs={{0,8},{4,12},{8,0},{12,4},{1,9},{5,13},{9,1},{13,5},{2,10},{6,14},... | collective-permute-start | bytes 2654216 | tf_op jit(solution)/shard_map/ppermute | solution.py:27
  212.5 29.2 %collective-permute-start.25 = (bf16[256,1536]{1,0:T(8,128)(2,1)}, bf16[256,1536]{1,0:T(8,128)(2,1)S(1)}, u32[]{:S(2)}, u32[]{:S(2)}) collective-permute-start(bf16[256,1536]{1,0:T(8,128)(2,1)} %get-tuple-element.445.refs_0_), channel_id=1, source_target_pairs={{0,4},{4,0},{8,12},{12,8},{1,5},{5,1},{9,13},{13,9},{2,6},{6,2},{1... | collective-permute-start | bytes 2359304 | tf_op jit(solution)/shard_map/ppermute | solution.py:27
  213.7 28.9 %collective-permute-start.26 = (bf16[256,1536]{1,0:T(8,128)(2,1)}, bf16[256,1536]{1,0:T(8,128)(2,1)S(1)}, u32[]{:S(2)}, u32[]{:S(2)}) collective-permute-start(bf16[256,1536]{1,0:T(8,128)(2,1)} %get-tuple-element.445.refs_0_), channel_id=1, source_target_pairs={{0,8},{4,12},{8,0},{12,4},{1,9},{5,13},{9,1},{13,5},{2,10},{6,14},... | collective-permute-start | bytes 2359304 | tf_op jit(solution)/shard_map/ppermute | solution.py:27
  250.7 26.2 %collective-permute-start.30 = (bf16[16,144,1536]{2,1,0:T(8,128)(2,1)}, bf16[16,144,1536]{2,1,0:T(8,128)(2,1)}, u32[]{:S(2)}, u32[]{:S(2)}) collective-permute-start(bf16[16,144,1536]{2,1,0:T(8,128)(2,1)} %bitcast.286), channel_id=1, source_target_pairs={{0,16},{16,0},{1,17},{17,1},{2,18},{18,2},{3,19},{19,3},{4,20},{20... | collective-permute-start | bytes 21233672 | tf_op jit(solution)/shard_map/ppermute | solution.py:27
  252.5 37.2 %collective-permute-start.31 = (bf16[256,1536]{1,0:T(8,128)(2,1)S(1)}, bf16[256,1536]{1,0:T(8,128)(2,1)S(1)}, u32[]{:S(2)}, u32[]{:S(2)}) collective-permute-start(bf16[256,1536]{1,0:T(8,128)(2,1)S(1)} %copy-done.9), channel_id=1, source_target_pairs={{0,12},{4,8},{8,4},{12,0},{1,13},{5,9},{9,5},{13,1},{2,14},{6,10},... | collective-permute-start | bytes 2359304 | tf_op jit(solution)/shard_map/ppermute | solution.py:27
  271.6 37.1 %collective-permute-start.37 = (bf16[384,1152]{1,0:T(8,128)(2,1)}, bf16[384,1152]{1,0:T(8,128)(2,1)}, u32[]{:S(2)}, u32[]{:S(2)}) collective-permute-start(bf16[384,1152]{1,0:T(8,128)(2,1)} %get-tuple-element.469.refs_0_), channel_id=1, source_target_pairs={{0,12},{4,8},{8,4},{12,0},{1,13},{5,9},{9,5},{13,1},{2,14},{6,10},... | collective-permute-start | bytes 2654216 | tf_op jit(solution)/shard_map/ppermute | solution.py:27
  315.1 22.9 %collective-permute-start.38 = (bf16[1536,1152]{1,0:T(8,128)(2,1)}, bf16[1536,1152]{1,0:T(8,128)(2,1)S(1)}, u32[]{:S(2)}, u32[]{:S(2)}) collective-permute-start(bf16[1536,1152]{1,0:T(8,128)(2,1)} %place.10.refs_5_.refs_4_), channel_id=1, source_target_pairs={{0,16},{16,0},{1,17},{17,1},{2,18},{18,2},{3,19},{19,3},{4,20},{20... | collective-permute-start | bytes 10616840 | tf_op jit(solution)/shard_map/ppermute | solution.py:27
  315.1 20.9 %collective-permute-start.39 = (bf16[256,1536]{1,0:T(8,128)(2,1)S(1)}, bf16[256,1536]{1,0:T(8,128)(2,1)S(1)}, u32[]{:S(2)}, u32[]{:S(2)}) collective-permute-start(bf16[256,1536]{1,0:T(8,128)(2,1)S(1)} %copy-done.59), channel_id=1, source_target_pairs={{0,12},{4,8},{8,4},{12,0},{1,13},{5,9},{9,5},{13,1},{2,14},{6,10},... | collective-permute-start | bytes 2359304 | tf_op jit(solution)/shard_map/ppermute | solution.py:27
  316.6 41.0 %collective-permute-start.42 = (bf16[4,1,144,1536]{3,2,1,0:T(8,128)(2,1)}, bf16[4,1,144,1536]{3,2,1,0:T(8,128)(2,1)}, u32[]{:S(2)}, u32[]{:S(2)}) collective-permute-start(bf16[4,1,144,1536]{3,2,1,0:T(8,128)(2,1)} %get-tuple-element.509.refs_0_), channel_id=1, source_target_pairs={{0,2},{2,3},{3,1},{1,0},{4,6},{6,7},{7,5},{5,4},{8,10},{10,11},{11... | collective-permute-start | bytes 5308424 | tf_op jit(solution)/shard_map/ppermute | solution.py:902
  357.6 40.2 %collective-permute-start.47 = (bf16[4,1,144,1536]{3,2,1,0:T(8,128)(2,1)}, bf16[4,1,144,1536]{3,2,1,0:T(8,128)(2,1)}, u32[]{:S(2)}, u32[]{:S(2)}) collective-permute-start(bf16[4,1,144,1536]{3,2,1,0:T(8,128)(2,1)} %collective-permute-done.42.refs_1_), channel_id=1, source_target_pairs={{0,2},{2,3},{3,1},{1,0},{4,6},{6,7},{7,5},{5,4},{8,10},{10,11},{11... | collective-permute-start | bytes 5308424 | tf_op jit(solution)/shard_map/ppermute | solution.py:902
  401.3 42.2 %collective-permute-start.51 = (bf16[4,1,144,1536]{3,2,1,0:T(8,128)(2,1)}, bf16[4,1,144,1536]{3,2,1,0:T(8,128)(2,1)}, u32[]{:S(2)}, u32[]{:S(2)}) collective-permute-start(bf16[4,1,144,1536]{3,2,1,0:T(8,128)(2,1)} %collective-permute-done.47.refs_2_), channel_id=1, source_target_pairs={{0,2},{2,3},{3,1},{1,0},{4,6},{6,7},{7,5},{5,4},{8,10},{10,11},{11... | collective-permute-start | bytes 5308424 | tf_op jit(solution)/shard_map/ppermute | solution.py:902
  450.6 28.2 %collective-permute-start.53 = (bf16[256,1536]{1,0:T(8,128)(2,1)S(1)}, bf16[256,1536]{1,0:T(8,128)(2,1)S(1)}, u32[]{:S(2)}, u32[]{:S(2)}) collective-permute-start(bf16[256,1536]{1,0:T(8,128)(2,1)S(1)} %copy-done.15), channel_id=1, source_target_pairs={{0,12},{4,8},{8,4},{12,0},{1,13},{5,9},{9,5},{13,1},{2,14},{6,10},... | collective-permute-start | bytes 2359304 | tf_op jit(solution)/shard_map/ppermute | solution.py:27
  499.1 36.2 %collective-permute-start.56 = (bf16[256,1536]{1,0:T(8,128)(2,1)S(1)}, bf16[256,1536]{1,0:T(8,128)(2,1)S(1)}, u32[]{:S(2)}, u32[]{:S(2)}) collective-permute-start(bf16[256,1536]{1,0:T(8,128)(2,1)S(1)} %get-tuple-element.534.refs_0_.cot_ref), channel_id=1, source_target_pairs={{0,12},{4,8},{8,4},{12,0},{1,13},{5,9},{9,5},{13,1},{2,14},{6,10},... | collective-permute-start | bytes 2359304 | tf_op jit(solution)/shard_map/ppermute | solution.py:27
  554.7 31.0 %collective-permute-start.59 = (bf16[256,1536]{1,0:T(8,128)(2,1)}, bf16[256,1536]{1,0:T(8,128)(2,1)}, u32[]{:S(2)}, u32[]{:S(2)}) collective-permute-start(bf16[256,1536]{1,0:T(8,128)(2,1)} %get-tuple-element.578), channel_id=1, source_target_pairs={{0,12},{4,8},{8,4},{12,0},{1,13},{5,9},{9,5},{13,1},{2,14},{6,10},... | collective-permute-start | bytes 2359304 | tf_op jit(solution)/shard_map/ppermute | solution.py:27
  556.1 33.0 %collective-permute-start.60 = (bf16[256,1536]{1,0:T(8,128)(2,1)S(1)}, bf16[256,1536]{1,0:T(8,128)(2,1)}, u32[]{:S(2)}, u32[]{:S(2)}) collective-permute-start(bf16[256,1536]{1,0:T(8,128)(2,1)S(1)} %copy-done.55), channel_id=1, source_target_pairs={{0,4},{4,0},{8,12},{12,8},{1,5},{5,1},{9,13},{13,9},{2,6},{6,2},{1... | collective-permute-start | bytes 2359304 | tf_op jit(solution)/shard_map/ppermute | solution.py:27
  557.0 32.7 %collective-permute-start.61 = (bf16[256,1536]{1,0:T(8,128)(2,1)S(1)}, bf16[256,1536]{1,0:T(8,128)(2,1)}, u32[]{:S(2)}, u32[]{:S(2)}) collective-permute-start(bf16[256,1536]{1,0:T(8,128)(2,1)S(1)} %copy-done.54), channel_id=1, source_target_pairs={{0,8},{4,12},{8,0},{12,4},{1,9},{5,13},{9,1},{13,5},{2,10},{6,14},... | collective-permute-start | bytes 2359304 | tf_op jit(solution)/shard_map/ppermute | solution.py:27
  601.0 27.6 %collective-permute-start.62 = (bf16[1536,768]{1,0:T(8,128)(2,1)}, bf16[1536,768]{1,0:T(8,128)(2,1)}, u32[]{:S(2)}, u32[]{:S(2)}) collective-permute-start(bf16[1536,768]{1,0:T(8,128)(2,1)} %get-tuple-element.615), channel_id=1, source_target_pairs={{0,16},{16,0},{1,17},{17,1},{2,18},{18,2},{3,19},{19,3},{4,20},{20... | collective-permute-start | bytes 7077896 | tf_op jit(solution)/shard_map/ppermute | solution.py:27
  606.0 41.7 %collective-permute-start.68 = (bf16[4,144,1536]{2,1,0:T(8,128)(2,1)}, bf16[4,144,1536]{2,1,0:T(8,128)(2,1)}, u32[]{:S(2)}, u32[]{:S(2)}) collective-permute-start(bf16[4,144,1536]{2,1,0:T(8,128)(2,1)} %fusion.9), channel_id=1, source_target_pairs={{0,2},{2,3},{3,1},{1,0},{4,6},{6,7},{7,5},{5,4},{8,10},{10,11},{11... | collective-permute-start | bytes 5308424 | tf_op jit(solution)/shard_map/ppermute | solution.py:943
  608.4 20.3 %collective-permute-start.63 = (bf16[256,1536]{1,0:T(8,128)(2,1)}, bf16[256,1536]{1,0:T(8,128)(2,1)S(1)}, u32[]{:S(2)}, u32[]{:S(2)}) collective-permute-start(bf16[256,1536]{1,0:T(8,128)(2,1)} %get-tuple-element.616), channel_id=1, source_target_pairs={{0,12},{4,8},{8,4},{12,0},{1,13},{5,9},{9,5},{13,1},{2,14},{6,10},... | collective-permute-start | bytes 2359304 | tf_op jit(solution)/shard_map/ppermute | solution.py:27
  636.6 24.7 %collective-permute-start.69 = (bf16[384,768]{1,0:T(8,128)(2,1)}, bf16[384,768]{1,0:T(8,128)(2,1)}, u32[]{:S(2)}, u32[]{:S(2)}) collective-permute-start(bf16[384,768]{1,0:T(8,128)(2,1)} %get-tuple-element.890), channel_id=1, source_target_pairs={{0,4},{4,0},{8,12},{12,8},{1,5},{5,1},{9,13},{13,9},{2,6},{6,2},{1... | collective-permute-start | bytes 1769480 | tf_op jit(solution)/shard_map/ppermute | solution.py:27
  639.6 27.9 %collective-permute-start.70 = (bf16[384,768]{1,0:T(8,128)(2,1)}, bf16[384,768]{1,0:T(8,128)(2,1)}, u32[]{:S(2)}, u32[]{:S(2)}) collective-permute-start(bf16[384,768]{1,0:T(8,128)(2,1)} %get-tuple-element.889), channel_id=1, source_target_pairs={{0,8},{4,12},{8,0},{12,4},{1,9},{5,13},{9,1},{13,5},{2,10},{6,14},... | collective-permute-start | bytes 1769480 | tf_op jit(solution)/shard_map/ppermute | solution.py:27
  640.8 26.7 %collective-permute-start.71 = (bf16[384,768]{1,0:T(8,128)(2,1)}, bf16[384,768]{1,0:T(8,128)(2,1)}, u32[]{:S(2)}, u32[]{:S(2)}) collective-permute-start(bf16[384,768]{1,0:T(8,128)(2,1)} %get-tuple-element.888), channel_id=1, source_target_pairs={{0,12},{4,8},{8,4},{12,0},{1,13},{5,9},{9,5},{13,1},{2,14},{6,10},... | collective-permute-start | bytes 1769480 | tf_op jit(solution)/shard_map/ppermute | solution.py:27
  667.5 21.1 %collective-permute-start.74 = (bf16[1536,1152]{1,0:T(8,128)(2,1)}, bf16[1536,1152]{1,0:T(8,128)(2,1)S(1)}, u32[]{:S(2)}, u32[]{:S(2)}) collective-permute-start(bf16[1536,1152]{1,0:T(8,128)(2,1)} %get-tuple-element.642), channel_id=1, source_target_pairs={{0,16},{16,0},{1,17},{17,1},{2,18},{18,2},{3,19},{19,3},{4,20},{20... | collective-permute-start | bytes 10616840 | tf_op jit(solution)/shard_map/ppermute | solution.py:27
  667.5 20.2 %collective-permute-start.72 = (bf16[256,1536]{1,0:T(8,128)(2,1)}, bf16[256,1536]{1,0:T(8,128)(2,1)S(1)}, u32[]{:S(2)}, u32[]{:S(2)}) collective-permute-start(bf16[256,1536]{1,0:T(8,128)(2,1)} %get-tuple-element.645.refs_0_.cot_ref), channel_id=1, source_target_pairs={{0,4},{4,0},{8,12},{12,8},{1,5},{5,1},{9,13},{13,9},{2,6},{6,2},{1... | collective-permute-start | bytes 2359304 | tf_op jit(solution)/shard_map/ppermute | solution.py:27
  674.4 56.1 %collective-permute-start.76 = (bf16[4,144,1536]{2,1,0:T(8,128)(2,1)}, bf16[4,144,1536]{2,1,0:T(8,128)(2,1)}, u32[]{:S(2)}, u32[]{:S(2)}) collective-permute-start(bf16[4,144,1536]{2,1,0:T(8,128)(2,1)} %fusion.5), channel_id=1, source_target_pairs={{0,2},{2,3},{3,1},{1,0},{4,6},{6,7},{7,5},{5,4},{8,10},{10,11},{11... | collective-permute-start | bytes 5308424 | tf_op jit(solution)/shard_map/ppermute | solution.py:943
  691.8 38.6 %collective-permute-start.77 = (bf16[384,1152]{1,0:T(8,128)(2,1)}, bf16[384,1152]{1,0:T(8,128)(2,1)}, u32[]{:S(2)}, u32[]{:S(2)}) collective-permute-start(bf16[384,1152]{1,0:T(8,128)(2,1)} %get-tuple-element.881), channel_id=1, source_target_pairs={{0,4},{4,0},{8,12},{12,8},{1,5},{5,1},{9,13},{13,9},{2,6},{6,2},{1... | collective-permute-start | bytes 2654216 | tf_op jit(solution)/shard_map/ppermute | solution.py:27
  692.7 38.0 %collective-permute-start.78 = (bf16[384,1152]{1,0:T(8,128)(2,1)}, bf16[384,1152]{1,0:T(8,128)(2,1)}, u32[]{:S(2)}, u32[]{:S(2)}) collective-permute-start(bf16[384,1152]{1,0:T(8,128)(2,1)} %get-tuple-element.880), channel_id=1, source_target_pairs={{0,8},{4,12},{8,0},{12,4},{1,9},{5,13},{9,1},{13,5},{2,10},{6,14},... | collective-permute-start | bytes 2654216 | tf_op jit(solution)/shard_map/ppermute | solution.py:27
  693.9 36.6 %collective-permute-start.75 = (bf16[256,1536]{1,0:T(8,128)(2,1)}, bf16[256,1536]{1,0:T(8,128)(2,1)}, u32[]{:S(2)}, u32[]{:S(2)}) collective-permute-start(bf16[256,1536]{1,0:T(8,128)(2,1)} %get-tuple-element.645.refs_0_.cot_ref), channel_id=1, source_target_pairs={{0,12},{4,8},{8,4},{12,0},{1,13},{5,9},{9,5},{13,1},{2,14},{6,10},... | collective-permute-start | bytes 2359304 | tf_op jit(solution)/shard_map/ppermute | solution.py:27
  735.2 41.8 %collective-permute-start.81 = (bf16[4,144,1536]{2,1,0:T(8,128)(2,1)}, bf16[4,144,1536]{2,1,0:T(8,128)(2,1)}, u32[]{:S(2)}, u32[]{:S(2)}) collective-permute-start(bf16[4,144,1536]{2,1,0:T(8,128)(2,1)} %fusion.4), channel_id=1, source_target_pairs={{0,2},{2,3},{3,1},{1,0},{4,6},{6,7},{7,5},{5,4},{8,10},{10,11},{11... | collective-permute-start | bytes 5308424 | tf_op jit(solution)/shard_map/ppermute | solution.py:943
  736.9 24.8 %collective-permute-start.79 = (bf16[256,1536]{1,0:T(8,128)(2,1)}, bf16[256,1536]{1,0:T(8,128)(2,1)}, u32[]{:S(2)}, u32[]{:S(2)}) collective-permute-start(bf16[256,1536]{1,0:T(8,128)(2,1)} %get-tuple-element.666), channel_id=1, source_target_pairs={{0,4},{4,0},{8,12},{12,8},{1,5},{5,1},{9,13},{13,9},{2,6},{6,2},{1... | collective-permute-start | bytes 2359304 | tf_op jit(solution)/shard_map/ppermute | solution.py:27
  738.1 38.9 %collective-permute-start.80 = (bf16[256,1536]{1,0:T(8,128)(2,1)}, bf16[256,1536]{1,0:T(8,128)(2,1)}, u32[]{:S(2)}, u32[]{:S(2)}) collective-permute-start(bf16[256,1536]{1,0:T(8,128)(2,1)} %get-tuple-element.667), channel_id=1, source_target_pairs={{0,8},{4,12},{8,0},{12,4},{1,9},{5,13},{9,1},{13,5},{2,10},{6,14},... | collective-permute-start | bytes 2359304 | tf_op jit(solution)/shard_map/ppermute | solution.py:27
  740.6 36.4 %collective-permute-start.83 = (bf16[384,1152]{1,0:T(8,128)(2,1)S(1)}, bf16[384,1152]{1,0:T(8,128)(2,1)S(1)}, u32[]{:S(2)}, u32[]{:S(2)}) collective-permute-start(bf16[384,1152]{1,0:T(8,128)(2,1)S(1)} %fusion.16), channel_id=1, source_target_pairs={{0,12},{4,8},{8,4},{12,0},{1,13},{5,9},{9,5},{13,1},{2,14},{6,10},... | collective-permute-start | bytes 2654216 | tf_op jit(solution)/shard_map/ppermute | solution.py:27
  779.1 33.2 %collective-permute-start.87 = (bf16[96,1920]{1,0:T(8,128)(2,1)S(1)}, bf16[96,1920]{1,0:T(8,128)(2,1)S(1)}, u32[]{:S(2)}, u32[]{:S(2)}) collective-permute-start(bf16[96,1920]{1,0:T(8,128)(2,1)S(1)} %get-tuple-element.912), channel_id=1, source_target_pairs={{0,3},{1,2},{2,1},{3,0},{4,7},{5,6},{6,5},{7,4},{8,11},{9,10},{10,... | collective-permute-start | bytes 1105928 | tf_op jit(solution)/shard_map/ppermute | solution.py:27
  781.7 31.8 %collective-permute-start.86 = (bf16[96,1920]{1,0:T(8,128)(2,1)S(1)}, bf16[96,1920]{1,0:T(8,128)(2,1)S(1)}, u32[]{:S(2)}, u32[]{:S(2)}) collective-permute-start(bf16[96,1920]{1,0:T(8,128)(2,1)S(1)} %get-tuple-element.913), channel_id=1, source_target_pairs={{0,2},{1,3},{2,0},{3,1},{4,6},{5,7},{6,4},{7,5},{8,10},{9,11},{10,... | collective-permute-start | bytes 1105928 | tf_op jit(solution)/shard_map/ppermute | solution.py:27
  782.0 31.5 %collective-permute-start.85 = (bf16[96,1920]{1,0:T(8,128)(2,1)S(1)}, bf16[96,1920]{1,0:T(8,128)(2,1)S(1)}, u32[]{:S(2)}, u32[]{:S(2)}) collective-permute-start(bf16[96,1920]{1,0:T(8,128)(2,1)S(1)} %get-tuple-element.911), channel_id=1, source_target_pairs={{0,1},{1,0},{2,3},{3,2},{4,5},{5,4},{6,7},{7,6},{8,9},{9,8},{10,11... | collective-permute-start | bytes 1105928 | tf_op jit(solution)/shard_map/ppermute | solution.py:27
  783.6 30.1 %collective-permute-start.84 = (bf16[256,1536]{1,0:T(8,128)(2,1)}, bf16[256,1536]{1,0:T(8,128)(2,1)}, u32[]{:S(2)}, u32[]{:S(2)}) collective-permute-start(bf16[256,1536]{1,0:T(8,128)(2,1)} %get-tuple-element.696), channel_id=1, source_target_pairs={{0,12},{4,8},{8,4},{12,0},{1,13},{5,9},{9,5},{13,1},{2,14},{6,10},... | collective-permute-start | bytes 2359304 | tf_op jit(solution)/shard_map/ppermute | solution.py:27
  825.1 21.2 %collective-permute-start.88 = (bf16[1536,768]{1,0:T(8,128)(2,1)}, bf16[1536,768]{1,0:T(8,128)(2,1)}, u32[]{:S(2)}, u32[]{:S(2)}) collective-permute-start(bf16[1536,768]{1,0:T(8,128)(2,1)} %get-tuple-element.746), channel_id=1, source_target_pairs={{0,16},{16,0},{1,17},{17,1},{2,18},{18,2},{3,19},{19,3},{4,20},{20... | collective-permute-start | bytes 7077896 | tf_op jit(solution)/shard_map/ppermute | solution.py:27
  829.4 50.7 %collective-permute-start.95 = (bf16[4,144,1536]{2,1,0:T(8,128)(2,1)}, bf16[4,144,1536]{2,1,0:T(8,128)(2,1)}, u32[]{:S(2)}, u32[]{:S(2)}) collective-permute-start(bf16[4,144,1536]{2,1,0:T(8,128)(2,1)} %fusion.10), channel_id=1, source_target_pairs={{0,2},{2,3},{3,1},{1,0},{4,6},{6,7},{7,5},{5,4},{8,10},{10,11},{11... | collective-permute-start | bytes 5308424 | tf_op jit(solution)/shard_map/ppermute | solution.py:943
  883.8 41.3 %collective-permute-start.106 = (bf16[4,144,1536]{2,1,0:T(8,128)(2,1)S(1)}, bf16[4,144,1536]{2,1,0:T(8,128)(2,1)S(1)}, u32[]{:S(2)}, u32[]{:S(2)}) collective-permute-start(bf16[4,144,1536]{2,1,0:T(8,128)(2,1)S(1)} %fusion.3), channel_id=1, source_target_pairs={{0,2},{2,3},{3,1},{1,0},{4,6},{6,7},{7,5},{5,4},{8,10},{10,11},{11... | collective-permute-start | bytes 5308424 | tf_op jit(solution)/shard_map/ppermute | solution.py:943
  887.5 54.1 %collective-permute-start.97 = (bf16[384,1152]{1,0:T(8,128)(2,1)S(1)}, bf16[384,1152]{1,0:T(8,128)(2,1)S(1)}, u32[]{:S(2)}, u32[]{:S(2)}) collective-permute-start(bf16[384,1152]{1,0:T(8,128)(2,1)S(1)} %get-tuple-element.878), channel_id=1, source_target_pairs={{0,4},{4,0},{8,12},{12,8},{1,5},{5,1},{9,13},{13,9},{2,6},{6,2},{1... | collective-permute-start | bytes 2654216 | tf_op jit(solution)/shard_map/ppermute | solution.py:27
  888.7 53.1 %collective-permute-start.98 = (bf16[384,1152]{1,0:T(8,128)(2,1)S(1)}, bf16[384,1152]{1,0:T(8,128)(2,1)S(1)}, u32[]{:S(2)}, u32[]{:S(2)}) collective-permute-start(bf16[384,1152]{1,0:T(8,128)(2,1)S(1)} %get-tuple-element.877), channel_id=1, source_target_pairs={{0,8},{4,12},{8,0},{12,4},{1,9},{5,13},{9,1},{13,5},{2,10},{6,14},... | collective-permute-start | bytes 2654216 | tf_op jit(solution)/shard_map/ppermute | solution.py:27
  889.6 52.2 %collective-permute-start.99 = (bf16[384,1152]{1,0:T(8,128)(2,1)S(1)}, bf16[384,1152]{1,0:T(8,128)(2,1)S(1)}, u32[]{:S(2)}, u32[]{:S(2)}) collective-permute-start(bf16[384,1152]{1,0:T(8,128)(2,1)S(1)} %get-tuple-element.876), channel_id=1, source_target_pairs={{0,12},{4,8},{8,4},{12,0},{1,13},{5,9},{9,5},{13,1},{2,14},{6,10},... | collective-permute-start | bytes 2654216 | tf_op jit(solution)/shard_map/ppermute | solution.py:27
  893.1 48.5 %collective-permute-start.100 = (bf16[384,768]{1,0:T(8,128)(2,1)S(1)}, bf16[384,768]{1,0:T(8,128)(2,1)S(1)}, u32[]{:S(2)}, u32[]{:S(2)}) collective-permute-start(bf16[384,768]{1,0:T(8,128)(2,1)S(1)} %fusion.44), channel_id=1, source_target_pairs={{0,12},{4,8},{8,4},{12,0},{1,13},{5,9},{9,5},{13,1},{2,14},{6,10},... | collective-permute-start | bytes 1769480 | tf_op jit(solution)/shard_map/ppermute | solution.py:27
  928.0 75.1 %collective-permute-start.107 = (bf16[4,144,1536]{2,1,0:T(8,128)(2,1)S(1)}, bf16[4,144,1536]{2,1,0:T(8,128)(2,1)S(1)}, u32[]{:S(2)}, u32[]{:S(2)}) collective-permute-start(bf16[4,144,1536]{2,1,0:T(8,128)(2,1)S(1)} %fusion.2), channel_id=1, source_target_pairs={{0,2},{2,3},{3,1},{1,0},{4,6},{6,7},{7,5},{5,4},{8,10},{10,11},{11... | collective-permute-start | bytes 5308424 | tf_op jit(solution)/shard_map/ppermute | solution.py:943
  944.0 36.5 %collective-permute-start.104 = (bf16[96,1920]{1,0:T(8,128)(2,1)S(1)}, bf16[96,1920]{1,0:T(8,128)(2,1)S(1)}, u32[]{:S(2)}, u32[]{:S(2)}) collective-permute-start(bf16[96,1920]{1,0:T(8,128)(2,1)S(1)} %get-tuple-element.909), channel_id=1, source_target_pairs={{0,3},{1,2},{2,1},{3,0},{4,7},{5,6},{6,5},{7,4},{8,11},{9,10},{10,... | collective-permute-start | bytes 1105928 | tf_op jit(solution)/shard_map/ppermute | solution.py:27
  946.4 56.3 %collective-permute-start.103 = (bf16[96,1920]{1,0:T(8,128)(2,1)S(1)}, bf16[96,1920]{1,0:T(8,128)(2,1)S(1)}, u32[]{:S(2)}, u32[]{:S(2)}) collective-permute-start(bf16[96,1920]{1,0:T(8,128)(2,1)S(1)} %get-tuple-element.910), channel_id=1, source_target_pairs={{0,2},{1,3},{2,0},{3,1},{4,6},{5,7},{6,4},{7,5},{8,10},{9,11},{10,... | collective-permute-start | bytes 1105928 | tf_op jit(solution)/shard_map/ppermute | solution.py:27
  947.1 55.7 %collective-permute-start.102 = (bf16[96,1920]{1,0:T(8,128)(2,1)S(1)}, bf16[96,1920]{1,0:T(8,128)(2,1)S(1)}, u32[]{:S(2)}, u32[]{:S(2)}) collective-permute-start(bf16[96,1920]{1,0:T(8,128)(2,1)S(1)} %get-tuple-element.908), channel_id=1, source_target_pairs={{0,1},{1,0},{2,3},{3,2},{4,5},{5,4},{6,7},{7,6},{8,9},{9,8},{10,11... | collective-permute-start | bytes 1105928 | tf_op jit(solution)/shard_map/ppermute | solution.py:27
  1006.2 23.4 %collective-permute-start.110 = (bf16[2,144,1536]{2,1,0:T(8,128)(2,1)S(1)}, bf16[2,144,1536]{2,1,0:T(8,128)(2,1)S(1)}, u32[]{:S(2)}, u32[]{:S(2)}) collective-permute-start(bf16[2,144,1536]{2,1,0:T(8,128)(2,1)S(1)} %get-tuple-element.897), channel_id=1, source_target_pairs={{0,12},{4,8},{8,4},{12,0},{1,13},{5,9},{9,5},{13,1},{2,14},{6,10},... | collective-permute-start | bytes 2654216 | tf_op jit(solution)/shard_map/ppermute | solution.py:27
  1007.7 40.5 %collective-permute-start.109 = (bf16[2,144,1536]{2,1,0:T(8,128)(2,1)S(1)}, bf16[2,144,1536]{2,1,0:T(8,128)(2,1)S(1)}, u32[]{:S(2)}, u32[]{:S(2)}) collective-permute-start(bf16[2,144,1536]{2,1,0:T(8,128)(2,1)S(1)} %get-tuple-element.896), channel_id=1, source_target_pairs={{0,8},{4,12},{8,0},{12,4},{1,9},{5,13},{9,1},{13,5},{2,10},{6,14},... | collective-permute-start | bytes 2654216 | tf_op jit(solution)/shard_map/ppermute | solution.py:27
  1008.9 39.3 %collective-permute-start.108 = (bf16[2,144,1536]{2,1,0:T(8,128)(2,1)S(1)}, bf16[2,144,1536]{2,1,0:T(8,128)(2,1)S(1)}, u32[]{:S(2)}, u32[]{:S(2)}) collective-permute-start(bf16[2,144,1536]{2,1,0:T(8,128)(2,1)S(1)} %get-tuple-element.895), channel_id=1, source_target_pairs={{0,4},{4,0},{8,12},{12,8},{1,5},{5,1},{9,13},{13,9},{2,6},{6,2},{1... | collective-permute-start | bytes 2654216 | tf_op jit(solution)/shard_map/ppermute | solution.py:27
  1010.0 43.5 %collective-permute-start.101 = (f32[256,1536]{1,0:T(8,128)S(1)}, f32[256,1536]{1,0:T(8,128)S(1)}, u32[]{:S(2)}, u32[]{:S(2)}) collective-permute-start(f32[256,1536]{1,0:T(8,128)S(1)} %broadcast_select_fusion.2), channel_id=1, source_target_pairs={{0,16},{16,0},{1,17},{17,1},{2,18},{18,2},{3,19},{19,3},{4,20},{20... | collective-permute-start | bytes 4718600 | tf_op jit(solution)/shard_map/ppermute | solution.py:27
  (123 other events, 1753.4 us)

commit v2 on v1

--- a/solution.py
+++ b/solution.py
@@ -632,7 +632,7 @@
             pltpu.VMEM((rows, width), f32),
         ],
         "enter_back",
-        13,
+        1,
     )
 
 
@@ -979,12 +979,13 @@
     def sum_square(parts):
         return sum(part.astype(f32) for part in parts).astype(bf16)
 
+    def send_deep(mine):
+        mine = mine.reshape(n_fsdp, shard_rows, -1)
+        parts = [swap(at(mine, depth ^ bit), "fsdp", bit) for bit in range(1, n_fsdp)]
+        return [at(mine, depth)] + parts
+
     def reduce_deep(mine):
-        mine = mine.reshape(n_fsdp, shard_rows, -1)
-        total = at(mine, depth).astype(f32)
-        for bit in range(1, n_fsdp):
-            total = total + swap(at(mine, depth ^ bit), "fsdp", bit).astype(f32)
-        return total
+        return sum(part.astype(f32) for part in send_deep(mine))
 
     if pieces == 1:
         units_here = jnp.arange(per_core, dtype=jnp.uint32)
@@ -1271,10 +1272,12 @@
         term,
         enter_first,
     )
-    grads, leave_parts, leave_grads, units_moving = tie(
-        grads, leave_parts, leave_grads, ring_move(units_moving)
-    )
-    enter_grads = (grads[0], swap(grads[1], "section", 1))
+    grads, leave_parts, leave_grads, units_moving, second_moved = tie(
+        grads, leave_parts, leave_grads, ring_move(units_moving), second_moved
+    )
+    enter_grads, second_scattered = tie(
+        (grads[0], swap(grads[1], "section", 1)), scatter_units(second_moved)
+    )
     units_moving = after(ring_move(ring_add(units_moving, 1)), enter_grads)
     enter_parts, leave_parts, first_entry = tie(
         trade_square(*enter_grads, range(n_ctx)),
@@ -1282,9 +1285,11 @@
         first_entry,
     )
     first_moving = [sum_square(parts) for parts in (enter_parts, leave_parts)]
-    first_dense = reduce_deep(jnp.concatenate(first_moving, axis=1))
-    scattered = scatter_units(ring_rest(ring_add(units_moving, 2), 3) + second_moved)
-    first_scattered, second_scattered = (scattered[:, :per_core], scattered[:, per_core:])
+    first_dense, first_scattered = tie(
+        send_deep(jnp.concatenate(first_moving, axis=1)),
+        scatter_units(ring_rest(ring_add(units_moving, 2), 3)),
+    )
+    first_dense = sum(part.astype(f32) for part in first_dense)
 
     layer_out = jnp.stack(layer_outs)
     input_grads = jnp.stack(keep_own(first_entry, second_entry))

time: 1080 us -> 1050 us (0.972)
  waiting for transfers between devices: 404 us -> 362 us
    ppermute x6, waiting for transfers between devices: 34 us -> 7.6 us  [ring_move(): lax.ppermute(moving, 'fsdp', ring_steps)]
    ppermute x100 -> x103, waiting for transfers between devices: 346 us -> 331 us  [swap(): lax.ppermute(value, axis, [(source, source ^ bit) for source in range(cou...]
    convert_element_type x4 -> x6, other arithmetic: 15.9 us -> 23.6 us  [ring_add(): (moved.astype(f32) + ring_part(terms, step + 1)).astype(bf16)]
    ppermute x100 -> x103, starting transfers between devices: 105 us -> 110 us  [swap(): lax.ppermute(value, axis, [(source, source ^ bit) for source in range(cou...]
  transfers between devices with their start and end apart: 112 -> 115, of which waited for: 58 -> 60; matrix products, arithmetic and copies ran while one was open for 10% -> 10% of each run, Pallas kernels for 34% -> 35%
where the time goes in v2:
time: 1050 us; the launch traced here: 1040 us
  Pallas kernels  402 us (38%)
  waiting for transfers between devices  362 us (34%)
  starting transfers between devices  136 us (13%)
  other arithmetic  87.9 us (8%)
  local copies, waits for them, and re-layouts  46 us (4%)
    ppermute x103, waiting for transfers between devices, swap(): lax.ppermute(value, axis, [(source, source ^ bit) for source in range(cou...  331 us
    ppermute x103, starting transfers between devices, swap(): lax.ppermute(value, axis, [(source, source ^ bit) for source in range(cou...  110 us
    pallas_call x8, Pallas kernels, expert_back_call(): pl.pallas_call(functools.partial(expert_back_kernel, blocks, 1 if before...  86 us
    pallas_call x8, Pallas kernels, expert_call(): pl.pallas_call(functools.partial(expert_kernel, blocks, 1 if before else...  77.7 us
    pallas_call x8, Pallas kernels, dense_call(): pl.pallas_call(kernel, grid_spec=pltpu.PrefetchScalarGridSpec(num_scalar_...  77.1 us
    pallas_call x4, Pallas kernels, expert_grads_call(): pl.pallas_call(functools.partial(expert_grads_kernel, len(picked), deep),...  54.8 us
    pallas_call x2, Pallas kernels, attend_back_call(): pl.pallas_call(attend_back_kernel, grid_spec=pltpu.PrefetchScalarGridSpec...  33.2 us
    pallas_call x2, Pallas kernels, attend_call(): pl.pallas_call(attend_kernel, grid_spec=pltpu.PrefetchScalarGridSpec(num_...  24.1 us
  transfers between devices with their start and end apart: 115, of which 60 were waited for; matrix products, arithmetic and copies ran while one was open for 10% of the time, Pallas kernels for 35%

profile of v2, /device:TPU:0, one launch (start us, length us, event | category | flops | bytes accessed | tf_op | source)
XLA Modules:
  0.0 1036.1 jit_solution(8716433811079925825)
XLA Ops:
  39.1 6.9 collective-permute-done.1.refs_1_
  48.8 30.0 %collective-permute-done.2.refs_2_ = bf16[96,3072]{1,0:T(8,128)(2,1)S(1)} collective-permute-done((bf16[96,3072]{1,0:T(8,128)(2,1)S(1)}, bf16[96,3072]{1,0:T(8,128)(2,1)S(1)}, u32[]{:S(2)}, u32[]{:S(2)}) %collective-permute-start.2) | collective-permute-done | bytes 589856 | tf_op jit(solution)/shard_map/ppermute | solution.py:27
  89.8 10.7 %collective-permute-start.15 = (bf16[4,1,144,1536]{3,2,1,0:T(8,128)(2,1)}, bf16[4,1,144,1536]{3,2,1,0:T(8,128)(2,1)}, u32[]{:S(2)}, u32[]{:S(2)}) collective-permute-start(bf16[4,1,144,1536]{3,2,1,0:T(8,128)(2,1)} %get-tuple-element.450.refs_0_), channel_id=1, source_target_pairs={{0,2},{2,3},{3,1},{1,0},{4,6},{6,7},{7,5},{5,4},{8,10},{10,11},{11... | collective-permute-start | bytes 5308424 | tf_op jit(solution)/shard_map/ppermute | solution.py:902
  105.2 19.0 %collective-permute-done.12.refs_1_ = bf16[384,1152]{1,0:T(8,128)(2,1)S(1)} collective-permute-done((bf16[384,1152]{1,0:T(8,128)(2,1)S(1)}, bf16[384,1152]{1,0:T(8,128)(2,1)S(1)}, u32[]{:S(2)}, u32[]{:S(2)}) %collective-permute-start.12) | collective-permute-done | bytes 884768 | tf_op jit(solution)/shard_map/ppermute | solution.py:27
  124.2 15.2 %collective-permute-done.13.refs_2_ = bf16[384,1152]{1,0:T(8,128)(2,1)S(1)} collective-permute-done((bf16[384,1152]{1,0:T(8,128)(2,1)S(1)}, bf16[384,1152]{1,0:T(8,128)(2,1)S(1)}, u32[]{:S(2)}, u32[]{:S(2)}) %collective-permute-start.13) | collective-permute-done | bytes 884768 | tf_op jit(solution)/shard_map/ppermute | solution.py:27
  156.8 6.9 enter.2
  170.1 6.7 collective-permute-done.21
  184.9 12.0 %attend.2.attended_ref = bf16[256,1536]{1,0:T(8,128)(2,1)} custom-call(s32[8]{0:T(128)} %select_n.165.ids_ref, bf16[256,2304]{1,0:T(8,128)(2,1)} %get-tuple-element.424.query_ref, bf16[1024,512]{1,0:T(8,128)(2,1)} %pad_maximum_fusion.5.key_ref.value_ref, bf16[1024,512]{1,0:T(8,128)(2,1)} %pad_maximum_fusion.5.key_ref.value_ref), custom_call_target="tpu_custom_call" | custom-call | flops 1000000000 | bytes 3000000 | tf_op jit(solution)/shard_map/attend/pallas_call | solution.py:100
  206.6 6.0 leave.2
  216.8 24.9 %collective-permute-done.25.refs_1_ = bf16[256,1536]{1,0:T(8,128)(2,1)S(1)} collective-permute-done((bf16[256,1536]{1,0:T(8,128)(2,1)}, bf16[256,1536]{1,0:T(8,128)(2,1)S(1)}, u32[]{:S(2)}, u32[]{:S(2)}) %collective-permute-start.25) | collective-permute-done | bytes 786464 | tf_op jit(solution)/shard_map/ppermute | solution.py:27
  243.5 7.2 order.2
  259.4 12.1 %expert.8 = (bf16[256,1536]{1,0:T(8,128)(2,1)}, bf16[256,1536]{1,0:T(8,128)(2,1)}, bf16[256,1536]{1,0:T(8,128)(2,1)}, bf16[480,1536]{1,0:T(8,128)(2,1)}, f32[480,768]{1,0:T(8,128)}, /*index=5*/f32[480,768]{1,0:T(8,128)}) custom-call(bf16[3,160,256]{2,1,0:T(8,128)(2,1)} %get-tuple-element.941.pick_ref, f32[3,160,1]{2,1,0:T(8,128)} %copy.330.share_ref, ...), custom_call_target="tpu_custom_call" | custom-call | flops 3000000000 | bytes 9000000 | tf_op jit(solution)/shard_map/expert/pallas_call | solution.py:262
  276.9 13.0 %expert.9 = (bf16[256,1536]{1,0:T(8,128)(2,1)}, bf16[256,1536]{1,0:T(8,128)(2,1)}, bf16[256,1536]{1,0:T(8,128)(2,1)}, bf16[480,1536]{1,0:T(8,128)(2,1)}, f32[480,768]{1,0:T(8,128)}, /*index=5*/f32[480,768]{1,0:T(8,128)}) custom-call(bf16[3,160,256]{2,1,0:T(8,128)(2,1)} %get-tuple-element.942.pick_ref, f32[3,160,1]{2,1,0:T(8,128)} %copy.331.share_ref, ...), custom_call_target="tpu_custom_call" | custom-call | flops 3000000000 | bytes 9000000 | tf_op jit(solution)/shard_map/expert/pallas_call | solution.py:262
  295.1 6.6 expert.10
  301.7 7.2 expert.11
  317.1 18.9 %collective-permute-done.39.refs_4_ = bf16[256,1536]{1,0:T(8,128)(2,1)S(1)} collective-permute-done((bf16[256,1536]{1,0:T(8,128)(2,1)S(1)}, bf16[256,1536]{1,0:T(8,128)(2,1)S(1)}, u32[]{:S(2)}, u32[]{:S(2)}) %collective-permute-start.39) | collective-permute-done | bytes 786464 | tf_op jit(solution)/shard_map/ppermute | solution.py:27
  340.5 8.4 enter.3
  351.5 6.0 collective-permute-done.42.refs_1_
  363.5 6.7 collective-permute-done.45
  376.5 12.0 %attend.3.attended_ref = bf16[256,1536]{1,0:T(8,128)(2,1)} custom-call(s32[8]{0:T(128)} %select_n.165.ids_ref, bf16[256,2304]{1,0:T(8,128)(2,1)} %get-tuple-element.497.query_ref, bf16[1024,512]{1,0:T(8,128)(2,1)} %pad_maximum_fusion.6.key_ref.value_ref, bf16[1024,512]{1,0:T(8,128)(2,1)} %pad_maximum_fusion.6.key_ref.value_ref), custom_call_target="tpu_custom_call" | custom-call | flops 1000000000 | bytes 3000000 | tf_op jit(solution)/shard_map/attend/pallas_call | solution.py:100
  391.4 6.3 collective-permute-done.47.refs_2_
  406.1 6.0 leave.3
  414.2 17.6 %collective-permute-done.49.refs_1_ = bf16[256,1536]{1,0:T(8,128)(2,1)S(1)} collective-permute-done((bf16[256,1536]{1,0:T(8,128)(2,1)}, bf16[256,1536]{1,0:T(8,128)(2,1)S(1)}, u32[]{:S(2)}, u32[]{:S(2)}) %collective-permute-start.49) | collective-permute-done | bytes 786464 | tf_op jit(solution)/shard_map/ppermute | solution.py:27
  432.4 11.0 %collective-permute-done.51.refs_3_ = bf16[4,1,144,1536]{3,2,1,0:T(8,128)(2,1)} collective-permute-done((bf16[4,1,144,1536]{3,2,1,0:T(8,128)(2,1)}, bf16[4,1,144,1536]{3,2,1,0:T(8,128)(2,1)}, u32[]{:S(2)}, u32[]{:S(2)}) %collective-permute-start.51) | collective-permute-done | bytes 1769504 | tf_op jit(solution)/shard_map/ppermute | solution.py:902
  443.4 7.0 order.3
  453.9 12.1 %expert.12 = (bf16[256,1536]{1,0:T(8,128)(2,1)}, bf16[256,1536]{1,0:T(8,128)(2,1)}, bf16[256,1536]{1,0:T(8,128)(2,1)}, bf16[480,1536]{1,0:T(8,128)(2,1)}, f32[480,768]{1,0:T(8,128)}, /*index=5*/f32[480,768]{1,0:T(8,128)}) custom-call(bf16[3,160,256]{2,1,0:T(8,128)(2,1)} %get-tuple-element.939.pick_ref, f32[3,160,1]{2,1,0:T(8,128)} %copy.336.share_ref, ...), custom_call_target="tpu_custom_call" | custom-call | flops 3000000000 | bytes 9000000 | tf_op jit(solution)/shard_map/expert/pallas_call | solution.py:262
  466.0 12.8 %expert.13 = (bf16[256,1536]{1,0:T(8,128)(2,1)}, bf16[256,1536]{1,0:T(8,128)(2,1)}, bf16[256,1536]{1,0:T(8,128)(2,1)}, bf16[480,1536]{1,0:T(8,128)(2,1)}, f32[480,768]{1,0:T(8,128)}, /*index=5*/f32[480,768]{1,0:T(8,128)}) custom-call(bf16[3,160,256]{2,1,0:T(8,128)(2,1)} %get-tuple-element.940.pick_ref, f32[3,160,1]{2,1,0:T(8,128)} %copy.337.share_ref, ...), custom_call_target="tpu_custom_call" | custom-call | flops 3000000000 | bytes 9000000 | tf_op jit(solution)/shard_map/expert/pallas_call | solution.py:262
  482.3 6.6 expert.14
  488.9 9.6 collective-permute-done.54.refs_1_
  500.4 7.2 expert.15
  507.6 13.3 %expert_back.8 = (bf16[256,1536]{1,0:T(8,128)(2,1)}, bf16[256,1536]{1,0:T(8,128)(2,1)}, bf16[256,1536]{1,0:T(8,128)(2,1)}, bf16[480,1536]{1,0:T(8,128)(2,1)}, bf...) custom-call(bf16[3,160,256]{2,1,0:T(8,128)(2,1)} %get-tuple-element.939.pick_ref, ...), custom_call_target="tpu_custom_call" | custom-call | flops 4000000000 | bytes 12000000 | tf_op jit(solution)/shard_map/expert_back/pallas_call | solution.py:322
  520.9 14.0 %expert_back.9 = (bf16[256,1536]{1,0:T(8,128)(2,1)}, bf16[256,1536]{1,0:T(8,128)(2,1)}, bf16[256,1536]{1,0:T(8,128)(2,1)}, bf16[480,1536]{1,0:T(8,128)(2,1)}, bf...) custom-call(bf16[3,160,256]{2,1,0:T(8,128)(2,1)} %get-tuple-element.940.pick_ref, ...), custom_call_target="tpu_custom_call" | custom-call | flops 4000000000 | bytes 12000000 | tf_op jit(solution)/shard_map/expert_back/pallas_call | solution.py:322
  536.9 7.5 expert_back.10
  544.5 8.0 expert_back.11
  558.7 13.6 %expert_grads.4 = bf16[16,144,1536]{2,1,0:T(8,128)(2,1)} custom-call(bf16[480,1536]{1,0:T(8,128)(2,1)} %get-tuple-element.588.refs_0_, bf16[160,1536]{1,0:T(8,128)(2,1)} %get-tuple-element.589.refs_1_, bf16[480,1536]{1,0:T(8,128)(2,1)} %get-tuple-element.590.refs_2_, bf16[160,1536]{1,0:T(8,128)(2,1)} %get-tuple-element.591.refs_3_, ...), custom_call_target="tpu_custom_call" | custom-call | flops 1000000000 | bytes 3000000 | tf_op jit(solution)/shard_map/expert_grads/pallas_call | solution.py:388
  572.3 13.8 %expert_grads.5 = bf16[16,144,1536]{2,1,0:T(8,128)(2,1)} custom-call(bf16[480,1536]{1,0:T(8,128)(2,1)} %get-tuple-element.598.refs_0_, bf16[160,1536]{1,0:T(8,128)(2,1)} %get-tuple-element.599.refs_1_, bf16[480,1536]{1,0:T(8,128)(2,1)} %get-tuple-element.600.refs_2_, bf16[160,1536]{1,0:T(8,128)(2,1)} %get-tuple-element.601.refs_3_, ...), custom_call_target="tpu_custom_call" | custom-call | flops 1000000000 | bytes 3000000 | tf_op jit(solution)/shard_map/expert_grads/pallas_call | solution.py:388
  590.3 11.3 %leave_back.2 = (f32[256,1536]{1,0:T(8,128)}, bf16[256,1536]{1,0:T(8,128)(2,1)}, bf16[256,1536]{1,0:T(8,128)(2,1)}, bf16[1536,768]{1,0:T(8,128)(2,1)}, bf16[1536,768]{1,0:T(8,128)(2,1)}) custom-call(s32[1]{0:T(128)} %bitcast.48.core_ref, f32[1,1536]{1,0:T(1,128)} %copy.344.gain_ref, f32[256,1536]{1,0:T(8,128)} %get-tuple-element.510.mid_ref, ...), custom_call_target="tpu_custom_call" | custom-call | flops 8000000000 | bytes 24000000 | tf_op jit(solution)/shard_map/leave_back/pallas_call | solution.py:439
  610.5 16.6 %attend_back.2 = (bf16[256,1536]{1,0:T(8,128)(2,1)}, bf16[256,512]{1,0:T(8,128)(2,1)}, bf16[256,512]{1,0:T(8,128)(2,1)}, bf16[256,512]{1,0:T(8,128)(2,1)}, bf16[256,512]{1,0:T(8,128)(2,1)}) custom-call(s32[8]{0:T(128)} %select_n.165.ids_ref, bf16[256,2304]{1,0:T(8,128)(2,1)} %get-tuple-element.497.query_ref, ...), custom_call_target="tpu_custom_call" | custom-call | flops 1000000000 | bytes 3000000 | tf_op jit(solution)/shard_map/attend_back/pallas_call | solution.py:150
  648.2 13.7 %enter_back.2 = (f32[256,1536]{1,0:T(8,128)}, bf16[256,1536]{1,0:T(8,128)(2,1)}, bf16[1536,1152]{1,0:T(8,128)(2,1)}, bf16[1536,1152]{1,0:T(8,128)(2,1)}) custom-call(s32[1]{0:T(128)} %bitcast.48.core_ref, f32[1,1536]{1,0:T(1,128)} %copy.347.gain_ref, bf16[256,1536]{1,0:T(8,128)(2,1)} %get-tuple-element.696.rows_ref, ...), custom_call_target="tpu_custom_call" | custom-call | flops 1000000000 | bytes 3000000 | tf_op jit(solution)/shard_map/enter_back/pallas_call | solution.py:439
  661.9 6.2 collective-permute-done.70
  670.3 4.8 fusion.5
  675.7 12.6 %collective-permute-done.72.refs_1_ = bf16[256,1536]{1,0:T(8,128)(2,1)S(1)} collective-permute-done((bf16[256,1536]{1,0:T(8,128)(2,1)}, bf16[256,1536]{1,0:T(8,128)(2,1)S(1)}, u32[]{:S(2)}, u32[]{:S(2)}) %collective-permute-start.72) | collective-permute-done | bytes 786464 | tf_op jit(solution)/shard_map/ppermute | solution.py:27
  695.8 13.7 %expert_back.12 = (bf16[256,1536]{1,0:T(8,128)(2,1)}, bf16[256,1536]{1,0:T(8,128)(2,1)}, bf16[256,1536]{1,0:T(8,128)(2,1)}, bf16[480,1536]{1,0:T(8,128)(2,1)}, b...) custom-call(bf16[3,160,256]{2,1,0:T(8,128)(2,1)} %get-tuple-element.941.pick_ref, ...), custom_call_target="tpu_custom_call" | custom-call | flops 4000000000 | bytes 12000000 | tf_op jit(solution)/shard_map/expert_back/pallas_call | solution.py:322
  709.5 14.0 %expert_back.13 = (bf16[256,1536]{1,0:T(8,128)(2,1)}, bf16[256,1536]{1,0:T(8,128)(2,1)}, bf16[256,1536]{1,0:T(8,128)(2,1)}, bf16[480,1536]{1,0:T(8,128)(2,1)}, b...) custom-call(bf16[3,160,256]{2,1,0:T(8,128)(2,1)} %get-tuple-element.942.pick_ref, ...), custom_call_target="tpu_custom_call" | custom-call | flops 4000000000 | bytes 12000000 | tf_op jit(solution)/shard_map/expert_back/pallas_call | solution.py:322
  723.5 7.5 collective-permute-done.75.refs_0_
  747.6 7.6 expert_back.14
  755.2 7.8 expert_back.15
  763.1 15.3 %collective-permute-done.80.refs_2_ = bf16[256,1536]{1,0:T(8,128)(2,1)} collective-permute-done((bf16[256,1536]{1,0:T(8,128)(2,1)}, bf16[256,1536]{1,0:T(8,128)(2,1)}, u32[]{:S(2)}, u32[]{:S(2)}) %collective-permute-start.80) | collective-permute-done | bytes 786464 | tf_op jit(solution)/shard_map/ppermute | solution.py:27
  786.1 13.6 %expert_grads.6 = bf16[16,144,1536]{2,1,0:T(8,128)(2,1)} custom-call(bf16[480,1536]{1,0:T(8,128)(2,1)} %get-tuple-element.706.refs_0_, bf16[160,1536]{1,0:T(8,128)(2,1)} %get-tuple-element.707.refs_1_, bf16[480,1536]{1,0:T(8,128)(2,1)} %get-tuple-element.708.refs_2_, bf16[160,1536]{1,0:T(8,128)(2,1)} %get-tuple-element.709.refs_3_, ...), custom_call_target="tpu_custom_call" | custom-call | flops 1000000000 | bytes 3000000 | tf_op jit(solution)/shard_map/expert_grads/pallas_call | solution.py:388
  799.7 13.9 %expert_grads.7 = bf16[16,144,1536]{2,1,0:T(8,128)(2,1)} custom-call(bf16[480,1536]{1,0:T(8,128)(2,1)} %get-tuple-element.716.refs_0_, bf16[160,1536]{1,0:T(8,128)(2,1)} %get-tuple-element.717.refs_1_, bf16[480,1536]{1,0:T(8,128)(2,1)} %get-tuple-element.718.refs_2_, bf16[160,1536]{1,0:T(8,128)(2,1)} %get-tuple-element.719.refs_3_, ...), custom_call_target="tpu_custom_call" | custom-call | flops 1000000000 | bytes 3000000 | tf_op jit(solution)/shard_map/expert_grads/pallas_call | solution.py:388
  815.0 11.3 %leave_back.3 = (f32[256,1536]{1,0:T(8,128)}, bf16[256,1536]{1,0:T(8,128)(2,1)}, bf16[256,1536]{1,0:T(8,128)(2,1)}, bf16[1536,768]{1,0:T(8,128)(2,1)}, bf16[1536,768]{1,0:T(8,128)(2,1)}) custom-call(s32[1]{0:T(128)} %bitcast.48.core_ref, f32[1,1536]{1,0:T(1,128)} %copy.329.gain_ref, f32[256,1536]{1,0:T(8,128)} %get-tuple-element.482.refs_0_.mid_ref, ...), custom_call_target="tpu_custom_call" | custom-call | flops 8000000000 | bytes 24000000 | tf_op jit(solution)/shard_map/leave_back/pallas_call | solution.py:439
  831.0 16.6 %attend_back.3 = (bf16[256,1536]{1,0:T(8,128)(2,1)}, bf16[256,512]{1,0:T(8,128)(2,1)}, bf16[256,512]{1,0:T(8,128)(2,1)}, bf16[256,512]{1,0:T(8,128)(2,1)}, bf16[256,512]{1,0:T(8,128)(2,1)}) custom-call(s32[8]{0:T(128)} %select_n.165.ids_ref, bf16[256,2304]{1,0:T(8,128)(2,1)} %get-tuple-element.424.query_ref, ...), custom_call_target="tpu_custom_call" | custom-call | flops 1000000000 | bytes 3000000 | tf_op jit(solution)/shard_map/attend_back/pallas_call | solution.py:150
  851.2 5.9 collective-permute-done.89.refs_1_
  857.1 5.3 collective-permute-done.90.refs_2_
  868.1 5.1 fusion.3
  873.1 13.6 %enter_back.3 = (f32[256,1536]{1,0:T(8,128)}, bf16[256,1536]{1,0:T(8,128)(2,1)}, bf16[1536,1152]{1,0:T(8,128)(2,1)}, bf16[1536,1152]{1,0:T(8,128)(2,1)}) custom-call(s32[1]{0:T(128)} %bitcast.48.core_ref, f32[1,1536]{1,0:T(1,128)} %copy.328.gain_ref, bf16[256,1536]{1,0:T(8,128)(2,1)} %get-tuple-element.421.refs_0_.rows_ref, ...), custom_call_target="tpu_custom_call" | custom-call | flops 1000000000 | bytes 3000000 | tf_op jit(solution)/shard_map/enter_back/pallas_call | solution.py:439
  897.0 10.5 %collective-permute-done.99 = bf16[1,144,1536]{2,1,0:T(8,128)(2,1)S(1)} collective-permute-done((bf16[1,144,1536]{2,1,0:T(8,128)(2,1)S(1)}, bf16[1,144,1536]{2,1,0:T(8,128)(2,1)S(1)}, u32[]{:S(2)}, u32[]{:S(2)}) %collective-permute-start.99) | collective-permute-done | bytes 442400 | tf_op jit(solution)/shard_map/ppermute | solution.py:27
  907.5 8.6 collective-permute-done.98
  925.3 6.4 collective-permute-done.108
  938.5 34.2 %collective-permute-done.103 = bf16[384,768]{1,0:T(8,128)(2,1)S(1)} collective-permute-done((bf16[384,768]{1,0:T(8,128)(2,1)S(1)}, bf16[384,768]{1,0:T(8,128)(2,1)S(1)}, u32[]{:S(2)}, u32[]{:S(2)}) %collective-permute-start.103) | collective-permute-done | bytes 589856 | tf_op jit(solution)/shard_map/ppermute | solution.py:27
  984.7 8.7 collective-permute-done.112
  995.9 5.3 collective-permute-done.111
  1004.0 13.5 %collective-permute-done.106 = bf16[96,1920]{1,0:T(8,128)(2,1)S(1)} collective-permute-done((bf16[96,1920]{1,0:T(8,128)(2,1)S(1)}, bf16[96,1920]{1,0:T(8,128)(2,1)S(1)}, u32[]{:S(2)}, u32[]{:S(2)}) %collective-permute-start.106) | collective-permute-done | bytes 368672 | tf_op jit(solution)/shard_map/ppermute | solution.py:27
  1026.9 8.7 finish.1
  (477 shorter events, 318.7 us)
Async XLA Ops:
  7.8 20.6 %collective-permute-start.4 = (bf16[4,1,144,1536]{3,2,0,1:T(8,128)(2,1)}, bf16[4,1,144,1536]{3,2,0,1:T(8,128)(2,1)}, u32[]{:S(2)}, u32[]{:S(2)}) collective-permute-start(bf16[4,1,144,1536]{3,2,0,1:T(8,128)(2,1)} %dynamic-slice_bitcast_fusion), channel_id=1, source_target_pairs={{0,16},{16,0},{1,17},{17,1},{2,18},{18,2},{3,19},{19,3},{4,20},{20... | collective-permute-start | bytes 5308424 | tf_op jit(solution)/shard_map/ppermute | solution.py:27
  33.0 51.0 %collective-permute-start.5 = (bf16[2,1,144,1536]{3,2,1,0:T(8,128)(2,1)S(1)}, bf16[2,1,144,1536]{3,2,1,0:T(8,128)(2,1)S(1)}, u32[]{:S(2)}, u32[]{:S(2)}) collective-permute-start(bf16[2,1,144,1536]{3,2,1,0:T(8,128)(2,1)S(1)} %get-tuple-element.912), channel_id=1, source_target_pairs={{0,4},{4,0},{8,12},{12,8},{1,5},{5,1},{9,13},{13,9},{2,6},{6,2},{1... | collective-permute-start | bytes 2654216 | tf_op jit(solution)/shard_map/ppermute | solution.py:27
  33.5 50.4 %collective-permute-start.6 = (bf16[2,1,144,1536]{3,2,1,0:T(8,128)(2,1)S(1)}, bf16[2,1,144,1536]{3,2,1,0:T(8,128)(2,1)S(1)}, u32[]{:S(2)}, u32[]{:S(2)}) collective-permute-start(bf16[2,1,144,1536]{3,2,1,0:T(8,128)(2,1)S(1)} %get-tuple-element.913), channel_id=1, source_target_pairs={{0,8},{4,12},{8,0},{12,4},{1,9},{5,13},{9,1},{13,5},{2,10},{6,14},... | collective-permute-start | bytes 2654216 | tf_op jit(solution)/shard_map/ppermute | solution.py:27
  35.0 48.9 %collective-permute-start.7 = (bf16[2,1,144,1536]{3,2,1,0:T(8,128)(2,1)S(1)}, bf16[2,1,144,1536]{3,2,1,0:T(8,128)(2,1)S(1)}, u32[]{:S(2)}, u32[]{:S(2)}) collective-permute-start(bf16[2,1,144,1536]{3,2,1,0:T(8,128)(2,1)S(1)} %get-tuple-element.910), channel_id=1, source_target_pairs={{0,12},{4,8},{8,4},{12,0},{1,13},{5,9},{9,5},{13,1},{2,14},{6,10},... | collective-permute-start | bytes 2654216 | tf_op jit(solution)/shard_map/ppermute | solution.py:27
  36.5 42.3 %collective-permute-start.2 = (bf16[96,3072]{1,0:T(8,128)(2,1)S(1)}, bf16[96,3072]{1,0:T(8,128)(2,1)S(1)}, u32[]{:S(2)}, u32[]{:S(2)}) collective-permute-start(bf16[96,3072]{1,0:T(8,128)(2,1)S(1)} %pad_maximum_fusion.8.refs_0_), channel_id=1, source_target_pairs={{0,2},{1,3},{2,0},{3,1},{4,6},{5,7},{6,4},{7,5},{8,10},{9,11},{10,... | collective-permute-start | bytes 1769480 | tf_op jit(solution)/shard_map/ppermute | solution.py:27
  46.0 32.7 %collective-permute-start.3 = (bf16[96,3072]{1,0:T(8,128)(2,1)S(1)}, bf16[96,3072]{1,0:T(8,128)(2,1)S(1)}, u32[]{:S(2)}, u32[]{:S(2)}) collective-permute-start(bf16[96,3072]{1,0:T(8,128)(2,1)S(1)} %pad_maximum_fusion.8.refs_0_), channel_id=1, source_target_pairs={{0,3},{1,2},{2,1},{3,0},{4,7},{5,6},{6,5},{7,4},{8,11},{9,10},{10,... | collective-permute-start | bytes 1769480 | tf_op jit(solution)/shard_map/ppermute | solution.py:27
  89.8 51.8 %collective-permute-start.15 = (bf16[4,1,144,1536]{3,2,1,0:T(8,128)(2,1)}, bf16[4,1,144,1536]{3,2,1,0:T(8,128)(2,1)}, u32[]{:S(2)}, u32[]{:S(2)}) collective-permute-start(bf16[4,1,144,1536]{3,2,1,0:T(8,128)(2,1)} %get-tuple-element.450.refs_0_), channel_id=1, source_target_pairs={{0,2},{2,3},{3,1},{1,0},{4,6},{6,7},{7,5},{5,4},{8,10},{10,11},{11... | collective-permute-start | bytes 5308424 | tf_op jit(solution)/shard_map/ppermute | solution.py:902
  101.6 22.6 %collective-permute-start.12 = (bf16[384,1152]{1,0:T(8,128)(2,1)S(1)}, bf16[384,1152]{1,0:T(8,128)(2,1)S(1)}, u32[]{:S(2)}, u32[]{:S(2)}) collective-permute-start(bf16[384,1152]{1,0:T(8,128)(2,1)S(1)} %get-tuple-element.417.refs_0_), channel_id=1, source_target_pairs={{0,4},{4,0},{8,12},{12,8},{1,5},{5,1},{9,13},{13,9},{2,6},{6,2},{1... | collective-permute-start | bytes 2654216 | tf_op jit(solution)/shard_map/ppermute | solution.py:27
  102.4 37.0 %collective-permute-start.13 = (bf16[384,1152]{1,0:T(8,128)(2,1)S(1)}, bf16[384,1152]{1,0:T(8,128)(2,1)S(1)}, u32[]{:S(2)}, u32[]{:S(2)}) collective-permute-start(bf16[384,1152]{1,0:T(8,128)(2,1)S(1)} %get-tuple-element.417.refs_0_), channel_id=1, source_target_pairs={{0,8},{4,12},{8,0},{12,4},{1,9},{5,13},{9,1},{13,5},{2,10},{6,14},... | collective-permute-start | bytes 2654216 | tf_op jit(solution)/shard_map/ppermute | solution.py:27
  104.0 36.7 %collective-permute-start.14 = (bf16[384,1152]{1,0:T(8,128)(2,1)S(1)}, bf16[384,1152]{1,0:T(8,128)(2,1)S(1)}, u32[]{:S(2)}, u32[]{:S(2)}) collective-permute-start(bf16[384,1152]{1,0:T(8,128)(2,1)S(1)} %get-tuple-element.417.refs_0_), channel_id=1, source_target_pairs={{0,12},{4,8},{8,4},{12,0},{1,13},{5,9},{9,5},{13,1},{2,14},{6,10},... | collective-permute-start | bytes 2654216 | tf_op jit(solution)/shard_map/ppermute | solution.py:27
  151.7 45.2 %collective-permute-start.23 = (bf16[4,1,144,1536]{3,2,1,0:T(8,128)(2,1)}, bf16[4,1,144,1536]{3,2,1,0:T(8,128)(2,1)}, u32[]{:S(2)}, u32[]{:S(2)}) collective-permute-start(bf16[4,1,144,1536]{3,2,1,0:T(8,128)(2,1)} %collective-permute-done.15.refs_1_), channel_id=1, source_target_pairs={{0,2},{2,3},{3,1},{1,0},{4,6},{6,7},{7,5},{5,4},{8,10},{10,11},{11... | collective-permute-start | bytes 5308424 | tf_op jit(solution)/shard_map/ppermute | solution.py:902
  201.7 41.3 %collective-permute-start.27 = (bf16[4,1,144,1536]{3,2,1,0:T(8,128)(2,1)}, bf16[4,1,144,1536]{3,2,1,0:T(8,128)(2,1)}, u32[]{:S(2)}, u32[]{:S(2)}) collective-permute-start(bf16[4,1,144,1536]{3,2,1,0:T(8,128)(2,1)} %collective-permute-done.23.refs_2_), channel_id=1, source_target_pairs={{0,2},{2,3},{3,1},{1,0},{4,6},{6,7},{7,5},{5,4},{8,10},{10,11},{11... | collective-permute-start | bytes 5308424 | tf_op jit(solution)/shard_map/ppermute | solution.py:902
  202.8 39.8 %collective-permute-start.28 = (bf16[384,1152]{1,0:T(8,128)(2,1)}, bf16[384,1152]{1,0:T(8,128)(2,1)S(1)}, u32[]{:S(2)}, u32[]{:S(2)}) collective-permute-start(bf16[384,1152]{1,0:T(8,128)(2,1)} %get-tuple-element.478.refs_0_), channel_id=1, source_target_pairs={{0,4},{4,0},{8,12},{12,8},{1,5},{5,1},{9,13},{13,9},{2,6},{6,2},{1... | collective-permute-start | bytes 2654216 | tf_op jit(solution)/shard_map/ppermute | solution.py:27
  204.1 38.6 %collective-permute-start.29 = (bf16[384,1152]{1,0:T(8,128)(2,1)}, bf16[384,1152]{1,0:T(8,128)(2,1)S(1)}, u32[]{:S(2)}, u32[]{:S(2)}) collective-permute-start(bf16[384,1152]{1,0:T(8,128)(2,1)} %get-tuple-element.478.refs_0_), channel_id=1, source_target_pairs={{0,8},{4,12},{8,0},{12,4},{1,9},{5,13},{9,1},{13,5},{2,10},{6,14},... | collective-permute-start | bytes 2654216 | tf_op jit(solution)/shard_map/ppermute | solution.py:27
  212.6 29.1 %collective-permute-start.25 = (bf16[256,1536]{1,0:T(8,128)(2,1)}, bf16[256,1536]{1,0:T(8,128)(2,1)S(1)}, u32[]{:S(2)}, u32[]{:S(2)}) collective-permute-start(bf16[256,1536]{1,0:T(8,128)(2,1)} %get-tuple-element.454.refs_0_), channel_id=1, source_target_pairs={{0,4},{4,0},{8,12},{12,8},{1,5},{5,1},{9,13},{13,9},{2,6},{6,2},{1... | collective-permute-start | bytes 2359304 | tf_op jit(solution)/shard_map/ppermute | solution.py:27
  213.8 28.8 %collective-permute-start.26 = (bf16[256,1536]{1,0:T(8,128)(2,1)}, bf16[256,1536]{1,0:T(8,128)(2,1)S(1)}, u32[]{:S(2)}, u32[]{:S(2)}) collective-permute-start(bf16[256,1536]{1,0:T(8,128)(2,1)} %get-tuple-element.454.refs_0_), channel_id=1, source_target_pairs={{0,8},{4,12},{8,0},{12,4},{1,9},{5,13},{9,1},{13,5},{2,10},{6,14},... | collective-permute-start | bytes 2359304 | tf_op jit(solution)/shard_map/ppermute | solution.py:27
  250.7 26.1 %collective-permute-start.30 = (bf16[16,144,1536]{2,1,0:T(8,128)(2,1)}, bf16[16,144,1536]{2,1,0:T(8,128)(2,1)}, u32[]{:S(2)}, u32[]{:S(2)}) collective-permute-start(bf16[16,144,1536]{2,1,0:T(8,128)(2,1)} %bitcast.277), channel_id=1, source_target_pairs={{0,16},{16,0},{1,17},{17,1},{2,18},{18,2},{3,19},{19,3},{4,20},{20... | collective-permute-start | bytes 21233672 | tf_op jit(solution)/shard_map/ppermute | solution.py:27
  252.5 37.4 %collective-permute-start.31 = (bf16[256,1536]{1,0:T(8,128)(2,1)S(1)}, bf16[256,1536]{1,0:T(8,128)(2,1)S(1)}, u32[]{:S(2)}, u32[]{:S(2)}) collective-permute-start(bf16[256,1536]{1,0:T(8,128)(2,1)S(1)} %copy-done.15), channel_id=1, source_target_pairs={{0,12},{4,8},{8,4},{12,0},{1,13},{5,9},{9,5},{13,1},{2,14},{6,10},... | collective-permute-start | bytes 2359304 | tf_op jit(solution)/shard_map/ppermute | solution.py:27
  271.5 37.4 %collective-permute-start.37 = (bf16[384,1152]{1,0:T(8,128)(2,1)}, bf16[384,1152]{1,0:T(8,128)(2,1)}, u32[]{:S(2)}, u32[]{:S(2)}) collective-permute-start(bf16[384,1152]{1,0:T(8,128)(2,1)} %get-tuple-element.478.refs_0_), channel_id=1, source_target_pairs={{0,12},{4,8},{8,4},{12,0},{1,13},{5,9},{9,5},{13,1},{2,14},{6,10},... | collective-permute-start | bytes 2654216 | tf_op jit(solution)/shard_map/ppermute | solution.py:27
  315.1 22.8 %collective-permute-start.38 = (bf16[1536,1152]{1,0:T(8,128)(2,1)}, bf16[1536,1152]{1,0:T(8,128)(2,1)S(1)}, u32[]{:S(2)}, u32[]{:S(2)}) collective-permute-start(bf16[1536,1152]{1,0:T(8,128)(2,1)} %place.10.refs_5_.refs_4_), channel_id=1, source_target_pairs={{0,16},{16,0},{1,17},{17,1},{2,18},{18,2},{3,19},{19,3},{4,20},{20... | collective-permute-start | bytes 10616840 | tf_op jit(solution)/shard_map/ppermute | solution.py:27
  315.1 20.9 %collective-permute-start.39 = (bf16[256,1536]{1,0:T(8,128)(2,1)S(1)}, bf16[256,1536]{1,0:T(8,128)(2,1)S(1)}, u32[]{:S(2)}, u32[]{:S(2)}) collective-permute-start(bf16[256,1536]{1,0:T(8,128)(2,1)S(1)} %copy-done.65), channel_id=1, source_target_pairs={{0,12},{4,8},{8,4},{12,0},{1,13},{5,9},{9,5},{13,1},{2,14},{6,10},... | collective-permute-start | bytes 2359304 | tf_op jit(solution)/shard_map/ppermute | solution.py:27
  316.5 41.0 %collective-permute-start.42 = (bf16[4,1,144,1536]{3,2,1,0:T(8,128)(2,1)}, bf16[4,1,144,1536]{3,2,1,0:T(8,128)(2,1)}, u32[]{:S(2)}, u32[]{:S(2)}) collective-permute-start(bf16[4,1,144,1536]{3,2,1,0:T(8,128)(2,1)} %get-tuple-element.518.refs_0_), channel_id=1, source_target_pairs={{0,2},{2,3},{3,1},{1,0},{4,6},{6,7},{7,5},{5,4},{8,10},{10,11},{11... | collective-permute-start | bytes 5308424 | tf_op jit(solution)/shard_map/ppermute | solution.py:902
  357.5 40.2 %collective-permute-start.47 = (bf16[4,1,144,1536]{3,2,1,0:T(8,128)(2,1)}, bf16[4,1,144,1536]{3,2,1,0:T(8,128)(2,1)}, u32[]{:S(2)}, u32[]{:S(2)}) collective-permute-start(bf16[4,1,144,1536]{3,2,1,0:T(8,128)(2,1)} %collective-permute-done.42.refs_1_), channel_id=1, source_target_pairs={{0,2},{2,3},{3,1},{1,0},{4,6},{6,7},{7,5},{5,4},{8,10},{10,11},{11... | collective-permute-start | bytes 5308424 | tf_op jit(solution)/shard_map/ppermute | solution.py:902
  401.2 42.2 %collective-permute-start.51 = (bf16[4,1,144,1536]{3,2,1,0:T(8,128)(2,1)}, bf16[4,1,144,1536]{3,2,1,0:T(8,128)(2,1)}, u32[]{:S(2)}, u32[]{:S(2)}) collective-permute-start(bf16[4,1,144,1536]{3,2,1,0:T(8,128)(2,1)} %collective-permute-done.47.refs_2_), channel_id=1, source_target_pairs={{0,2},{2,3},{3,1},{1,0},{4,6},{6,7},{7,5},{5,4},{8,10},{10,11},{11... | collective-permute-start | bytes 5308424 | tf_op jit(solution)/shard_map/ppermute | solution.py:902
  450.5 28.4 %collective-permute-start.53 = (bf16[256,1536]{1,0:T(8,128)(2,1)S(1)}, bf16[256,1536]{1,0:T(8,128)(2,1)S(1)}, u32[]{:S(2)}, u32[]{:S(2)}) collective-permute-start(bf16[256,1536]{1,0:T(8,128)(2,1)S(1)} %copy-done.21), channel_id=1, source_target_pairs={{0,12},{4,8},{8,4},{12,0},{1,13},{5,9},{9,5},{13,1},{2,14},{6,10},... | collective-permute-start | bytes 2359304 | tf_op jit(solution)/shard_map/ppermute | solution.py:27
  498.8 36.1 %collective-permute-start.56 = (bf16[256,1536]{1,0:T(8,128)(2,1)S(1)}, bf16[256,1536]{1,0:T(8,128)(2,1)S(1)}, u32[]{:S(2)}, u32[]{:S(2)}) collective-permute-start(bf16[256,1536]{1,0:T(8,128)(2,1)S(1)} %get-tuple-element.543.refs_0_.cot_ref), channel_id=1, source_target_pairs={{0,12},{4,8},{8,4},{12,0},{1,13},{5,9},{9,5},{13,1},{2,14},{6,10},... | collective-permute-start | bytes 2359304 | tf_op jit(solution)/shard_map/ppermute | solution.py:27
  555.2 30.8 %collective-permute-start.59 = (bf16[256,1536]{1,0:T(8,128)(2,1)}, bf16[256,1536]{1,0:T(8,128)(2,1)}, u32[]{:S(2)}, u32[]{:S(2)}) collective-permute-start(bf16[256,1536]{1,0:T(8,128)(2,1)} %get-tuple-element.587), channel_id=1, source_target_pairs={{0,12},{4,8},{8,4},{12,0},{1,13},{5,9},{9,5},{13,1},{2,14},{6,10},... | collective-permute-start | bytes 2359304 | tf_op jit(solution)/shard_map/ppermute | solution.py:27
  556.8 32.9 %collective-permute-start.60 = (bf16[256,1536]{1,0:T(8,128)(2,1)S(1)}, bf16[256,1536]{1,0:T(8,128)(2,1)S(1)}, u32[]{:S(2)}, u32[]{:S(2)}) collective-permute-start(bf16[256,1536]{1,0:T(8,128)(2,1)S(1)} %copy-done.61), channel_id=1, source_target_pairs={{0,4},{4,0},{8,12},{12,8},{1,5},{5,1},{9,13},{13,9},{2,6},{6,2},{1... | collective-permute-start | bytes 2359304 | tf_op jit(solution)/shard_map/ppermute | solution.py:27
  557.5 32.7 %collective-permute-start.61 = (bf16[256,1536]{1,0:T(8,128)(2,1)S(1)}, bf16[256,1536]{1,0:T(8,128)(2,1)}, u32[]{:S(2)}, u32[]{:S(2)}) collective-permute-start(bf16[256,1536]{1,0:T(8,128)(2,1)S(1)} %copy-done.60), channel_id=1, source_target_pairs={{0,8},{4,12},{8,0},{12,4},{1,9},{5,13},{9,1},{13,5},{2,10},{6,14},... | collective-permute-start | bytes 2359304 | tf_op jit(solution)/shard_map/ppermute | solution.py:27
  601.5 27.7 %collective-permute-start.62 = (bf16[1536,768]{1,0:T(8,128)(2,1)}, bf16[1536,768]{1,0:T(8,128)(2,1)}, u32[]{:S(2)}, u32[]{:S(2)}) collective-permute-start(bf16[1536,768]{1,0:T(8,128)(2,1)} %get-tuple-element.624), channel_id=1, source_target_pairs={{0,16},{16,0},{1,17},{17,1},{2,18},{18,2},{3,19},{19,3},{4,20},{20... | collective-permute-start | bytes 7077896 | tf_op jit(solution)/shard_map/ppermute | solution.py:27
  606.5 41.7 %collective-permute-start.68 = (bf16[4,144,1536]{2,1,0:T(8,128)(2,1)}, bf16[4,144,1536]{2,1,0:T(8,128)(2,1)}, u32[]{:S(2)}, u32[]{:S(2)}) collective-permute-start(bf16[4,144,1536]{2,1,0:T(8,128)(2,1)} %fusion.9), channel_id=1, source_target_pairs={{0,2},{2,3},{3,1},{1,0},{4,6},{6,7},{7,5},{5,4},{8,10},{10,11},{11... | collective-permute-start | bytes 5308424 | tf_op jit(solution)/shard_map/ppermute | solution.py:943
  608.9 20.4 %collective-permute-start.63 = (bf16[256,1536]{1,0:T(8,128)(2,1)}, bf16[256,1536]{1,0:T(8,128)(2,1)}, u32[]{:S(2)}, u32[]{:S(2)}) collective-permute-start(bf16[256,1536]{1,0:T(8,128)(2,1)} %get-tuple-element.625), channel_id=1, source_target_pairs={{0,12},{4,8},{8,4},{12,0},{1,13},{5,9},{9,5},{13,1},{2,14},{6,10},... | collective-permute-start | bytes 2359304 | tf_op jit(solution)/shard_map/ppermute | solution.py:27
  637.1 24.8 %collective-permute-start.69 = (bf16[384,768]{1,0:T(8,128)(2,1)}, bf16[384,768]{1,0:T(8,128)(2,1)}, u32[]{:S(2)}, u32[]{:S(2)}) collective-permute-start(bf16[384,768]{1,0:T(8,128)(2,1)} %get-tuple-element.906), channel_id=1, source_target_pairs={{0,4},{4,0},{8,12},{12,8},{1,5},{5,1},{9,13},{13,9},{2,6},{6,2},{1... | collective-permute-start | bytes 1769480 | tf_op jit(solution)/shard_map/ppermute | solution.py:27
  638.7 29.4 %collective-permute-start.70 = (bf16[384,768]{1,0:T(8,128)(2,1)}, bf16[384,768]{1,0:T(8,128)(2,1)}, u32[]{:S(2)}, u32[]{:S(2)}) collective-permute-start(bf16[384,768]{1,0:T(8,128)(2,1)} %get-tuple-element.905), channel_id=1, source_target_pairs={{0,8},{4,12},{8,0},{12,4},{1,9},{5,13},{9,1},{13,5},{2,10},{6,14},... | collective-permute-start | bytes 1769480 | tf_op jit(solution)/shard_map/ppermute | solution.py:27
  641.5 26.6 %collective-permute-start.71 = (bf16[384,768]{1,0:T(8,128)(2,1)}, bf16[384,768]{1,0:T(8,128)(2,1)}, u32[]{:S(2)}, u32[]{:S(2)}) collective-permute-start(bf16[384,768]{1,0:T(8,128)(2,1)} %get-tuple-element.904), channel_id=1, source_target_pairs={{0,12},{4,8},{8,4},{12,0},{1,13},{5,9},{9,5},{13,1},{2,14},{6,10},... | collective-permute-start | bytes 1769480 | tf_op jit(solution)/shard_map/ppermute | solution.py:27
  668.1 21.0 %collective-permute-start.74 = (bf16[1536,1152]{1,0:T(8,128)(2,1)}, bf16[1536,1152]{1,0:T(8,128)(2,1)S(1)}, u32[]{:S(2)}, u32[]{:S(2)}) collective-permute-start(bf16[1536,1152]{1,0:T(8,128)(2,1)} %get-tuple-element.651), channel_id=1, source_target_pairs={{0,16},{16,0},{1,17},{17,1},{2,18},{18,2},{3,19},{19,3},{4,20},{20... | collective-permute-start | bytes 10616840 | tf_op jit(solution)/shard_map/ppermute | solution.py:27
  675.1 55.9 %collective-permute-start.76 = (bf16[4,144,1536]{2,1,0:T(8,128)(2,1)}, bf16[4,144,1536]{2,1,0:T(8,128)(2,1)}, u32[]{:S(2)}, u32[]{:S(2)}) collective-permute-start(bf16[4,144,1536]{2,1,0:T(8,128)(2,1)} %fusion.5), channel_id=1, source_target_pairs={{0,2},{2,3},{3,1},{1,0},{4,6},{6,7},{7,5},{5,4},{8,10},{10,11},{11... | collective-permute-start | bytes 5308424 | tf_op jit(solution)/shard_map/ppermute | solution.py:943
  692.3 38.7 %collective-permute-start.77 = (bf16[384,1152]{1,0:T(8,128)(2,1)}, bf16[384,1152]{1,0:T(8,128)(2,1)}, u32[]{:S(2)}, u32[]{:S(2)}) collective-permute-start(bf16[384,1152]{1,0:T(8,128)(2,1)} %get-tuple-element.897), channel_id=1, source_target_pairs={{0,4},{4,0},{8,12},{12,8},{1,5},{5,1},{9,13},{13,9},{2,6},{6,2},{1... | collective-permute-start | bytes 2654216 | tf_op jit(solution)/shard_map/ppermute | solution.py:27
  693.2 38.0 %collective-permute-start.78 = (bf16[384,1152]{1,0:T(8,128)(2,1)}, bf16[384,1152]{1,0:T(8,128)(2,1)}, u32[]{:S(2)}, u32[]{:S(2)}) collective-permute-start(bf16[384,1152]{1,0:T(8,128)(2,1)} %get-tuple-element.896), channel_id=1, source_target_pairs={{0,8},{4,12},{8,0},{12,4},{1,9},{5,13},{9,1},{13,5},{2,10},{6,14},... | collective-permute-start | bytes 2654216 | tf_op jit(solution)/shard_map/ppermute | solution.py:27
  694.5 36.5 %collective-permute-start.75 = (bf16[256,1536]{1,0:T(8,128)(2,1)}, bf16[256,1536]{1,0:T(8,128)(2,1)S(1)}, u32[]{:S(2)}, u32[]{:S(2)}) collective-permute-start(bf16[256,1536]{1,0:T(8,128)(2,1)} %get-tuple-element.654.refs_0_.cot_ref), channel_id=1, source_target_pairs={{0,12},{4,8},{8,4},{12,0},{1,13},{5,9},{9,5},{13,1},{2,14},{6,10},... | collective-permute-start | bytes 2359304 | tf_op jit(solution)/shard_map/ppermute | solution.py:27
  736.6 41.7 %collective-permute-start.81 = (bf16[4,144,1536]{2,1,0:T(8,128)(2,1)}, bf16[4,144,1536]{2,1,0:T(8,128)(2,1)}, u32[]{:S(2)}, u32[]{:S(2)}) collective-permute-start(bf16[4,144,1536]{2,1,0:T(8,128)(2,1)} %fusion.4), channel_id=1, source_target_pairs={{0,2},{2,3},{3,1},{1,0},{4,6},{6,7},{7,5},{5,4},{8,10},{10,11},{11... | collective-permute-start | bytes 5308424 | tf_op jit(solution)/shard_map/ppermute | solution.py:943
  738.2 24.8 %collective-permute-start.79 = (bf16[256,1536]{1,0:T(8,128)(2,1)}, bf16[256,1536]{1,0:T(8,128)(2,1)}, u32[]{:S(2)}, u32[]{:S(2)}) collective-permute-start(bf16[256,1536]{1,0:T(8,128)(2,1)} %get-tuple-element.675), channel_id=1, source_target_pairs={{0,4},{4,0},{8,12},{12,8},{1,5},{5,1},{9,13},{13,9},{2,6},{6,2},{1... | collective-permute-start | bytes 2359304 | tf_op jit(solution)/shard_map/ppermute | solution.py:27
  739.4 38.9 %collective-permute-start.80 = (bf16[256,1536]{1,0:T(8,128)(2,1)}, bf16[256,1536]{1,0:T(8,128)(2,1)}, u32[]{:S(2)}, u32[]{:S(2)}) collective-permute-start(bf16[256,1536]{1,0:T(8,128)(2,1)} %get-tuple-element.676), channel_id=1, source_target_pairs={{0,8},{4,12},{8,0},{12,4},{1,9},{5,13},{9,1},{13,5},{2,10},{6,14},... | collective-permute-start | bytes 2359304 | tf_op jit(solution)/shard_map/ppermute | solution.py:27
  741.7 36.6 %collective-permute-start.83 = (bf16[384,1152]{1,0:T(8,128)(2,1)S(1)}, bf16[384,1152]{1,0:T(8,128)(2,1)S(1)}, u32[]{:S(2)}, u32[]{:S(2)}) collective-permute-start(bf16[384,1152]{1,0:T(8,128)(2,1)S(1)} %fusion.14), channel_id=1, source_target_pairs={{0,12},{4,8},{8,4},{12,0},{1,13},{5,9},{9,5},{13,1},{2,14},{6,10},... | collective-permute-start | bytes 2654216 | tf_op jit(solution)/shard_map/ppermute | solution.py:27
  780.4 33.2 %collective-permute-start.87 = (bf16[96,1920]{1,0:T(8,128)(2,1)S(1)}, bf16[96,1920]{1,0:T(8,128)(2,1)S(1)}, u32[]{:S(2)}, u32[]{:S(2)}) collective-permute-start(bf16[96,1920]{1,0:T(8,128)(2,1)S(1)} %get-tuple-element.933), channel_id=1, source_target_pairs={{0,3},{1,2},{2,1},{3,0},{4,7},{5,6},{6,5},{7,4},{8,11},{9,10},{10,... | collective-permute-start | bytes 1105928 | tf_op jit(solution)/shard_map/ppermute | solution.py:27
  783.0 31.7 %collective-permute-start.86 = (bf16[96,1920]{1,0:T(8,128)(2,1)S(1)}, bf16[96,1920]{1,0:T(8,128)(2,1)S(1)}, u32[]{:S(2)}, u32[]{:S(2)}) collective-permute-start(bf16[96,1920]{1,0:T(8,128)(2,1)S(1)} %get-tuple-element.934), channel_id=1, source_target_pairs={{0,2},{1,3},{2,0},{3,1},{4,6},{5,7},{6,4},{7,5},{8,10},{9,11},{10,... | collective-permute-start | bytes 1105928 | tf_op jit(solution)/shard_map/ppermute | solution.py:27
  783.3 31.4 %collective-permute-start.85 = (bf16[96,1920]{1,0:T(8,128)(2,1)S(1)}, bf16[96,1920]{1,0:T(8,128)(2,1)S(1)}, u32[]{:S(2)}, u32[]{:S(2)}) collective-permute-start(bf16[96,1920]{1,0:T(8,128)(2,1)S(1)} %get-tuple-element.932), channel_id=1, source_target_pairs={{0,1},{1,0},{2,3},{3,2},{4,5},{5,4},{6,7},{7,6},{8,9},{9,8},{10,11... | collective-permute-start | bytes 1105928 | tf_op jit(solution)/shard_map/ppermute | solution.py:27
  784.8 30.1 %collective-permute-start.84 = (bf16[256,1536]{1,0:T(8,128)(2,1)}, bf16[256,1536]{1,0:T(8,128)(2,1)}, u32[]{:S(2)}, u32[]{:S(2)}) collective-permute-start(bf16[256,1536]{1,0:T(8,128)(2,1)} %get-tuple-element.705), channel_id=1, source_target_pairs={{0,12},{4,8},{8,4},{12,0},{1,13},{5,9},{9,5},{13,1},{2,14},{6,10},... | collective-permute-start | bytes 2359304 | tf_op jit(solution)/shard_map/ppermute | solution.py:27
  826.3 21.3 %collective-permute-start.88 = (bf16[1536,768]{1,0:T(8,128)(2,1)}, bf16[1536,768]{1,0:T(8,128)(2,1)}, u32[]{:S(2)}, u32[]{:S(2)}) collective-permute-start(bf16[1536,768]{1,0:T(8,128)(2,1)} %get-tuple-element.755), channel_id=1, source_target_pairs={{0,16},{16,0},{1,17},{17,1},{2,18},{18,2},{3,19},{19,3},{4,20},{20... | collective-permute-start | bytes 7077896 | tf_op jit(solution)/shard_map/ppermute | solution.py:27
  830.7 56.0 %collective-permute-start.95 = (bf16[4,144,1536]{2,1,0:T(8,128)(2,1)}, bf16[4,144,1536]{2,1,0:T(8,128)(2,1)}, u32[]{:S(2)}, u32[]{:S(2)}) collective-permute-start(bf16[4,144,1536]{2,1,0:T(8,128)(2,1)} %fusion.10), channel_id=1, source_target_pairs={{0,2},{2,3},{3,1},{1,0},{4,6},{6,7},{7,5},{5,4},{8,10},{10,11},{11... | collective-permute-start | bytes 5308424 | tf_op jit(solution)/shard_map/ppermute | solution.py:943
  865.9 20.8 %collective-permute-start.92 = (bf16[384,768]{1,0:T(8,128)(2,1)}, bf16[384,768]{1,0:T(8,128)(2,1)}, u32[]{:S(2)}, u32[]{:S(2)}) collective-permute-start(bf16[384,768]{1,0:T(8,128)(2,1)} %get-tuple-element.902), channel_id=1, source_target_pairs={{0,4},{4,0},{8,12},{12,8},{1,5},{5,1},{9,13},{13,9},{2,6},{6,2},{1... | collective-permute-start | bytes 1769480 | tf_op jit(solution)/shard_map/ppermute | solution.py:27
  886.7 29.5 %collective-permute-start.96 = (bf16[1536,1152]{1,0:T(8,128)(2,1)}, bf16[1536,1152]{1,0:T(8,128)(2,1)S(1)}, u32[]{:S(2)}, u32[]{:S(2)}) collective-permute-start(bf16[1536,1152]{1,0:T(8,128)(2,1)} %get-tuple-element.777), channel_id=1, source_target_pairs={{0,16},{16,0},{1,17},{17,1},{2,18},{18,2},{3,19},{19,3},{4,20},{20... | collective-permute-start | bytes 10616840 | tf_op jit(solution)/shard_map/ppermute | solution.py:27
  890.3 41.5 %collective-permute-start.108 = (bf16[4,144,1536]{2,1,0:T(8,128)(2,1)S(1)}, bf16[4,144,1536]{2,1,0:T(8,128)(2,1)S(1)}, u32[]{:S(2)}, u32[]{:S(2)}) collective-permute-start(bf16[4,144,1536]{2,1,0:T(8,128)(2,1)S(1)} %fusion.2), channel_id=1, source_target_pairs={{0,2},{2,3},{3,1},{1,0},{4,6},{6,7},{7,5},{5,4},{8,10},{10,11},{11... | collective-permute-start | bytes 5308424 | tf_op jit(solution)/shard_map/ppermute | solution.py:943
  894.8 21.2 %collective-permute-start.98 = (bf16[1,144,1536]{2,1,0:T(8,128)(2,1)S(1)}, bf16[1,144,1536]{2,1,0:T(8,128)(2,1)S(1)}, u32[]{:S(2)}, u32[]{:S(2)}) collective-permute-start(bf16[1,144,1536]{2,1,0:T(8,128)(2,1)S(1)} %get-tuple-element.926), channel_id=1, source_target_pairs={{0,8},{4,12},{8,0},{12,4},{1,9},{5,13},{9,1},{13,5},{2,10},{6,14},... | collective-permute-start | bytes 1327112 | tf_op jit(solution)/shard_map/ppermute | solution.py:27
  918.9 53.8 %collective-permute-start.100 = (bf16[384,1152]{1,0:T(8,128)(2,1)S(1)}, bf16[384,1152]{1,0:T(8,128)(2,1)S(1)}, u32[]{:S(2)}, u32[]{:S(2)}) collective-permute-start(bf16[384,1152]{1,0:T(8,128)(2,1)S(1)} %get-tuple-element.894), channel_id=1, source_target_pairs={{0,4},{4,0},{8,12},{12,8},{1,5},{5,1},{9,13},{13,9},{2,6},{6,2},{1... | collective-permute-start | bytes 2654216 | tf_op jit(solution)/shard_map/ppermute | solution.py:27
  920.2 52.9 %collective-permute-start.101 = (bf16[384,1152]{1,0:T(8,128)(2,1)S(1)}, bf16[384,1152]{1,0:T(8,128)(2,1)S(1)}, u32[]{:S(2)}, u32[]{:S(2)}) collective-permute-start(bf16[384,1152]{1,0:T(8,128)(2,1)S(1)} %get-tuple-element.893), channel_id=1, source_target_pairs={{0,8},{4,12},{8,0},{12,4},{1,9},{5,13},{9,1},{13,5},{2,10},{6,14},... | collective-permute-start | bytes 2654216 | tf_op jit(solution)/shard_map/ppermute | solution.py:27
  920.9 52.2 %collective-permute-start.102 = (bf16[384,1152]{1,0:T(8,128)(2,1)S(1)}, bf16[384,1152]{1,0:T(8,128)(2,1)S(1)}, u32[]{:S(2)}, u32[]{:S(2)}) collective-permute-start(bf16[384,1152]{1,0:T(8,128)(2,1)S(1)} %get-tuple-element.892), channel_id=1, source_target_pairs={{0,12},{4,8},{8,4},{12,0},{1,13},{5,9},{9,5},{13,1},{2,14},{6,10},... | collective-permute-start | bytes 2654216 | tf_op jit(solution)/shard_map/ppermute | solution.py:27
  923.9 48.8 %collective-permute-start.103 = (bf16[384,768]{1,0:T(8,128)(2,1)S(1)}, bf16[384,768]{1,0:T(8,128)(2,1)S(1)}, u32[]{:S(2)}, u32[]{:S(2)}) collective-permute-start(bf16[384,768]{1,0:T(8,128)(2,1)S(1)} %fusion.33), channel_id=1, source_target_pairs={{0,12},{4,8},{8,4},{12,0},{1,13},{5,9},{9,5},{13,1},{2,14},{6,10},... | collective-permute-start | bytes 1769480 | tf_op jit(solution)/shard_map/ppermute | solution.py:27
  934.5 41.8 %collective-permute-start.109 = (bf16[4,144,1536]{2,1,0:T(8,128)(2,1)S(1)}, bf16[4,144,1536]{2,1,0:T(8,128)(2,1)S(1)}, u32[]{:S(2)}, u32[]{:S(2)}) collective-permute-start(bf16[4,144,1536]{2,1,0:T(8,128)(2,1)S(1)} %fusion.1), channel_id=1, source_target_pairs={{0,2},{2,3},{3,1},{1,0},{4,6},{6,7},{7,5},{5,4},{8,10},{10,11},{11... | collective-permute-start | bytes 5308424 | tf_op jit(solution)/shard_map/ppermute | solution.py:943
  973.3 46.5 %collective-permute-start.104 = (f32[256,1536]{1,0:T(8,128)S(1)}, f32[256,1536]{1,0:T(8,128)S(1)}, u32[]{:S(2)}, u32[]{:S(2)}) collective-permute-start(f32[256,1536]{1,0:T(8,128)S(1)} %broadcast_select_fusion.2), channel_id=1, source_target_pairs={{0,16},{16,0},{1,17},{17,1},{2,18},{18,2},{3,19},{19,3},{4,20},{20... | collective-permute-start | bytes 4718600 | tf_op jit(solution)/shard_map/ppermute | solution.py:27
  980.6 20.7 %collective-permute-start.111 = (bf16[1,144,1536]{2,1,0:T(8,128)(2,1)S(1)}, bf16[1,144,1536]{2,1,0:T(8,128)(2,1)S(1)}, u32[]{:S(2)}, u32[]{:S(2)}) collective-permute-start(bf16[1,144,1536]{2,1,0:T(8,128)(2,1)S(1)} %get-tuple-element.922), channel_id=1, source_target_pairs={{0,8},{4,12},{8,0},{12,4},{1,9},{5,13},{9,1},{13,5},{2,10},{6,14},... | collective-permute-start | bytes 1327112 | tf_op jit(solution)/shard_map/ppermute | solution.py:27
  981.7 22.0 %collective-permute-start.110 = (bf16[1,144,1536]{2,1,0:T(8,128)(2,1)S(1)}, bf16[1,144,1536]{2,1,0:T(8,128)(2,1)S(1)}, u32[]{:S(2)}, u32[]{:S(2)}) collective-permute-start(bf16[1,144,1536]{2,1,0:T(8,128)(2,1)S(1)} %get-tuple-element.923), channel_id=1, source_target_pairs={{0,4},{4,0},{8,12},{12,8},{1,5},{5,1},{9,13},{13,9},{2,6},{6,2},{1... | collective-permute-start | bytes 1327112 | tf_op jit(solution)/shard_map/ppermute | solution.py:27
  983.1 20.9 %collective-permute-start.105 = (bf16[96,1920]{1,0:T(8,128)(2,1)S(1)}, bf16[96,1920]{1,0:T(8,128)(2,1)S(1)}, u32[]{:S(2)}, u32[]{:S(2)}) collective-permute-start(bf16[96,1920]{1,0:T(8,128)(2,1)S(1)} %get-tuple-element.930), channel_id=1, source_target_pairs={{0,1},{1,0},{2,3},{3,2},{4,5},{5,4},{6,7},{7,6},{8,9},{9,8},{10,11... | collective-permute-start | bytes 1105928 | tf_op jit(solution)/shard_map/ppermute | solution.py:27
  993.3 24.2 %collective-permute-start.106 = (bf16[96,1920]{1,0:T(8,128)(2,1)S(1)}, bf16[96,1920]{1,0:T(8,128)(2,1)S(1)}, u32[]{:S(2)}, u32[]{:S(2)}) collective-permute-start(bf16[96,1920]{1,0:T(8,128)(2,1)S(1)} %get-tuple-element.929), channel_id=1, source_target_pairs={{0,2},{1,3},{2,0},{3,1},{4,6},{5,7},{6,4},{7,5},{8,10},{9,11},{10,... | collective-permute-start | bytes 1105928 | tf_op jit(solution)/shard_map/ppermute | solution.py:27
  (129 other events, 1861.1 us)

commit v3 on v2

--- a/solution.py
+++ b/solution.py
@@ -1275,20 +1275,21 @@
     grads, leave_parts, leave_grads, units_moving, second_moved = tie(
         grads, leave_parts, leave_grads, ring_move(units_moving), second_moved
     )
-    enter_grads, second_scattered = tie(
-        (grads[0], swap(grads[1], "section", 1)), scatter_units(second_moved)
-    )
-    units_moving = after(ring_move(ring_add(units_moving, 1)), enter_grads)
+    enter_grads = (grads[0], swap(grads[1], "section", 1))
+    enter_parts, units_moving = tie(
+        trade_square(*enter_grads, [0, *early]), ring_move(ring_add(units_moving, 1))
+    )
     enter_parts, leave_parts, first_entry = tie(
-        trade_square(*enter_grads, range(n_ctx)),
+        enter_parts + trade_square(*enter_grads, late),
         leave_parts + trade_square(*leave_grads, late),
         first_entry,
     )
     first_moving = [sum_square(parts) for parts in (enter_parts, leave_parts)]
-    first_dense, first_scattered = tie(
+    first_dense, scattered = tie(
         send_deep(jnp.concatenate(first_moving, axis=1)),
-        scatter_units(ring_rest(ring_add(units_moving, 2), 3)),
-    )
+        scatter_units(ring_rest(ring_add(units_moving, 2), 3) + second_moved),
+    )
+    first_scattered, second_scattered = (scattered[:, :per_core], scattered[:, per_core:])
     first_dense = sum(part.astype(f32) for part in first_dense)
 
     layer_out = jnp.stack(layer_outs)

time: 1050 us -> 1070 us (1.019)
  waiting for transfers between devices: 362 us -> 380 us
    ppermute x6, waiting for transfers between devices: 7.6 us -> 39.5 us  [ring_move(): lax.ppermute(moving, 'fsdp', ring_steps)]
    ppermute x103 -> x100, waiting for transfers between devices: 331 us -> 317 us  [swap(): lax.ppermute(value, axis, [(source, source ^ bit) for source in range(cou...]
    convert_element_type x6 -> x5, other arithmetic: 23.6 us -> 21 us  [ring_add(): (moved.astype(f32) + ring_part(terms, step + 1)).astype(bf16)]
    ppermute x103 -> x100, starting transfers between devices: 110 us -> 109 us  [swap(): lax.ppermute(value, axis, [(source, source ^ bit) for source in range(cou...]
  transfers between devices with their start and end apart: 115 -> 112, of which waited for: 60 -> 58; matrix products, arithmetic and copies ran while one was open for 10% -> 10% of each run, Pallas kernels for 35% -> 34%
where the time goes in v3:
time: 1070 us; the launch traced here: 1050 us
  Pallas kernels  402 us (38%)
  waiting for transfers between devices  380 us (36%)
  starting transfers between devices  135 us (13%)
  other arithmetic  88.3 us (8%)
  local copies, waits for them, and re-layouts  43 us (4%)
    ppermute x100, waiting for transfers between devices, swap(): lax.ppermute(value, axis, [(source, source ^ bit) for source in range(cou...  317 us
    ppermute x100, starting transfers between devices, swap(): lax.ppermute(value, axis, [(source, source ^ bit) for source in range(cou...  109 us
    pallas_call x8, Pallas kernels, expert_back_call(): pl.pallas_call(functools.partial(expert_back_kernel, blocks, 1 if before...  86 us
    pallas_call x8, Pallas kernels, expert_call(): pl.pallas_call(functools.partial(expert_kernel, blocks, 1 if before else...  77.7 us
    pallas_call x8, Pallas kernels, dense_call(): pl.pallas_call(kernel, grid_spec=pltpu.PrefetchScalarGridSpec(num_scalar_...  77.1 us
    pallas_call x4, Pallas kernels, expert_grads_call(): pl.pallas_call(functools.partial(expert_grads_kernel, len(picked), deep),...  54.8 us
    ppermute x6, waiting for transfers between devices, ring_move(): lax.ppermute(moving, 'fsdp', ring_steps)  39.5 us
    pallas_call x2, Pallas kernels, attend_back_call(): pl.pallas_call(attend_back_kernel, grid_spec=pltpu.PrefetchScalarGridSpec...  33.2 us
  transfers between devices with their start and end apart: 112, of which 58 were waited for; matrix products, arithmetic and copies ran while one was open for 10% of the time, Pallas kernels for 34%

profile of v3, /device:TPU:0, one launch (start us, length us, event | category | flops | bytes accessed | tf_op | source)
XLA Modules:
  0.0 1050.4 jit_solution(1632835064084280577)
XLA Ops:
  39.1 6.9 collective-permute-done.1.refs_1_
  48.8 30.0 %collective-permute-done.2.refs_2_ = bf16[96,3072]{1,0:T(8,128)(2,1)S(1)} collective-permute-done((bf16[96,3072]{1,0:T(8,128)(2,1)S(1)}, bf16[96,3072]{1,0:T(8,128)(2,1)S(1)}, u32[]{:S(2)}, u32[]{:S(2)}) %collective-permute-start.2) | collective-permute-done | bytes 589856 | tf_op jit(solution)/shard_map/ppermute | solution.py:27
  89.8 10.7 %collective-permute-start.15 = (bf16[4,1,144,1536]{3,2,1,0:T(8,128)(2,1)}, bf16[4,1,144,1536]{3,2,1,0:T(8,128)(2,1)}, u32[]{:S(2)}, u32[]{:S(2)}) collective-permute-start(bf16[4,1,144,1536]{3,2,1,0:T(8,128)(2,1)} %get-tuple-element.450.refs_0_), channel_id=1, source_target_pairs={{0,2},{2,3},{3,1},{1,0},{4,6},{6,7},{7,5},{5,4},{8,10},{10,11},{11... | collective-permute-start | bytes 5308424 | tf_op jit(solution)/shard_map/ppermute | solution.py:902
  105.1 19.0 %collective-permute-done.12.refs_1_ = bf16[384,1152]{1,0:T(8,128)(2,1)S(1)} collective-permute-done((bf16[384,1152]{1,0:T(8,128)(2,1)S(1)}, bf16[384,1152]{1,0:T(8,128)(2,1)S(1)}, u32[]{:S(2)}, u32[]{:S(2)}) %collective-permute-start.12) | collective-permute-done | bytes 884768 | tf_op jit(solution)/shard_map/ppermute | solution.py:27
  124.2 15.2 %collective-permute-done.13.refs_2_ = bf16[384,1152]{1,0:T(8,128)(2,1)S(1)} collective-permute-done((bf16[384,1152]{1,0:T(8,128)(2,1)S(1)}, bf16[384,1152]{1,0:T(8,128)(2,1)S(1)}, u32[]{:S(2)}, u32[]{:S(2)}) %collective-permute-start.13) | collective-permute-done | bytes 884768 | tf_op jit(solution)/shard_map/ppermute | solution.py:27
  156.8 6.9 enter.2
  170.1 6.7 collective-permute-done.21
  185.0 12.1 %attend.2.attended_ref = bf16[256,1536]{1,0:T(8,128)(2,1)} custom-call(s32[8]{0:T(128)} %select_n.165.ids_ref, bf16[256,2304]{1,0:T(8,128)(2,1)} %get-tuple-element.424.query_ref, bf16[1024,512]{1,0:T(8,128)(2,1)} %pad_maximum_fusion.4.key_ref.value_ref, bf16[1024,512]{1,0:T(8,128)(2,1)} %pad_maximum_fusion.4.key_ref.value_ref), custom_call_target="tpu_custom_call" | custom-call | flops 1000000000 | bytes 3000000 | tf_op jit(solution)/shard_map/attend/pallas_call | solution.py:100
  206.6 6.0 leave.2
  216.7 25.0 %collective-permute-done.25.refs_1_ = bf16[256,1536]{1,0:T(8,128)(2,1)S(1)} collective-permute-done((bf16[256,1536]{1,0:T(8,128)(2,1)}, bf16[256,1536]{1,0:T(8,128)(2,1)S(1)}, u32[]{:S(2)}, u32[]{:S(2)}) %collective-permute-start.25) | collective-permute-done | bytes 786464 | tf_op jit(solution)/shard_map/ppermute | solution.py:27
  243.5 7.2 order.2
  259.5 12.2 %expert.8 = (bf16[256,1536]{1,0:T(8,128)(2,1)}, bf16[256,1536]{1,0:T(8,128)(2,1)}, bf16[256,1536]{1,0:T(8,128)(2,1)}, bf16[480,1536]{1,0:T(8,128)(2,1)}, f32[480,768]{1,0:T(8,128)}, /*index=5*/f32[480,768]{1,0:T(8,128)}) custom-call(bf16[3,160,256]{2,1,0:T(8,128)(2,1)} %get-tuple-element.937.pick_ref, f32[3,160,1]{2,1,0:T(8,128)} %copy.330.share_ref, ...), custom_call_target="tpu_custom_call" | custom-call | flops 3000000000 | bytes 9000000 | tf_op jit(solution)/shard_map/expert/pallas_call | solution.py:262
  276.9 12.9 %expert.9 = (bf16[256,1536]{1,0:T(8,128)(2,1)}, bf16[256,1536]{1,0:T(8,128)(2,1)}, bf16[256,1536]{1,0:T(8,128)(2,1)}, bf16[480,1536]{1,0:T(8,128)(2,1)}, f32[480,768]{1,0:T(8,128)}, /*index=5*/f32[480,768]{1,0:T(8,128)}) custom-call(bf16[3,160,256]{2,1,0:T(8,128)(2,1)} %get-tuple-element.938.pick_ref, f32[3,160,1]{2,1,0:T(8,128)} %copy.331.share_ref, ...), custom_call_target="tpu_custom_call" | custom-call | flops 3000000000 | bytes 9000000 | tf_op jit(solution)/shard_map/expert/pallas_call | solution.py:262
  295.1 6.5 expert.10
  301.6 7.3 expert.11
  317.1 18.9 %collective-permute-done.39.refs_4_ = bf16[256,1536]{1,0:T(8,128)(2,1)S(1)} collective-permute-done((bf16[256,1536]{1,0:T(8,128)(2,1)S(1)}, bf16[256,1536]{1,0:T(8,128)(2,1)S(1)}, u32[]{:S(2)}, u32[]{:S(2)}) %collective-permute-start.39) | collective-permute-done | bytes 786464 | tf_op jit(solution)/shard_map/ppermute | solution.py:27
  340.5 8.4 enter.3
  351.6 5.9 collective-permute-done.42.refs_1_
  363.5 6.7 collective-permute-done.45
  376.6 12.0 %attend.3.attended_ref = bf16[256,1536]{1,0:T(8,128)(2,1)} custom-call(s32[8]{0:T(128)} %select_n.165.ids_ref, bf16[256,2304]{1,0:T(8,128)(2,1)} %get-tuple-element.497.query_ref, bf16[1024,512]{1,0:T(8,128)(2,1)} %pad_maximum_fusion.5.key_ref.value_ref, bf16[1024,512]{1,0:T(8,128)(2,1)} %pad_maximum_fusion.5.key_ref.value_ref), custom_call_target="tpu_custom_call" | custom-call | flops 1000000000 | bytes 3000000 | tf_op jit(solution)/shard_map/attend/pallas_call | solution.py:100
  391.4 6.4 collective-permute-done.47.refs_2_
  406.1 6.0 leave.3
  414.3 17.7 %collective-permute-done.49.refs_1_ = bf16[256,1536]{1,0:T(8,128)(2,1)S(1)} collective-permute-done((bf16[256,1536]{1,0:T(8,128)(2,1)}, bf16[256,1536]{1,0:T(8,128)(2,1)S(1)}, u32[]{:S(2)}, u32[]{:S(2)}) %collective-permute-start.49) | collective-permute-done | bytes 786464 | tf_op jit(solution)/shard_map/ppermute | solution.py:27
  432.5 10.9 %collective-permute-done.51.refs_3_ = bf16[4,1,144,1536]{3,2,1,0:T(8,128)(2,1)} collective-permute-done((bf16[4,1,144,1536]{3,2,1,0:T(8,128)(2,1)}, bf16[4,1,144,1536]{3,2,1,0:T(8,128)(2,1)}, u32[]{:S(2)}, u32[]{:S(2)}) %collective-permute-start.51) | collective-permute-done | bytes 1769504 | tf_op jit(solution)/shard_map/ppermute | solution.py:902
  443.4 7.1 order.3
  454.0 12.1 %expert.12 = (bf16[256,1536]{1,0:T(8,128)(2,1)}, bf16[256,1536]{1,0:T(8,128)(2,1)}, bf16[256,1536]{1,0:T(8,128)(2,1)}, bf16[480,1536]{1,0:T(8,128)(2,1)}, f32[480,768]{1,0:T(8,128)}, /*index=5*/f32[480,768]{1,0:T(8,128)}) custom-call(bf16[3,160,256]{2,1,0:T(8,128)(2,1)} %get-tuple-element.935.pick_ref, f32[3,160,1]{2,1,0:T(8,128)} %copy.336.share_ref, ...), custom_call_target="tpu_custom_call" | custom-call | flops 3000000000 | bytes 9000000 | tf_op jit(solution)/shard_map/expert/pallas_call | solution.py:262
  466.1 12.8 %expert.13 = (bf16[256,1536]{1,0:T(8,128)(2,1)}, bf16[256,1536]{1,0:T(8,128)(2,1)}, bf16[256,1536]{1,0:T(8,128)(2,1)}, bf16[480,1536]{1,0:T(8,128)(2,1)}, f32[480,768]{1,0:T(8,128)}, /*index=5*/f32[480,768]{1,0:T(8,128)}) custom-call(bf16[3,160,256]{2,1,0:T(8,128)(2,1)} %get-tuple-element.936.pick_ref, f32[3,160,1]{2,1,0:T(8,128)} %copy.337.share_ref, ...), custom_call_target="tpu_custom_call" | custom-call | flops 3000000000 | bytes 9000000 | tf_op jit(solution)/shard_map/expert/pallas_call | solution.py:262
  482.4 6.6 expert.14
  489.0 9.6 collective-permute-done.54.refs_1_
  500.6 7.2 expert.15
  507.8 13.3 %expert_back.8 = (bf16[256,1536]{1,0:T(8,128)(2,1)}, bf16[256,1536]{1,0:T(8,128)(2,1)}, bf16[256,1536]{1,0:T(8,128)(2,1)}, bf16[480,1536]{1,0:T(8,128)(2,1)}, bf...) custom-call(bf16[3,160,256]{2,1,0:T(8,128)(2,1)} %get-tuple-element.935.pick_ref, ...), custom_call_target="tpu_custom_call" | custom-call | flops 4000000000 | bytes 12000000 | tf_op jit(solution)/shard_map/expert_back/pallas_call | solution.py:322
  521.1 14.0 %expert_back.9 = (bf16[256,1536]{1,0:T(8,128)(2,1)}, bf16[256,1536]{1,0:T(8,128)(2,1)}, bf16[256,1536]{1,0:T(8,128)(2,1)}, bf16[480,1536]{1,0:T(8,128)(2,1)}, bf...) custom-call(bf16[3,160,256]{2,1,0:T(8,128)(2,1)} %get-tuple-element.936.pick_ref, ...), custom_call_target="tpu_custom_call" | custom-call | flops 4000000000 | bytes 12000000 | tf_op jit(solution)/shard_map/expert_back/pallas_call | solution.py:322
  537.0 7.6 expert_back.10
  544.6 8.0 expert_back.11
  558.8 13.5 %expert_grads.4 = bf16[16,144,1536]{2,1,0:T(8,128)(2,1)} custom-call(bf16[480,1536]{1,0:T(8,128)(2,1)} %get-tuple-element.588.refs_0_, bf16[160,1536]{1,0:T(8,128)(2,1)} %get-tuple-element.589.refs_1_, bf16[480,1536]{1,0:T(8,128)(2,1)} %get-tuple-element.590.refs_2_, bf16[160,1536]{1,0:T(8,128)(2,1)} %get-tuple-element.591.refs_3_, ...), custom_call_target="tpu_custom_call" | custom-call | flops 1000000000 | bytes 3000000 | tf_op jit(solution)/shard_map/expert_grads/pallas_call | solution.py:388
  572.3 13.8 %expert_grads.5 = bf16[16,144,1536]{2,1,0:T(8,128)(2,1)} custom-call(bf16[480,1536]{1,0:T(8,128)(2,1)} %get-tuple-element.598.refs_0_, bf16[160,1536]{1,0:T(8,128)(2,1)} %get-tuple-element.599.refs_1_, bf16[480,1536]{1,0:T(8,128)(2,1)} %get-tuple-element.600.refs_2_, bf16[160,1536]{1,0:T(8,128)(2,1)} %get-tuple-element.601.refs_3_, ...), custom_call_target="tpu_custom_call" | custom-call | flops 1000000000 | bytes 3000000 | tf_op jit(solution)/shard_map/expert_grads/pallas_call | solution.py:388
  590.3 11.3 %leave_back.2 = (f32[256,1536]{1,0:T(8,128)}, bf16[256,1536]{1,0:T(8,128)(2,1)}, bf16[256,1536]{1,0:T(8,128)(2,1)}, bf16[1536,768]{1,0:T(8,128)(2,1)}, bf16[1536,768]{1,0:T(8,128)(2,1)}) custom-call(s32[1]{0:T(128)} %bitcast.48.core_ref, f32[1,1536]{1,0:T(1,128)} %copy.344.gain_ref, f32[256,1536]{1,0:T(8,128)} %get-tuple-element.510.mid_ref, ...), custom_call_target="tpu_custom_call" | custom-call | flops 8000000000 | bytes 24000000 | tf_op jit(solution)/shard_map/leave_back/pallas_call | solution.py:439
  610.6 16.6 %attend_back.2 = (bf16[256,1536]{1,0:T(8,128)(2,1)}, bf16[256,512]{1,0:T(8,128)(2,1)}, bf16[256,512]{1,0:T(8,128)(2,1)}, bf16[256,512]{1,0:T(8,128)(2,1)}, bf16[256,512]{1,0:T(8,128)(2,1)}) custom-call(s32[8]{0:T(128)} %select_n.165.ids_ref, bf16[256,2304]{1,0:T(8,128)(2,1)} %get-tuple-element.497.query_ref, ...), custom_call_target="tpu_custom_call" | custom-call | flops 1000000000 | bytes 3000000 | tf_op jit(solution)/shard_map/attend_back/pallas_call | solution.py:150
  632.8 4.4 fusion.38
  648.2 13.7 %enter_back.2 = (f32[256,1536]{1,0:T(8,128)}, bf16[256,1536]{1,0:T(8,128)(2,1)}, bf16[1536,1152]{1,0:T(8,128)(2,1)}, bf16[1536,1152]{1,0:T(8,128)(2,1)}) custom-call(s32[1]{0:T(128)} %bitcast.48.core_ref, f32[1,1536]{1,0:T(1,128)} %copy.347.gain_ref, bf16[256,1536]{1,0:T(8,128)(2,1)} %get-tuple-element.696.rows_ref, ...), custom_call_target="tpu_custom_call" | custom-call | flops 1000000000 | bytes 3000000 | tf_op jit(solution)/shard_map/enter_back/pallas_call | solution.py:439
  661.9 6.3 collective-permute-done.70
  670.4 4.8 fusion.5
  675.8 12.6 %collective-permute-done.72.refs_1_ = bf16[256,1536]{1,0:T(8,128)(2,1)S(1)} collective-permute-done((bf16[256,1536]{1,0:T(8,128)(2,1)}, bf16[256,1536]{1,0:T(8,128)(2,1)S(1)}, u32[]{:S(2)}, u32[]{:S(2)}) %collective-permute-start.72) | collective-permute-done | bytes 786464 | tf_op jit(solution)/shard_map/ppermute | solution.py:27
  695.9 13.6 %expert_back.12 = (bf16[256,1536]{1,0:T(8,128)(2,1)}, bf16[256,1536]{1,0:T(8,128)(2,1)}, bf16[256,1536]{1,0:T(8,128)(2,1)}, bf16[480,1536]{1,0:T(8,128)(2,1)}, b...) custom-call(bf16[3,160,256]{2,1,0:T(8,128)(2,1)} %get-tuple-element.937.pick_ref, ...), custom_call_target="tpu_custom_call" | custom-call | flops 4000000000 | bytes 12000000 | tf_op jit(solution)/shard_map/expert_back/pallas_call | solution.py:322
  709.5 14.0 %expert_back.13 = (bf16[256,1536]{1,0:T(8,128)(2,1)}, bf16[256,1536]{1,0:T(8,128)(2,1)}, bf16[256,1536]{1,0:T(8,128)(2,1)}, bf16[480,1536]{1,0:T(8,128)(2,1)}, b...) custom-call(bf16[3,160,256]{2,1,0:T(8,128)(2,1)} %get-tuple-element.938.pick_ref, ...), custom_call_target="tpu_custom_call" | custom-call | flops 4000000000 | bytes 12000000 | tf_op jit(solution)/shard_map/expert_back/pallas_call | solution.py:322
  723.6 7.5 collective-permute-done.75.refs_0_
  732.0 4.7 fusion.4
  747.6 7.6 expert_back.14
  755.3 7.8 expert_back.15
  763.1 15.3 %collective-permute-done.80.refs_2_ = bf16[256,1536]{1,0:T(8,128)(2,1)} collective-permute-done((bf16[256,1536]{1,0:T(8,128)(2,1)}, bf16[256,1536]{1,0:T(8,128)(2,1)}, u32[]{:S(2)}, u32[]{:S(2)}) %collective-permute-start.80) | collective-permute-done | bytes 786464 | tf_op jit(solution)/shard_map/ppermute | solution.py:27
  786.2 13.6 %expert_grads.6 = bf16[16,144,1536]{2,1,0:T(8,128)(2,1)} custom-call(bf16[480,1536]{1,0:T(8,128)(2,1)} %get-tuple-element.706.refs_0_, bf16[160,1536]{1,0:T(8,128)(2,1)} %get-tuple-element.707.refs_1_, bf16[480,1536]{1,0:T(8,128)(2,1)} %get-tuple-element.708.refs_2_, bf16[160,1536]{1,0:T(8,128)(2,1)} %get-tuple-element.709.refs_3_, ...), custom_call_target="tpu_custom_call" | custom-call | flops 1000000000 | bytes 3000000 | tf_op jit(solution)/shard_map/expert_grads/pallas_call | solution.py:388
  799.8 13.9 %expert_grads.7 = bf16[16,144,1536]{2,1,0:T(8,128)(2,1)} custom-call(bf16[480,1536]{1,0:T(8,128)(2,1)} %get-tuple-element.716.refs_0_, bf16[160,1536]{1,0:T(8,128)(2,1)} %get-tuple-element.717.refs_1_, bf16[480,1536]{1,0:T(8,128)(2,1)} %get-tuple-element.718.refs_2_, bf16[160,1536]{1,0:T(8,128)(2,1)} %get-tuple-element.719.refs_3_, ...), custom_call_target="tpu_custom_call" | custom-call | flops 1000000000 | bytes 3000000 | tf_op jit(solution)/shard_map/expert_grads/pallas_call | solution.py:388
  815.1 11.3 %leave_back.3 = (f32[256,1536]{1,0:T(8,128)}, bf16[256,1536]{1,0:T(8,128)(2,1)}, bf16[256,1536]{1,0:T(8,128)(2,1)}, bf16[1536,768]{1,0:T(8,128)(2,1)}, bf16[1536,768]{1,0:T(8,128)(2,1)}) custom-call(s32[1]{0:T(128)} %bitcast.48.core_ref, f32[1,1536]{1,0:T(1,128)} %copy.329.gain_ref, f32[256,1536]{1,0:T(8,128)} %get-tuple-element.482.refs_0_.mid_ref, ...), custom_call_target="tpu_custom_call" | custom-call | flops 8000000000 | bytes 24000000 | tf_op jit(solution)/shard_map/leave_back/pallas_call | solution.py:439
  831.0 16.6 %attend_back.3 = (bf16[256,1536]{1,0:T(8,128)(2,1)}, bf16[256,512]{1,0:T(8,128)(2,1)}, bf16[256,512]{1,0:T(8,128)(2,1)}, bf16[256,512]{1,0:T(8,128)(2,1)}, bf16[256,512]{1,0:T(8,128)(2,1)}) custom-call(s32[8]{0:T(128)} %select_n.165.ids_ref, bf16[256,2304]{1,0:T(8,128)(2,1)} %get-tuple-element.424.query_ref, ...), custom_call_target="tpu_custom_call" | custom-call | flops 1000000000 | bytes 3000000 | tf_op jit(solution)/shard_map/attend_back/pallas_call | solution.py:150
  851.2 5.9 collective-permute-done.89.refs_1_
  857.1 5.3 collective-permute-done.90.refs_2_
  868.1 5.1 fusion.3
  873.2 13.6 %enter_back.3 = (f32[256,1536]{1,0:T(8,128)}, bf16[256,1536]{1,0:T(8,128)(2,1)}, bf16[1536,1152]{1,0:T(8,128)(2,1)}, bf16[1536,1152]{1,0:T(8,128)(2,1)}) custom-call(s32[1]{0:T(128)} %bitcast.48.core_ref, f32[1,1536]{1,0:T(1,128)} %copy.328.gain_ref, bf16[256,1536]{1,0:T(8,128)(2,1)} %get-tuple-element.421.refs_0_.rows_ref, ...), custom_call_target="tpu_custom_call" | custom-call | flops 1000000000 | bytes 3000000 | tf_op jit(solution)/shard_map/enter_back/pallas_call | solution.py:439
  896.2 35.6 %collective-permute-done.99 = bf16[4,144,1536]{2,1,0:T(8,128)(2,1)S(1)} collective-permute-done((bf16[4,144,1536]{2,1,0:T(8,128)(2,1)S(1)}, bf16[4,144,1536]{2,1,0:T(8,128)(2,1)S(1)}, u32[]{:S(2)}, u32[]{:S(2)}) %collective-permute-start.99) | collective-permute-done | bytes 1769504 | tf_op jit(solution)/shard_map/ppermute | solution.py:943
  944.6 28.2 %collective-permute-done.101 = bf16[384,768]{1,0:T(8,128)(2,1)S(1)} collective-permute-done((bf16[384,768]{1,0:T(8,128)(2,1)S(1)}, bf16[384,768]{1,0:T(8,128)(2,1)S(1)}, u32[]{:S(2)}, u32[]{:S(2)}) %collective-permute-start.101) | collective-permute-done | bytes 589856 | tf_op jit(solution)/shard_map/ppermute | solution.py:27
  987.3 15.4 %collective-permute-done.109 = bf16[2,144,1536]{2,1,0:T(8,128)(2,1)S(1)} collective-permute-done((bf16[2,144,1536]{2,1,0:T(8,128)(2,1)S(1)}, bf16[2,144,1536]{2,1,0:T(8,128)(2,1)S(1)}, u32[]{:S(2)}, u32[]{:S(2)}) %collective-permute-start.109) | collective-permute-done | bytes 884768 | tf_op jit(solution)/shard_map/ppermute | solution.py:27
  1006.1 13.3 %collective-permute-done.108 = bf16[2,144,1536]{2,1,0:T(8,128)(2,1)S(1)} collective-permute-done((bf16[2,144,1536]{2,1,0:T(8,128)(2,1)S(1)}, bf16[2,144,1536]{2,1,0:T(8,128)(2,1)S(1)}, u32[]{:S(2)}, u32[]{:S(2)}) %collective-permute-start.108) | collective-permute-done | bytes 884768 | tf_op jit(solution)/shard_map/ppermute | solution.py:27
  1022.5 9.4 collective-permute-done.105
  1041.2 8.7 finish.1
  (469 shorter events, 308.9 us)
Async XLA Ops:
  7.8 20.6 %collective-permute-start.4 = (bf16[4,1,144,1536]{3,2,0,1:T(8,128)(2,1)}, bf16[4,1,144,1536]{3,2,0,1:T(8,128)(2,1)}, u32[]{:S(2)}, u32[]{:S(2)}) collective-permute-start(bf16[4,1,144,1536]{3,2,0,1:T(8,128)(2,1)} %dynamic-slice_bitcast_fusion), channel_id=1, source_target_pairs={{0,16},{16,0},{1,17},{17,1},{2,18},{18,2},{3,19},{19,3},{4,20},{20... | collective-permute-start | bytes 5308424 | tf_op jit(solution)/shard_map/ppermute | solution.py:27
  33.0 51.0 %collective-permute-start.5 = (bf16[2,1,144,1536]{3,2,1,0:T(8,128)(2,1)S(1)}, bf16[2,1,144,1536]{3,2,1,0:T(8,128)(2,1)S(1)}, u32[]{:S(2)}, u32[]{:S(2)}) collective-permute-start(bf16[2,1,144,1536]{3,2,1,0:T(8,128)(2,1)S(1)} %get-tuple-element.916), channel_id=1, source_target_pairs={{0,4},{4,0},{8,12},{12,8},{1,5},{5,1},{9,13},{13,9},{2,6},{6,2},{1... | collective-permute-start | bytes 2654216 | tf_op jit(solution)/shard_map/ppermute | solution.py:27
  33.5 50.4 %collective-permute-start.6 = (bf16[2,1,144,1536]{3,2,1,0:T(8,128)(2,1)S(1)}, bf16[2,1,144,1536]{3,2,1,0:T(8,128)(2,1)S(1)}, u32[]{:S(2)}, u32[]{:S(2)}) collective-permute-start(bf16[2,1,144,1536]{3,2,1,0:T(8,128)(2,1)S(1)} %get-tuple-element.917), channel_id=1, source_target_pairs={{0,8},{4,12},{8,0},{12,4},{1,9},{5,13},{9,1},{13,5},{2,10},{6,14},... | collective-permute-start | bytes 2654216 | tf_op jit(solution)/shard_map/ppermute | solution.py:27
  35.0 48.9 %collective-permute-start.7 = (bf16[2,1,144,1536]{3,2,1,0:T(8,128)(2,1)S(1)}, bf16[2,1,144,1536]{3,2,1,0:T(8,128)(2,1)S(1)}, u32[]{:S(2)}, u32[]{:S(2)}) collective-permute-start(bf16[2,1,144,1536]{3,2,1,0:T(8,128)(2,1)S(1)} %get-tuple-element.914), channel_id=1, source_target_pairs={{0,12},{4,8},{8,4},{12,0},{1,13},{5,9},{9,5},{13,1},{2,14},{6,10},... | collective-permute-start | bytes 2654216 | tf_op jit(solution)/shard_map/ppermute | solution.py:27
  36.5 42.3 %collective-permute-start.2 = (bf16[96,3072]{1,0:T(8,128)(2,1)S(1)}, bf16[96,3072]{1,0:T(8,128)(2,1)S(1)}, u32[]{:S(2)}, u32[]{:S(2)}) collective-permute-start(bf16[96,3072]{1,0:T(8,128)(2,1)S(1)} %pad_maximum_fusion.7.refs_0_), channel_id=1, source_target_pairs={{0,2},{1,3},{2,0},{3,1},{4,6},{5,7},{6,4},{7,5},{8,10},{9,11},{10,... | collective-permute-start | bytes 1769480 | tf_op jit(solution)/shard_map/ppermute | solution.py:27
  46.0 32.7 %collective-permute-start.3 = (bf16[96,3072]{1,0:T(8,128)(2,1)S(1)}, bf16[96,3072]{1,0:T(8,128)(2,1)S(1)}, u32[]{:S(2)}, u32[]{:S(2)}) collective-permute-start(bf16[96,3072]{1,0:T(8,128)(2,1)S(1)} %pad_maximum_fusion.7.refs_0_), channel_id=1, source_target_pairs={{0,3},{1,2},{2,1},{3,0},{4,7},{5,6},{6,5},{7,4},{8,11},{9,10},{10,... | collective-permute-start | bytes 1769480 | tf_op jit(solution)/shard_map/ppermute | solution.py:27
  89.8 51.8 %collective-permute-start.15 = (bf16[4,1,144,1536]{3,2,1,0:T(8,128)(2,1)}, bf16[4,1,144,1536]{3,2,1,0:T(8,128)(2,1)}, u32[]{:S(2)}, u32[]{:S(2)}) collective-permute-start(bf16[4,1,144,1536]{3,2,1,0:T(8,128)(2,1)} %get-tuple-element.450.refs_0_), channel_id=1, source_target_pairs={{0,2},{2,3},{3,1},{1,0},{4,6},{6,7},{7,5},{5,4},{8,10},{10,11},{11... | collective-permute-start | bytes 5308424 | tf_op jit(solution)/shard_map/ppermute | solution.py:902
  101.6 22.6 %collective-permute-start.12 = (bf16[384,1152]{1,0:T(8,128)(2,1)S(1)}, bf16[384,1152]{1,0:T(8,128)(2,1)S(1)}, u32[]{:S(2)}, u32[]{:S(2)}) collective-permute-start(bf16[384,1152]{1,0:T(8,128)(2,1)S(1)} %get-tuple-element.417.refs_0_), channel_id=1, source_target_pairs={{0,4},{4,0},{8,12},{12,8},{1,5},{5,1},{9,13},{13,9},{2,6},{6,2},{1... | collective-permute-start | bytes 2654216 | tf_op jit(solution)/shard_map/ppermute | solution.py:27
  102.4 37.0 %collective-permute-start.13 = (bf16[384,1152]{1,0:T(8,128)(2,1)S(1)}, bf16[384,1152]{1,0:T(8,128)(2,1)S(1)}, u32[]{:S(2)}, u32[]{:S(2)}) collective-permute-start(bf16[384,1152]{1,0:T(8,128)(2,1)S(1)} %get-tuple-element.417.refs_0_), channel_id=1, source_target_pairs={{0,8},{4,12},{8,0},{12,4},{1,9},{5,13},{9,1},{13,5},{2,10},{6,14},... | collective-permute-start | bytes 2654216 | tf_op jit(solution)/shard_map/ppermute | solution.py:27
  103.9 36.7 %collective-permute-start.14 = (bf16[384,1152]{1,0:T(8,128)(2,1)S(1)}, bf16[384,1152]{1,0:T(8,128)(2,1)S(1)}, u32[]{:S(2)}, u32[]{:S(2)}) collective-permute-start(bf16[384,1152]{1,0:T(8,128)(2,1)S(1)} %get-tuple-element.417.refs_0_), channel_id=1, source_target_pairs={{0,12},{4,8},{8,4},{12,0},{1,13},{5,9},{9,5},{13,1},{2,14},{6,10},... | collective-permute-start | bytes 2654216 | tf_op jit(solution)/shard_map/ppermute | solution.py:27
  151.7 45.3 %collective-permute-start.23 = (bf16[4,1,144,1536]{3,2,1,0:T(8,128)(2,1)}, bf16[4,1,144,1536]{3,2,1,0:T(8,128)(2,1)}, u32[]{:S(2)}, u32[]{:S(2)}) collective-permute-start(bf16[4,1,144,1536]{3,2,1,0:T(8,128)(2,1)} %collective-permute-done.15.refs_1_), channel_id=1, source_target_pairs={{0,2},{2,3},{3,1},{1,0},{4,6},{6,7},{7,5},{5,4},{8,10},{10,11},{11... | collective-permute-start | bytes 5308424 | tf_op jit(solution)/shard_map/ppermute | solution.py:902
  201.7 41.3 %collective-permute-start.27 = (bf16[4,1,144,1536]{3,2,1,0:T(8,128)(2,1)}, bf16[4,1,144,1536]{3,2,1,0:T(8,128)(2,1)}, u32[]{:S(2)}, u32[]{:S(2)}) collective-permute-start(bf16[4,1,144,1536]{3,2,1,0:T(8,128)(2,1)} %collective-permute-done.23.refs_2_), channel_id=1, source_target_pairs={{0,2},{2,3},{3,1},{1,0},{4,6},{6,7},{7,5},{5,4},{8,10},{10,11},{11... | collective-permute-start | bytes 5308424 | tf_op jit(solution)/shard_map/ppermute | solution.py:902
  202.8 39.8 %collective-permute-start.28 = (bf16[384,1152]{1,0:T(8,128)(2,1)}, bf16[384,1152]{1,0:T(8,128)(2,1)S(1)}, u32[]{:S(2)}, u32[]{:S(2)}) collective-permute-start(bf16[384,1152]{1,0:T(8,128)(2,1)} %get-tuple-element.478.refs_0_), channel_id=1, source_target_pairs={{0,4},{4,0},{8,12},{12,8},{1,5},{5,1},{9,13},{13,9},{2,6},{6,2},{1... | collective-permute-start | bytes 2654216 | tf_op jit(solution)/shard_map/ppermute | solution.py:27
  204.0 38.6 %collective-permute-start.29 = (bf16[384,1152]{1,0:T(8,128)(2,1)}, bf16[384,1152]{1,0:T(8,128)(2,1)S(1)}, u32[]{:S(2)}, u32[]{:S(2)}) collective-permute-start(bf16[384,1152]{1,0:T(8,128)(2,1)} %get-tuple-element.478.refs_0_), channel_id=1, source_target_pairs={{0,8},{4,12},{8,0},{12,4},{1,9},{5,13},{9,1},{13,5},{2,10},{6,14},... | collective-permute-start | bytes 2654216 | tf_op jit(solution)/shard_map/ppermute | solution.py:27
  212.5 29.1 %collective-permute-start.25 = (bf16[256,1536]{1,0:T(8,128)(2,1)}, bf16[256,1536]{1,0:T(8,128)(2,1)S(1)}, u32[]{:S(2)}, u32[]{:S(2)}) collective-permute-start(bf16[256,1536]{1,0:T(8,128)(2,1)} %get-tuple-element.454.refs_0_), channel_id=1, source_target_pairs={{0,4},{4,0},{8,12},{12,8},{1,5},{5,1},{9,13},{13,9},{2,6},{6,2},{1... | collective-permute-start | bytes 2359304 | tf_op jit(solution)/shard_map/ppermute | solution.py:27
  213.8 28.9 %collective-permute-start.26 = (bf16[256,1536]{1,0:T(8,128)(2,1)}, bf16[256,1536]{1,0:T(8,128)(2,1)S(1)}, u32[]{:S(2)}, u32[]{:S(2)}) collective-permute-start(bf16[256,1536]{1,0:T(8,128)(2,1)} %get-tuple-element.454.refs_0_), channel_id=1, source_target_pairs={{0,8},{4,12},{8,0},{12,4},{1,9},{5,13},{9,1},{13,5},{2,10},{6,14},... | collective-permute-start | bytes 2359304 | tf_op jit(solution)/shard_map/ppermute | solution.py:27
  250.7 26.2 %collective-permute-start.30 = (bf16[16,144,1536]{2,1,0:T(8,128)(2,1)}, bf16[16,144,1536]{2,1,0:T(8,128)(2,1)}, u32[]{:S(2)}, u32[]{:S(2)}) collective-permute-start(bf16[16,144,1536]{2,1,0:T(8,128)(2,1)} %bitcast.281), channel_id=1, source_target_pairs={{0,16},{16,0},{1,17},{17,1},{2,18},{18,2},{3,19},{19,3},{4,20},{20... | collective-permute-start | bytes 21233672 | tf_op jit(solution)/shard_map/ppermute | solution.py:27
  252.5 37.4 %collective-permute-start.31 = (bf16[256,1536]{1,0:T(8,128)(2,1)S(1)}, bf16[256,1536]{1,0:T(8,128)(2,1)S(1)}, u32[]{:S(2)}, u32[]{:S(2)}) collective-permute-start(bf16[256,1536]{1,0:T(8,128)(2,1)S(1)} %copy-done.15), channel_id=1, source_target_pairs={{0,12},{4,8},{8,4},{12,0},{1,13},{5,9},{9,5},{13,1},{2,14},{6,10},... | collective-permute-start | bytes 2359304 | tf_op jit(solution)/shard_map/ppermute | solution.py:27
  271.6 37.3 %collective-permute-start.37 = (bf16[384,1152]{1,0:T(8,128)(2,1)}, bf16[384,1152]{1,0:T(8,128)(2,1)}, u32[]{:S(2)}, u32[]{:S(2)}) collective-permute-start(bf16[384,1152]{1,0:T(8,128)(2,1)} %get-tuple-element.478.refs_0_), channel_id=1, source_target_pairs={{0,12},{4,8},{8,4},{12,0},{1,13},{5,9},{9,5},{13,1},{2,14},{6,10},... | collective-permute-start | bytes 2654216 | tf_op jit(solution)/shard_map/ppermute | solution.py:27
  315.1 22.8 %collective-permute-start.38 = (bf16[1536,1152]{1,0:T(8,128)(2,1)}, bf16[1536,1152]{1,0:T(8,128)(2,1)S(1)}, u32[]{:S(2)}, u32[]{:S(2)}) collective-permute-start(bf16[1536,1152]{1,0:T(8,128)(2,1)} %place.10.refs_5_.refs_4_), channel_id=1, source_target_pairs={{0,16},{16,0},{1,17},{17,1},{2,18},{18,2},{3,19},{19,3},{4,20},{20... | collective-permute-start | bytes 10616840 | tf_op jit(solution)/shard_map/ppermute | solution.py:27
  315.2 20.9 %collective-permute-start.39 = (bf16[256,1536]{1,0:T(8,128)(2,1)S(1)}, bf16[256,1536]{1,0:T(8,128)(2,1)S(1)}, u32[]{:S(2)}, u32[]{:S(2)}) collective-permute-start(bf16[256,1536]{1,0:T(8,128)(2,1)S(1)} %copy-done.65), channel_id=1, source_target_pairs={{0,12},{4,8},{8,4},{12,0},{1,13},{5,9},{9,5},{13,1},{2,14},{6,10},... | collective-permute-start | bytes 2359304 | tf_op jit(solution)/shard_map/ppermute | solution.py:27
  316.6 41.0 %collective-permute-start.42 = (bf16[4,1,144,1536]{3,2,1,0:T(8,128)(2,1)}, bf16[4,1,144,1536]{3,2,1,0:T(8,128)(2,1)}, u32[]{:S(2)}, u32[]{:S(2)}) collective-permute-start(bf16[4,1,144,1536]{3,2,1,0:T(8,128)(2,1)} %get-tuple-element.518.refs_0_), channel_id=1, source_target_pairs={{0,2},{2,3},{3,1},{1,0},{4,6},{6,7},{7,5},{5,4},{8,10},{10,11},{11... | collective-permute-start | bytes 5308424 | tf_op jit(solution)/shard_map/ppermute | solution.py:902
  357.6 40.2 %collective-permute-start.47 = (bf16[4,1,144,1536]{3,2,1,0:T(8,128)(2,1)}, bf16[4,1,144,1536]{3,2,1,0:T(8,128)(2,1)}, u32[]{:S(2)}, u32[]{:S(2)}) collective-permute-start(bf16[4,1,144,1536]{3,2,1,0:T(8,128)(2,1)} %collective-permute-done.42.refs_1_), channel_id=1, source_target_pairs={{0,2},{2,3},{3,1},{1,0},{4,6},{6,7},{7,5},{5,4},{8,10},{10,11},{11... | collective-permute-start | bytes 5308424 | tf_op jit(solution)/shard_map/ppermute | solution.py:902
  401.3 42.1 %collective-permute-start.51 = (bf16[4,1,144,1536]{3,2,1,0:T(8,128)(2,1)}, bf16[4,1,144,1536]{3,2,1,0:T(8,128)(2,1)}, u32[]{:S(2)}, u32[]{:S(2)}) collective-permute-start(bf16[4,1,144,1536]{3,2,1,0:T(8,128)(2,1)} %collective-permute-done.47.refs_2_), channel_id=1, source_target_pairs={{0,2},{2,3},{3,1},{1,0},{4,6},{6,7},{7,5},{5,4},{8,10},{10,11},{11... | collective-permute-start | bytes 5308424 | tf_op jit(solution)/shard_map/ppermute | solution.py:902
  450.5 28.4 %collective-permute-start.53 = (bf16[256,1536]{1,0:T(8,128)(2,1)S(1)}, bf16[256,1536]{1,0:T(8,128)(2,1)S(1)}, u32[]{:S(2)}, u32[]{:S(2)}) collective-permute-start(bf16[256,1536]{1,0:T(8,128)(2,1)S(1)} %copy-done.21), channel_id=1, source_target_pairs={{0,12},{4,8},{8,4},{12,0},{1,13},{5,9},{9,5},{13,1},{2,14},{6,10},... | collective-permute-start | bytes 2359304 | tf_op jit(solution)/shard_map/ppermute | solution.py:27
  498.9 36.2 %collective-permute-start.56 = (bf16[256,1536]{1,0:T(8,128)(2,1)S(1)}, bf16[256,1536]{1,0:T(8,128)(2,1)S(1)}, u32[]{:S(2)}, u32[]{:S(2)}) collective-permute-start(bf16[256,1536]{1,0:T(8,128)(2,1)S(1)} %get-tuple-element.543.refs_0_.cot_ref), channel_id=1, source_target_pairs={{0,12},{4,8},{8,4},{12,0},{1,13},{5,9},{9,5},{13,1},{2,14},{6,10},... | collective-permute-start | bytes 2359304 | tf_op jit(solution)/shard_map/ppermute | solution.py:27
  555.3 30.8 %collective-permute-start.59 = (bf16[256,1536]{1,0:T(8,128)(2,1)}, bf16[256,1536]{1,0:T(8,128)(2,1)}, u32[]{:S(2)}, u32[]{:S(2)}) collective-permute-start(bf16[256,1536]{1,0:T(8,128)(2,1)} %get-tuple-element.587), channel_id=1, source_target_pairs={{0,12},{4,8},{8,4},{12,0},{1,13},{5,9},{9,5},{13,1},{2,14},{6,10},... | collective-permute-start | bytes 2359304 | tf_op jit(solution)/shard_map/ppermute | solution.py:27
  556.9 32.9 %collective-permute-start.60 = (bf16[256,1536]{1,0:T(8,128)(2,1)S(1)}, bf16[256,1536]{1,0:T(8,128)(2,1)S(1)}, u32[]{:S(2)}, u32[]{:S(2)}) collective-permute-start(bf16[256,1536]{1,0:T(8,128)(2,1)S(1)} %copy-done.61), channel_id=1, source_target_pairs={{0,4},{4,0},{8,12},{12,8},{1,5},{5,1},{9,13},{13,9},{2,6},{6,2},{1... | collective-permute-start | bytes 2359304 | tf_op jit(solution)/shard_map/ppermute | solution.py:27
  557.6 32.7 %collective-permute-start.61 = (bf16[256,1536]{1,0:T(8,128)(2,1)S(1)}, bf16[256,1536]{1,0:T(8,128)(2,1)}, u32[]{:S(2)}, u32[]{:S(2)}) collective-permute-start(bf16[256,1536]{1,0:T(8,128)(2,1)S(1)} %copy-done.60), channel_id=1, source_target_pairs={{0,8},{4,12},{8,0},{12,4},{1,9},{5,13},{9,1},{13,5},{2,10},{6,14},... | collective-permute-start | bytes 2359304 | tf_op jit(solution)/shard_map/ppermute | solution.py:27
  601.6 27.7 %collective-permute-start.62 = (bf16[1536,768]{1,0:T(8,128)(2,1)}, bf16[1536,768]{1,0:T(8,128)(2,1)}, u32[]{:S(2)}, u32[]{:S(2)}) collective-permute-start(bf16[1536,768]{1,0:T(8,128)(2,1)} %get-tuple-element.624), channel_id=1, source_target_pairs={{0,16},{16,0},{1,17},{17,1},{2,18},{18,2},{3,19},{19,3},{4,20},{20... | collective-permute-start | bytes 7077896 | tf_op jit(solution)/shard_map/ppermute | solution.py:27
  606.5 41.7 %collective-permute-start.68 = (bf16[4,144,1536]{2,1,0:T(8,128)(2,1)}, bf16[4,144,1536]{2,1,0:T(8,128)(2,1)}, u32[]{:S(2)}, u32[]{:S(2)}) collective-permute-start(bf16[4,144,1536]{2,1,0:T(8,128)(2,1)} %fusion.9), channel_id=1, source_target_pairs={{0,2},{2,3},{3,1},{1,0},{4,6},{6,7},{7,5},{5,4},{8,10},{10,11},{11... | collective-permute-start | bytes 5308424 | tf_op jit(solution)/shard_map/ppermute | solution.py:943
  608.9 20.4 %collective-permute-start.63 = (bf16[256,1536]{1,0:T(8,128)(2,1)}, bf16[256,1536]{1,0:T(8,128)(2,1)}, u32[]{:S(2)}, u32[]{:S(2)}) collective-permute-start(bf16[256,1536]{1,0:T(8,128)(2,1)} %get-tuple-element.625), channel_id=1, source_target_pairs={{0,12},{4,8},{8,4},{12,0},{1,13},{5,9},{9,5},{13,1},{2,14},{6,10},... | collective-permute-start | bytes 2359304 | tf_op jit(solution)/shard_map/ppermute | solution.py:27
  637.2 24.7 %collective-permute-start.69 = (bf16[384,768]{1,0:T(8,128)(2,1)}, bf16[384,768]{1,0:T(8,128)(2,1)}, u32[]{:S(2)}, u32[]{:S(2)}) collective-permute-start(bf16[384,768]{1,0:T(8,128)(2,1)} %get-tuple-element.906), channel_id=1, source_target_pairs={{0,4},{4,0},{8,12},{12,8},{1,5},{5,1},{9,13},{13,9},{2,6},{6,2},{1... | collective-permute-start | bytes 1769480 | tf_op jit(solution)/shard_map/ppermute | solution.py:27
  638.8 29.4 %collective-permute-start.70 = (bf16[384,768]{1,0:T(8,128)(2,1)}, bf16[384,768]{1,0:T(8,128)(2,1)}, u32[]{:S(2)}, u32[]{:S(2)}) collective-permute-start(bf16[384,768]{1,0:T(8,128)(2,1)} %get-tuple-element.905), channel_id=1, source_target_pairs={{0,8},{4,12},{8,0},{12,4},{1,9},{5,13},{9,1},{13,5},{2,10},{6,14},... | collective-permute-start | bytes 1769480 | tf_op jit(solution)/shard_map/ppermute | solution.py:27
  641.6 26.7 %collective-permute-start.71 = (bf16[384,768]{1,0:T(8,128)(2,1)}, bf16[384,768]{1,0:T(8,128)(2,1)}, u32[]{:S(2)}, u32[]{:S(2)}) collective-permute-start(bf16[384,768]{1,0:T(8,128)(2,1)} %get-tuple-element.904), channel_id=1, source_target_pairs={{0,12},{4,8},{8,4},{12,0},{1,13},{5,9},{9,5},{13,1},{2,14},{6,10},... | collective-permute-start | bytes 1769480 | tf_op jit(solution)/shard_map/ppermute | solution.py:27
  668.2 21.0 %collective-permute-start.74 = (bf16[1536,1152]{1,0:T(8,128)(2,1)}, bf16[1536,1152]{1,0:T(8,128)(2,1)S(1)}, u32[]{:S(2)}, u32[]{:S(2)}) collective-permute-start(bf16[1536,1152]{1,0:T(8,128)(2,1)} %get-tuple-element.651), channel_id=1, source_target_pairs={{0,16},{16,0},{1,17},{17,1},{2,18},{18,2},{3,19},{19,3},{4,20},{20... | collective-permute-start | bytes 10616840 | tf_op jit(solution)/shard_map/ppermute | solution.py:27
  668.2 20.2 %collective-permute-start.72 = (bf16[256,1536]{1,0:T(8,128)(2,1)}, bf16[256,1536]{1,0:T(8,128)(2,1)S(1)}, u32[]{:S(2)}, u32[]{:S(2)}) collective-permute-start(bf16[256,1536]{1,0:T(8,128)(2,1)} %get-tuple-element.654.refs_0_.cot_ref), channel_id=1, source_target_pairs={{0,4},{4,0},{8,12},{12,8},{1,5},{5,1},{9,13},{13,9},{2,6},{6,2},{1... | collective-permute-start | bytes 2359304 | tf_op jit(solution)/shard_map/ppermute | solution.py:27
  669.4 19.9 %collective-permute-start.73 = (bf16[256,1536]{1,0:T(8,128)(2,1)}, bf16[256,1536]{1,0:T(8,128)(2,1)S(1)}, u32[]{:S(2)}, u32[]{:S(2)}) collective-permute-start(bf16[256,1536]{1,0:T(8,128)(2,1)} %get-tuple-element.654.refs_0_.cot_ref), channel_id=1, source_target_pairs={{0,8},{4,12},{8,0},{12,4},{1,9},{5,13},{9,1},{13,5},{2,10},{6,14},... | collective-permute-start | bytes 2359304 | tf_op jit(solution)/shard_map/ppermute | solution.py:27
  675.2 55.9 %collective-permute-start.76 = (bf16[4,144,1536]{2,1,0:T(8,128)(2,1)}, bf16[4,144,1536]{2,1,0:T(8,128)(2,1)}, u32[]{:S(2)}, u32[]{:S(2)}) collective-permute-start(bf16[4,144,1536]{2,1,0:T(8,128)(2,1)} %fusion.5), channel_id=1, source_target_pairs={{0,2},{2,3},{3,1},{1,0},{4,6},{6,7},{7,5},{5,4},{8,10},{10,11},{11... | collective-permute-start | bytes 5308424 | tf_op jit(solution)/shard_map/ppermute | solution.py:943
  692.4 38.7 %collective-permute-start.77 = (bf16[384,1152]{1,0:T(8,128)(2,1)}, bf16[384,1152]{1,0:T(8,128)(2,1)}, u32[]{:S(2)}, u32[]{:S(2)}) collective-permute-start(bf16[384,1152]{1,0:T(8,128)(2,1)} %get-tuple-element.897), channel_id=1, source_target_pairs={{0,4},{4,0},{8,12},{12,8},{1,5},{5,1},{9,13},{13,9},{2,6},{6,2},{1... | collective-permute-start | bytes 2654216 | tf_op jit(solution)/shard_map/ppermute | solution.py:27
  693.3 38.0 %collective-permute-start.78 = (bf16[384,1152]{1,0:T(8,128)(2,1)}, bf16[384,1152]{1,0:T(8,128)(2,1)}, u32[]{:S(2)}, u32[]{:S(2)}) collective-permute-start(bf16[384,1152]{1,0:T(8,128)(2,1)} %get-tuple-element.896), channel_id=1, source_target_pairs={{0,8},{4,12},{8,0},{12,4},{1,9},{5,13},{9,1},{13,5},{2,10},{6,14},... | collective-permute-start | bytes 2654216 | tf_op jit(solution)/shard_map/ppermute | solution.py:27
  694.6 36.5 %collective-permute-start.75 = (bf16[256,1536]{1,0:T(8,128)(2,1)}, bf16[256,1536]{1,0:T(8,128)(2,1)S(1)}, u32[]{:S(2)}, u32[]{:S(2)}) collective-permute-start(bf16[256,1536]{1,0:T(8,128)(2,1)} %get-tuple-element.654.refs_0_.cot_ref), channel_id=1, source_target_pairs={{0,12},{4,8},{8,4},{12,0},{1,13},{5,9},{9,5},{13,1},{2,14},{6,10},... | collective-permute-start | bytes 2359304 | tf_op jit(solution)/shard_map/ppermute | solution.py:27
  736.7 41.7 %collective-permute-start.81 = (bf16[4,144,1536]{2,1,0:T(8,128)(2,1)}, bf16[4,144,1536]{2,1,0:T(8,128)(2,1)}, u32[]{:S(2)}, u32[]{:S(2)}) collective-permute-start(bf16[4,144,1536]{2,1,0:T(8,128)(2,1)} %fusion.4), channel_id=1, source_target_pairs={{0,2},{2,3},{3,1},{1,0},{4,6},{6,7},{7,5},{5,4},{8,10},{10,11},{11... | collective-permute-start | bytes 5308424 | tf_op jit(solution)/shard_map/ppermute | solution.py:943
  738.3 24.8 %collective-permute-start.79 = (bf16[256,1536]{1,0:T(8,128)(2,1)}, bf16[256,1536]{1,0:T(8,128)(2,1)}, u32[]{:S(2)}, u32[]{:S(2)}) collective-permute-start(bf16[256,1536]{1,0:T(8,128)(2,1)} %get-tuple-element.675), channel_id=1, source_target_pairs={{0,4},{4,0},{8,12},{12,8},{1,5},{5,1},{9,13},{13,9},{2,6},{6,2},{1... | collective-permute-start | bytes 2359304 | tf_op jit(solution)/shard_map/ppermute | solution.py:27
  739.5 38.9 %collective-permute-start.80 = (bf16[256,1536]{1,0:T(8,128)(2,1)}, bf16[256,1536]{1,0:T(8,128)(2,1)}, u32[]{:S(2)}, u32[]{:S(2)}) collective-permute-start(bf16[256,1536]{1,0:T(8,128)(2,1)} %get-tuple-element.676), channel_id=1, source_target_pairs={{0,8},{4,12},{8,0},{12,4},{1,9},{5,13},{9,1},{13,5},{2,10},{6,14},... | collective-permute-start | bytes 2359304 | tf_op jit(solution)/shard_map/ppermute | solution.py:27
  741.8 36.6 %collective-permute-start.83 = (bf16[384,1152]{1,0:T(8,128)(2,1)S(1)}, bf16[384,1152]{1,0:T(8,128)(2,1)S(1)}, u32[]{:S(2)}, u32[]{:S(2)}) collective-permute-start(bf16[384,1152]{1,0:T(8,128)(2,1)S(1)} %fusion.15), channel_id=1, source_target_pairs={{0,12},{4,8},{8,4},{12,0},{1,13},{5,9},{9,5},{13,1},{2,14},{6,10},... | collective-permute-start | bytes 2654216 | tf_op jit(solution)/shard_map/ppermute | solution.py:27
  780.5 33.2 %collective-permute-start.87 = (bf16[96,1920]{1,0:T(8,128)(2,1)S(1)}, bf16[96,1920]{1,0:T(8,128)(2,1)S(1)}, u32[]{:S(2)}, u32[]{:S(2)}) collective-permute-start(bf16[96,1920]{1,0:T(8,128)(2,1)S(1)} %get-tuple-element.929), channel_id=1, source_target_pairs={{0,3},{1,2},{2,1},{3,0},{4,7},{5,6},{6,5},{7,4},{8,11},{9,10},{10,... | collective-permute-start | bytes 1105928 | tf_op jit(solution)/shard_map/ppermute | solution.py:27
  783.1 31.7 %collective-permute-start.86 = (bf16[96,1920]{1,0:T(8,128)(2,1)S(1)}, bf16[96,1920]{1,0:T(8,128)(2,1)S(1)}, u32[]{:S(2)}, u32[]{:S(2)}) collective-permute-start(bf16[96,1920]{1,0:T(8,128)(2,1)S(1)} %get-tuple-element.930), channel_id=1, source_target_pairs={{0,2},{1,3},{2,0},{3,1},{4,6},{5,7},{6,4},{7,5},{8,10},{9,11},{10,... | collective-permute-start | bytes 1105928 | tf_op jit(solution)/shard_map/ppermute | solution.py:27
  783.4 31.4 %collective-permute-start.85 = (bf16[96,1920]{1,0:T(8,128)(2,1)S(1)}, bf16[96,1920]{1,0:T(8,128)(2,1)S(1)}, u32[]{:S(2)}, u32[]{:S(2)}) collective-permute-start(bf16[96,1920]{1,0:T(8,128)(2,1)S(1)} %get-tuple-element.928), channel_id=1, source_target_pairs={{0,1},{1,0},{2,3},{3,2},{4,5},{5,4},{6,7},{7,6},{8,9},{9,8},{10,11... | collective-permute-start | bytes 1105928 | tf_op jit(solution)/shard_map/ppermute | solution.py:27
  784.9 30.1 %collective-permute-start.84 = (bf16[256,1536]{1,0:T(8,128)(2,1)}, bf16[256,1536]{1,0:T(8,128)(2,1)}, u32[]{:S(2)}, u32[]{:S(2)}) collective-permute-start(bf16[256,1536]{1,0:T(8,128)(2,1)} %get-tuple-element.705), channel_id=1, source_target_pairs={{0,12},{4,8},{8,4},{12,0},{1,13},{5,9},{9,5},{13,1},{2,14},{6,10},... | collective-permute-start | bytes 2359304 | tf_op jit(solution)/shard_map/ppermute | solution.py:27
  826.3 21.3 %collective-permute-start.88 = (bf16[1536,768]{1,0:T(8,128)(2,1)}, bf16[1536,768]{1,0:T(8,128)(2,1)}, u32[]{:S(2)}, u32[]{:S(2)}) collective-permute-start(bf16[1536,768]{1,0:T(8,128)(2,1)} %get-tuple-element.755), channel_id=1, source_target_pairs={{0,16},{16,0},{1,17},{17,1},{2,18},{18,2},{3,19},{19,3},{4,20},{20... | collective-permute-start | bytes 7077896 | tf_op jit(solution)/shard_map/ppermute | solution.py:27
  830.7 56.1 %collective-permute-start.95 = (bf16[4,144,1536]{2,1,0:T(8,128)(2,1)}, bf16[4,144,1536]{2,1,0:T(8,128)(2,1)}, u32[]{:S(2)}, u32[]{:S(2)}) collective-permute-start(bf16[4,144,1536]{2,1,0:T(8,128)(2,1)} %fusion.10), channel_id=1, source_target_pairs={{0,2},{2,3},{3,1},{1,0},{4,6},{6,7},{7,5},{5,4},{8,10},{10,11},{11... | collective-permute-start | bytes 5308424 | tf_op jit(solution)/shard_map/ppermute | solution.py:943
  866.0 20.8 %collective-permute-start.92 = (bf16[384,768]{1,0:T(8,128)(2,1)}, bf16[384,768]{1,0:T(8,128)(2,1)}, u32[]{:S(2)}, u32[]{:S(2)}) collective-permute-start(bf16[384,768]{1,0:T(8,128)(2,1)} %get-tuple-element.902), channel_id=1, source_target_pairs={{0,4},{4,0},{8,12},{12,8},{1,5},{5,1},{9,13},{13,9},{2,6},{6,2},{1... | collective-permute-start | bytes 1769480 | tf_op jit(solution)/shard_map/ppermute | solution.py:27
  890.5 41.2 %collective-permute-start.99 = (bf16[4,144,1536]{2,1,0:T(8,128)(2,1)S(1)}, bf16[4,144,1536]{2,1,0:T(8,128)(2,1)S(1)}, u32[]{:S(2)}, u32[]{:S(2)}) collective-permute-start(bf16[4,144,1536]{2,1,0:T(8,128)(2,1)S(1)} %fusion.2), channel_id=1, source_target_pairs={{0,2},{2,3},{3,1},{1,0},{4,6},{6,7},{7,5},{5,4},{8,10},{10,11},{11... | collective-permute-start | bytes 5308424 | tf_op jit(solution)/shard_map/ppermute | solution.py:943
  894.2 37.6 %collective-permute-start.97 = (bf16[384,1152]{1,0:T(8,128)(2,1)S(1)}, bf16[384,1152]{1,0:T(8,128)(2,1)S(1)}, u32[]{:S(2)}, u32[]{:S(2)}) collective-permute-start(bf16[384,1152]{1,0:T(8,128)(2,1)S(1)} %get-tuple-element.894), channel_id=1, source_target_pairs={{0,4},{4,0},{8,12},{12,8},{1,5},{5,1},{9,13},{13,9},{2,6},{6,2},{1... | collective-permute-start | bytes 2654216 | tf_op jit(solution)/shard_map/ppermute | solution.py:27
  895.4 36.4 %collective-permute-start.98 = (bf16[384,1152]{1,0:T(8,128)(2,1)S(1)}, bf16[384,1152]{1,0:T(8,128)(2,1)S(1)}, u32[]{:S(2)}, u32[]{:S(2)}) collective-permute-start(bf16[384,1152]{1,0:T(8,128)(2,1)S(1)} %get-tuple-element.893), channel_id=1, source_target_pairs={{0,8},{4,12},{8,0},{12,4},{1,9},{5,13},{9,1},{13,5},{2,10},{6,14},... | collective-permute-start | bytes 2654216 | tf_op jit(solution)/shard_map/ppermute | solution.py:27
  934.6 41.5 %collective-permute-start.106 = (bf16[4,144,1536]{2,1,0:T(8,128)(2,1)S(1)}, bf16[4,144,1536]{2,1,0:T(8,128)(2,1)S(1)}, u32[]{:S(2)}, u32[]{:S(2)}) collective-permute-start(bf16[4,144,1536]{2,1,0:T(8,128)(2,1)S(1)} %fusion.1), channel_id=1, source_target_pairs={{0,2},{2,3},{3,1},{1,0},{4,6},{6,7},{7,5},{5,4},{8,10},{10,11},{11... | collective-permute-start | bytes 5308424 | tf_op jit(solution)/shard_map/ppermute | solution.py:943
  938.3 34.5 %collective-permute-start.100 = (bf16[384,1152]{1,0:T(8,128)(2,1)S(1)}, bf16[384,1152]{1,0:T(8,128)(2,1)S(1)}, u32[]{:S(2)}, u32[]{:S(2)}) collective-permute-start(bf16[384,1152]{1,0:T(8,128)(2,1)S(1)} %get-tuple-element.892), channel_id=1, source_target_pairs={{0,12},{4,8},{8,4},{12,0},{1,13},{5,9},{9,5},{13,1},{2,14},{6,10},... | collective-permute-start | bytes 2654216 | tf_op jit(solution)/shard_map/ppermute | solution.py:27
  941.1 31.8 %collective-permute-start.101 = (bf16[384,768]{1,0:T(8,128)(2,1)S(1)}, bf16[384,768]{1,0:T(8,128)(2,1)S(1)}, u32[]{:S(2)}, u32[]{:S(2)}) collective-permute-start(bf16[384,768]{1,0:T(8,128)(2,1)S(1)} %fusion.41), channel_id=1, source_target_pairs={{0,12},{4,8},{8,4},{12,0},{1,13},{5,9},{9,5},{13,1},{2,14},{6,10},... | collective-permute-start | bytes 1769480 | tf_op jit(solution)/shard_map/ppermute | solution.py:27
  973.1 61.1 %collective-permute-start.102 = (f32[256,1536]{1,0:T(8,128)S(1)}, f32[256,1536]{1,0:T(8,128)S(1)}, u32[]{:S(2)}, u32[]{:S(2)}) collective-permute-start(f32[256,1536]{1,0:T(8,128)S(1)} %broadcast_select_fusion.2), channel_id=1, source_target_pairs={{0,16},{16,0},{1,17},{17,1},{2,18},{18,2},{3,19},{19,3},{4,20},{20... | collective-permute-start | bytes 4718600 | tf_op jit(solution)/shard_map/ppermute | solution.py:27
  979.2 23.6 %collective-permute-start.109 = (bf16[2,144,1536]{2,1,0:T(8,128)(2,1)S(1)}, bf16[2,144,1536]{2,1,0:T(8,128)(2,1)S(1)}, u32[]{:S(2)}, u32[]{:S(2)}) collective-permute-start(bf16[2,144,1536]{2,1,0:T(8,128)(2,1)S(1)} %get-tuple-element.913), channel_id=1, source_target_pairs={{0,12},{4,8},{8,4},{12,0},{1,13},{5,9},{9,5},{13,1},{2,14},{6,10},... | collective-permute-start | bytes 2654216 | tf_op jit(solution)/shard_map/ppermute | solution.py:27
  980.6 38.9 %collective-permute-start.108 = (bf16[2,144,1536]{2,1,0:T(8,128)(2,1)S(1)}, bf16[2,144,1536]{2,1,0:T(8,128)(2,1)S(1)}, u32[]{:S(2)}, u32[]{:S(2)}) collective-permute-start(bf16[2,144,1536]{2,1,0:T(8,128)(2,1)S(1)} %get-tuple-element.912), channel_id=1, source_target_pairs={{0,8},{4,12},{8,0},{12,4},{1,9},{5,13},{9,1},{13,5},{2,10},{6,14},... | collective-permute-start | bytes 2654216 | tf_op jit(solution)/shard_map/ppermute | solution.py:27
  981.9 40.1 %collective-permute-start.107 = (bf16[2,144,1536]{2,1,0:T(8,128)(2,1)S(1)}, bf16[2,144,1536]{2,1,0:T(8,128)(2,1)S(1)}, u32[]{:S(2)}, u32[]{:S(2)}) collective-permute-start(bf16[2,144,1536]{2,1,0:T(8,128)(2,1)S(1)} %get-tuple-element.911), channel_id=1, source_target_pairs={{0,4},{4,0},{8,12},{12,8},{1,5},{5,1},{9,13},{13,9},{2,6},{6,2},{1... | collective-permute-start | bytes 2654216 | tf_op jit(solution)/shard_map/ppermute | solution.py:27
  985.0 37.5 %collective-permute-start.103 = (bf16[96,1920]{1,0:T(8,128)(2,1)S(1)}, bf16[96,1920]{1,0:T(8,128)(2,1)S(1)}, u32[]{:S(2)}, u32[]{:S(2)}) collective-permute-start(bf16[96,1920]{1,0:T(8,128)(2,1)S(1)} %get-tuple-element.926), channel_id=1, source_target_pairs={{0,1},{1,0},{2,3},{3,2},{4,5},{5,4},{6,7},{7,6},{8,9},{9,8},{10,11... | collective-permute-start | bytes 1105928 | tf_op jit(solution)/shard_map/ppermute | solution.py:27
  (126 other events, 1741.0 us)
